TPU v7x, 32 devices: a whole 2x2x4 slice. The times are simulated.
32 devices in a mesh: wide: 8 (over y, x, core), narrow: 4 (over z).
Axes of the slice: x: 2, y: 2, z: 4, core: 2. Of those that a mesh axis runs over, the one named last changes fastest.
Arguments:
- tokens: bfloat16 [8, 4, 128, 1152], P(None, 'narrow', 'wide'), may hold values from -6 to 6
- cotangent: bfloat16 [8, 4, 128, 1152], P(None, 'narrow', 'wide'), may hold values from -6 to 6
- seq_lengths: int32 [8, 2], P('wide'), may hold values from 0 to 512, as said below
- query_weight: bfloat16 [1152, 1024], P('wide', 'narrow'), may hold values from -0.1875 to 0.1875
- key_weight: bfloat16 [1152, 256], P('wide'), may hold values from -0.1875 to 0.1875
- value_weight: bfloat16 [1152, 256], P('wide'), may hold values from -0.1875 to 0.1875
- outproj_weight: bfloat16 [1152, 1024], P('wide', 'narrow'), may hold values from -0.1875 to 0.1875
- gate_weight: bfloat16 [1152, 6912], P('wide', 'narrow'), may hold values from -0.1875 to 0.1875
- up_weight: bfloat16 [1152, 6912], P('wide', 'narrow'), may hold values from -0.1875 to 0.1875
- down_weight: bfloat16 [1152, 6912], P('wide', 'narrow'), may hold values from -0.078125 to 0.078125
- attn_gain: bfloat16 [1152], P('wide'), may hold values from -0.5 to 0.5
- attnout_gain: bfloat16 [1152], P('wide'), may hold values from -0.5 to 0.5
- ffn_gain: bfloat16 [1152], P('wide'), may hold values from -0.5 to 0.5
- ffnout_gain: bfloat16 [1152], P('wide'), may hold values from -0.5 to 0.5
- query_gain: bfloat16 [256], P('wide'), may hold values from -0.5 to 0.5
- key_gain: bfloat16 [256], P('wide'), may hold values from -0.5 to 0.5
Outputs:
- layer_out: bfloat16 [8, 4, 128, 1152], P(None, 'narrow', 'wide')
- input_grad: bfloat16 [8, 4, 128, 1152], P(None, 'narrow', 'wide')
- query_grad: float32 [1152, 1024], P('wide', 'narrow')
- key_grad: float32 [1152, 256], P('wide')
- value_grad: float32 [1152, 256], P('wide')
- outproj_grad: float32 [1152, 1024], P('wide', 'narrow')
- gate_grad: float32 [1152, 6912], P('wide', 'narrow')
- up_grad: float32 [1152, 6912], P('wide', 'narrow')
- down_grad: float32 [1152, 6912], P('wide', 'narrow')
- attngain_grad: float32 [1152], P('wide')
- attnoutgain_grad: float32 [1152], P('wide')
- ffngain_grad: float32 [1152], P('wide')
- ffnoutgain_grad: float32 [1152], P('wide')
- querygain_grad: float32 [256], P('wide')
- keygain_grad: float32 [256], P('wide')
Inputs may be any that keep to these rules, and one draw needn't show every extreme that they name: `seq_lengths`: row b holds the lengths of the two sequences that stand in order at the start of bucket b, the rest of the bucket being padding; the longer exceeds 3 * 128, the two sum to at most 512, and in every draw some bucket holds one sequence of 512 tokens.
All inputs are finite; a program needn't handle non-finite values.
Results may differ from a plain program's by a relative error of at most 0.025.
Values may be sent and summed in bfloat16 or wider, within the bound.
No kernel may reach another device: no remote copies, remote signals or barrier semaphores. Data moves between devices by JAX's collectives and lax.ppermute only.
A program may use at most 192 MiB of HBM per device.

v0:
```python
import math

import jax
import jax.numpy as jnp
from jax import lax
from jax.sharding import PartitionSpec as P

EPS = 1e-06
SCALE = 0.0625
LOGBASE = math.log(1000000.0)


def norm_gain(value, gain):
    return value * lax.rsqrt(jnp.mean(value * value, axis=-1, keepdims=True) + EPS) * (1.0 + gain)


def gain_term(value, grad):
    ratio = lax.rsqrt(jnp.mean(value * value, axis=-1, keepdims=True) + EPS)
    return jnp.sum(grad * value * ratio, axis=0)


def norm_back(value, grad, gain):
    return jax.vjp(lambda inner: norm_gain(inner, gain), value)[1](grad)[0]


def gelu_tanh(value):
    return (
        0.5
        * value
        * (1.0 + jnp.tanh(0.7978845608028654 * (value + 0.044715 * value * value * value)))
    )


def activation(gate_in, up_in):
    return gelu_tanh(gate_in) * up_in


def rope_tables(place, width):
    half = width // 2
    expo = jnp.arange(half, dtype=jnp.float32) * (-2.0 / width)
    freqs = jnp.exp(expo * LOGBASE)
    angle = place.astype(jnp.float32)[:, None] * freqs[None, :]
    return (jnp.cos(angle), jnp.sin(angle))


def rotate(value, cosine, sine):
    half = value.shape[-1] // 2
    first = value[..., :half]
    second = value[..., half:]
    return jnp.concatenate(
        [first * cosine - second * sine, second * cosine + first * sine], axis=-1
    )


def bucket_layout(lengths, rows):
    position = jnp.arange(rows, dtype=jnp.int32)
    first = lengths[0]
    ends = lengths[0] + lengths[1]
    segment = jnp.where(position < first, 0, jnp.where(position < ends, 1, 2)).astype(jnp.int32)
    begin = jnp.where(segment == 0, 0, jnp.where(segment == 1, first, ends))
    return (segment, position - begin)


def on_device(
    tokens,
    cotangent,
    seq_lengths,
    query_weight,
    key_weight,
    value_weight,
    outproj_weight,
    gate_weight,
    up_weight,
    down_weight,
    attn_gain,
    attnout_gain,
    ffn_gain,
    ffnout_gain,
    query_gain,
    key_gain,
):
    width = tokens.shape[3]
    arrived = (
        lax.all_to_all(tokens, "wide", split_axis=0, concat_axis=2, tiled=True),
        lax.all_to_all(cotangent, "wide", split_axis=0, concat_axis=2, tiled=True),
    )
    own_x = arrived[0].reshape(-1, width)
    own_dy = arrived[1].reshape(-1, width)
    quarter = own_x.shape[0]
    rows = quarter * lax.axis_size("narrow")
    start_own = lax.axis_index("narrow") * quarter
    fetched = (
        lax.all_gather(query_weight, "wide", axis=0, tiled=True),
        lax.all_gather(key_weight, "wide", axis=0, tiled=True),
        lax.all_gather(value_weight, "wide", axis=0, tiled=True),
        lax.all_gather(outproj_weight, "wide", axis=0, tiled=True),
        lax.all_gather(gate_weight, "wide", axis=0, tiled=True),
        lax.all_gather(up_weight, "wide", axis=0, tiled=True),
        lax.all_gather(down_weight, "wide", axis=0, tiled=True),
        lax.all_gather(attn_gain, "wide", axis=0, tiled=True),
        lax.all_gather(attnout_gain, "wide", axis=0, tiled=True),
        lax.all_gather(ffn_gain, "wide", axis=0, tiled=True),
        lax.all_gather(ffnout_gain, "wide", axis=0, tiled=True),
        lax.all_gather(query_gain, "wide", axis=0, tiled=True),
        lax.all_gather(key_gain, "wide", axis=0, tiled=True),
    )
    w_query, w_key, w_value, w_outproj, w_gate, w_up, w_down = fetched[:7]
    gain_attn, gain_attnout, gain_ffn, gain_ffnout, gain_query, gain_key = [
        g.astype(jnp.float32) for g in fetched[7:]
    ]
    head = w_key.shape[1]
    heads_here = w_query.shape[1] // head
    segment, place = bucket_layout(seq_lengths[0], rows)
    valid = (segment < 2).astype(jnp.float32)

    def mine(value):
        return lax.dynamic_slice_in_dim(value, start_own, quarter, 0)

    x_loc, dy_loc = (
        lax.all_gather(own_x, "narrow", axis=0, tiled=True),
        lax.all_gather(own_dy, "narrow", axis=0, tiled=True),
    )

    def own_part(value):
        return mine(value)

    def total(value):
        return lax.psum(value.astype(jnp.bfloat16), "narrow").astype(jnp.float32)

    cosine, sine = rope_tables(place, head)

    def shape_queries(raw, gain):
        return rotate(norm_gain(raw, gain), cosine[:, None, :], sine[:, None, :])

    def shape_keys(raw, gain, cos_rows, sin_rows):
        return rotate(norm_gain(raw, gain), cos_rows, sin_rows)

    x_f = x_loc.astype(jnp.float32)
    xn1 = norm_gain(x_f, gain_attn).astype(jnp.bfloat16)
    q_raw = jnp.dot(xn1, w_query, preferred_element_type=jnp.float32).reshape(
        rows, heads_here, head
    )
    k_raw = jnp.dot(xn1, w_key, preferred_element_type=jnp.float32)
    values = jnp.dot(xn1, w_value, preferred_element_type=jnp.float32).astype(jnp.bfloat16)
    queries = shape_queries(q_raw, gain_query).astype(jnp.bfloat16)
    keys = shape_keys(k_raw, gain_key, cosine, sine).astype(jnp.bfloat16)
    block = min(512, rows)
    count = rows // block
    key_pos = jnp.arange(rows, dtype=jnp.int32)

    def masked_scores(index):
        begin = index * block
        row_pos = begin + jnp.arange(block, dtype=jnp.int32)
        allowed = (segment[:, None] == segment[None, :]) & (key_pos[None, :] <= row_pos[:, None])
        scores = (
            jnp.einsum("qhd,kd->hqk", queries, keys, preferred_element_type=jnp.float32) * SCALE
        )
        return (jnp.where(allowed[None], scores, -1e30), queries)

    def forward_block(index):
        scores, unused = masked_scores(index)
        top = jnp.max(scores, axis=-1, keepdims=True)
        raised = jnp.exp(scores - top)
        summed = jnp.sum(raised, axis=-1, keepdims=True)
        probs = (raised / summed).astype(jnp.bfloat16)
        result = jnp.einsum("hqk,kd->qhd", probs, values, preferred_element_type=jnp.float32)
        return (result.astype(jnp.bfloat16), (top + jnp.log(summed))[..., 0])

    attended, log_totals = lax.map(forward_block, jnp.arange(count, dtype=jnp.int32))
    attended = attended.reshape(rows, heads_here * head)
    mixed_loc = total(
        jnp.einsum("rk,dk->rd", attended, w_outproj, preferred_element_type=jnp.float32)
    )
    resid = x_f + norm_gain(mixed_loc, gain_attnout)
    xn2 = norm_gain(resid, gain_ffn).astype(jnp.bfloat16)
    gate = jnp.dot(xn2, w_gate, preferred_element_type=jnp.float32)
    up = jnp.dot(xn2, w_up, preferred_element_type=jnp.float32)
    act = activation(gate, up).astype(jnp.bfloat16)
    ffn_loc = total(jnp.einsum("rf,df->rd", act, w_down, preferred_element_type=jnp.float32))
    out_own = own_part(resid + norm_gain(ffn_loc, gain_ffnout)).astype(jnp.bfloat16)
    fetched = (
        lax.all_gather(query_weight, "wide", axis=0, tiled=True),
        lax.all_gather(key_weight, "wide", axis=0, tiled=True),
        lax.all_gather(value_weight, "wide", axis=0, tiled=True),
        lax.all_gather(outproj_weight, "wide", axis=0, tiled=True),
        lax.all_gather(gate_weight, "wide", axis=0, tiled=True),
        lax.all_gather(up_weight, "wide", axis=0, tiled=True),
        lax.all_gather(down_weight, "wide", axis=0, tiled=True),
        lax.all_gather(attn_gain, "wide", axis=0, tiled=True),
        lax.all_gather(attnout_gain, "wide", axis=0, tiled=True),
        lax.all_gather(ffn_gain, "wide", axis=0, tiled=True),
        lax.all_gather(ffnout_gain, "wide", axis=0, tiled=True),
        lax.all_gather(query_gain, "wide", axis=0, tiled=True),
        lax.all_gather(key_gain, "wide", axis=0, tiled=True),
    )
    w_query, w_key, w_value, w_outproj, w_gate, w_up, w_down = fetched[:7]
    gain_attn, gain_attnout, gain_ffn, gain_ffnout, gain_query, gain_key = [
        g.astype(jnp.float32) for g in fetched[7:]
    ]
    d_out = dy_loc.astype(jnp.float32) * valid[:, None]
    d_ffn = norm_back(ffn_loc, d_out, gain_ffnout)
    grad_ffnout = gain_term(own_part(ffn_loc), own_part(d_out))
    d_ffn_all = d_ffn.astype(jnp.bfloat16)
    grad_down = jnp.einsum("rd,rf->df", d_ffn_all, act, preferred_element_type=jnp.float32)
    d_act = jnp.dot(d_ffn_all, w_down, preferred_element_type=jnp.float32)
    d_gate, d_up = jax.vjp(activation, gate, up)[1](d_act)
    d_gate = d_gate.astype(jnp.bfloat16)
    d_up = d_up.astype(jnp.bfloat16)
    grad_gate = jnp.einsum("rd,rf->df", xn2, d_gate, preferred_element_type=jnp.float32)
    grad_up = jnp.einsum("rd,rf->df", xn2, d_up, preferred_element_type=jnp.float32)
    d_xn2 = total(
        jnp.einsum("rf,df->rd", d_gate, w_gate, preferred_element_type=jnp.float32)
        + jnp.einsum("rf,df->rd", d_up, w_up, preferred_element_type=jnp.float32)
    )
    d_resid = d_out + norm_back(resid, d_xn2, gain_ffn)
    grad_ffn = gain_term(own_part(resid), own_part(d_xn2))
    d_mixed = norm_back(mixed_loc, d_resid, gain_attnout)
    grad_attnout = gain_term(own_part(mixed_loc), own_part(d_resid))
    d_mixed_all = d_mixed.astype(jnp.bfloat16)
    grad_outproj = jnp.einsum(
        "rd,rk->dk", d_mixed_all, attended, preferred_element_type=jnp.float32
    )
    d_att = jnp.dot(d_mixed_all, w_outproj, preferred_element_type=jnp.float32).astype(jnp.bfloat16)
    d_att = d_att.reshape(rows, heads_here, head)

    def backward_block(carry, index):
        key_sum, value_sum = carry
        scores, q_block = masked_scores(index)
        probs = jnp.exp(scores - log_totals[index][..., None])
        d_probs = jnp.einsum("qhd,kd->hqk", d_att, values, preferred_element_type=jnp.float32)
        centre = jnp.sum(d_probs * probs, axis=-1, keepdims=True)
        d_scores = (probs * (d_probs - centre)).astype(jnp.bfloat16)
        d_query = (
            jnp.einsum("hqk,kd->qhd", d_scores, keys, preferred_element_type=jnp.float32) * SCALE
        )
        key_sum = (
            key_sum
            + jnp.einsum("hqk,qhd->kd", d_scores, q_block, preferred_element_type=jnp.float32)
            * SCALE
        )
        value_sum = value_sum + jnp.einsum(
            "hqk,qhd->kd", probs.astype(jnp.bfloat16), d_att, preferred_element_type=jnp.float32
        )
        return ((key_sum, value_sum), d_query)

    empty = jnp.zeros((rows, head), jnp.float32)
    (key_part, value_part), d_queries = lax.scan(
        backward_block, (empty, empty), jnp.arange(count, dtype=jnp.int32)
    )
    d_queries = d_queries.reshape(rows, heads_here, head)
    d_queries = lax.optimization_barrier(d_queries.astype(jnp.bfloat16)).astype(jnp.float32)
    d_q_raw, grad_query_gain = jax.vjp(shape_queries, q_raw, gain_query)[1](d_queries)
    d_q_raw = d_q_raw.reshape(rows, heads_here * head).astype(jnp.bfloat16)
    grad_query = jnp.einsum("rd,rk->dk", xn1, d_q_raw, preferred_element_type=jnp.float32)
    d_xn1_part = jnp.einsum("rk,dk->rd", d_q_raw, w_query, preferred_element_type=jnp.float32)
    joined = own_part(total(jnp.concatenate([d_xn1_part, key_part, value_part], axis=1)))
    d_xn1 = joined[:, :width]
    d_keys = lax.optimization_barrier(joined[:, width : width + head].astype(jnp.bfloat16)).astype(
        jnp.float32
    )
    d_values = joined[:, width + head :].astype(jnp.bfloat16)
    cos_own = mine(cosine)
    sin_own = mine(sine)
    d_k_raw, grad_key_gain = jax.vjp(
        lambda raw, gain: shape_keys(raw, gain, cos_own, sin_own), mine(k_raw), gain_key
    )[1](d_keys)
    d_k_raw = d_k_raw.astype(jnp.bfloat16)
    xn1_own = mine(xn1)
    grad_key = jnp.einsum("rd,rk->dk", xn1_own, d_k_raw, preferred_element_type=jnp.float32)
    grad_value = jnp.einsum("rd,rk->dk", xn1_own, d_values, preferred_element_type=jnp.float32)
    d_xn1 = (
        d_xn1
        + jnp.einsum("rk,dk->rd", d_k_raw, w_key, preferred_element_type=jnp.float32)
        + jnp.einsum("rk,dk->rd", d_values, w_value, preferred_element_type=jnp.float32)
    )
    x_own = own_part(x_f)
    d_x = own_part(d_resid) + norm_back(x_own, d_xn1, gain_attn)
    grad_attn = gain_term(x_own, d_xn1)
    summed = (
        lax.psum_scatter(
            grad_query.astype(jnp.bfloat16), "wide", scatter_dimension=0, tiled=True
        ).astype(jnp.float32),
        lax.psum_scatter(
            grad_key.astype(jnp.bfloat16), "wide", scatter_dimension=0, tiled=True
        ).astype(jnp.float32),
        lax.psum_scatter(
            grad_value.astype(jnp.bfloat16), "wide", scatter_dimension=0, tiled=True
        ).astype(jnp.float32),
        lax.psum_scatter(
            grad_outproj.astype(jnp.bfloat16), "wide", scatter_dimension=0, tiled=True
        ).astype(jnp.float32),
        lax.psum_scatter(
            grad_gate.astype(jnp.bfloat16), "wide", scatter_dimension=0, tiled=True
        ).astype(jnp.float32),
        lax.psum_scatter(
            grad_up.astype(jnp.bfloat16), "wide", scatter_dimension=0, tiled=True
        ).astype(jnp.float32),
        lax.psum_scatter(
            grad_down.astype(jnp.bfloat16), "wide", scatter_dimension=0, tiled=True
        ).astype(jnp.float32),
        lax.psum_scatter(
            grad_attn.astype(jnp.bfloat16), "wide", scatter_dimension=0, tiled=True
        ).astype(jnp.float32),
        lax.psum_scatter(
            grad_attnout.astype(jnp.bfloat16), "wide", scatter_dimension=0, tiled=True
        ).astype(jnp.float32),
        lax.psum_scatter(
            grad_ffn.astype(jnp.bfloat16), "wide", scatter_dimension=0, tiled=True
        ).astype(jnp.float32),
        lax.psum_scatter(
            grad_ffnout.astype(jnp.bfloat16), "wide", scatter_dimension=0, tiled=True
        ).astype(jnp.float32),
        lax.psum_scatter(
            grad_query_gain.astype(jnp.bfloat16), "wide", scatter_dimension=0, tiled=True
        ).astype(jnp.float32),
        lax.psum_scatter(
            grad_key_gain.astype(jnp.bfloat16), "wide", scatter_dimension=0, tiled=True
        ).astype(jnp.float32),
    )
    s_query, s_key, s_value, s_outproj, s_gate, s_up, s_down = summed[:7]
    s_attn, s_attnout, s_ffn, s_ffnout, s_qgain, s_kgain = summed[7:]
    shared = (
        lax.psum(s_key.astype(jnp.bfloat16), "narrow").astype(jnp.float32),
        lax.psum(s_value.astype(jnp.bfloat16), "narrow").astype(jnp.float32),
        lax.psum(s_attn.astype(jnp.bfloat16), "narrow").astype(jnp.float32),
        lax.psum(s_attnout.astype(jnp.bfloat16), "narrow").astype(jnp.float32),
        lax.psum(s_ffn.astype(jnp.bfloat16), "narrow").astype(jnp.float32),
        lax.psum(s_ffnout.astype(jnp.bfloat16), "narrow").astype(jnp.float32),
        lax.psum(s_qgain.astype(jnp.bfloat16), "narrow").astype(jnp.float32),
        lax.psum(s_kgain.astype(jnp.bfloat16), "narrow").astype(jnp.float32),
    )
    leaving = (
        lax.all_to_all(
            out_own.reshape(1, 1, quarter, width), "wide", split_axis=2, concat_axis=0, tiled=True
        ),
        lax.all_to_all(
            d_x.astype(jnp.bfloat16).reshape(1, 1, quarter, width),
            "wide",
            split_axis=2,
            concat_axis=0,
            tiled=True,
        ),
    )
    return (
        leaving[0],
        leaving[1],
        s_query,
        shared[0],
        shared[1],
        s_outproj,
        s_gate,
        s_up,
        s_down,
        shared[2],
        shared[3],
        shared[4],
        shared[5],
        shared[6],
        shared[7],
    )


def solution(mesh):
    return jax.shard_map(
        on_device,
        mesh=mesh,
        in_specs=(
            P(None, "narrow", "wide", None),
            P(None, "narrow", "wide", None),
            P("wide", None),
            P("wide", "narrow"),
            P("wide", None),
            P("wide", None),
            P("wide", "narrow"),
            P("wide", "narrow"),
            P("wide", "narrow"),
            P("wide", "narrow"),
            P("wide"),
            P("wide"),
            P("wide"),
            P("wide"),
            P("wide"),
            P("wide"),
        ),
        out_specs=(
            P(None, "narrow", "wide", None),
            P(None, "narrow", "wide", None),
            P("wide", "narrow"),
            P("wide", None),
            P("wide", None),
            P("wide", "narrow"),
            P("wide", "narrow"),
            P("wide", "narrow"),
            P("wide", "narrow"),
            P("wide"),
            P("wide"),
            P("wide"),
            P("wide"),
            P("wide"),
            P("wide"),
        ),
        check_vma=False,
    )
```

profile of v0, /device:TPU:0, one launch (start us, length us, event | category | flops | bytes accessed | tf_op | source)
XLA Modules:
  0.0 791.5 jit_solution(17322599702040119533)
XLA Ops:
  8.1 12.5 %all_to_all.42 = bf16[8,1,16,1152]{3,2,1,0:T(8,128)(2,1)S(1)} all-to-all(bf16[8,1,16,1152]{3,2,1,0:T(8,128)(2,1)} %param.16), channel_id=1, replica_groups=mesh['wide'=8,'narrow'=4] {'wide'}, dimensions={0} | all-to-all | bytes 589824 | tf_op jit(solution)/shard_map/all_to_all | solution.py:84
  31.9 23.9 %all-reduce.17 = (bf16[1152]{0:T(1024)(128)(2,1)S(1)}, bf16[256]{0:T(256)(128)(2,1)S(1)}, bf16[256]{0:T(256)(128)(2,1)S(1)}, bf16[1152]{0:T(1024)(128)(2,1)}, bf...) all-reduce(bf16[1152]{0:T(1024)(128)(2,1)S(1)} %dynamic-update-slice, ...), channel_id=1, replica_groups=mesh['wide'=8,'narrow'=4] {'wide'}, use_global_device_ids=true, to_apply=%add.4 | all-reduce | flops 5120 | bytes 20480
  56.5 9.5 %all_gather.61 = bf16[1152,256]{1,0:T(8,128)(2,1)S(1)} all-gather(bf16[144,256]{1,0:T(8,128)(2,1)} %param.20), channel_id=1, replica_groups=mesh['wide'=8,'narrow'=4] {'wide'}, dimensions={0}, use_global_device_ids=true | all-gather | bytes 663552 | tf_op jit(solution)/shard_map/all_gather | solution.py:94
  66.0 9.5 %all_gather.63 = bf16[1152,256]{1,0:T(8,128)(2,1)S(1)} all-gather(bf16[144,256]{1,0:T(8,128)(2,1)} %param.19), channel_id=1, replica_groups=mesh['wide'=8,'narrow'=4] {'wide'}, dimensions={0}, use_global_device_ids=true | all-gather | bytes 663552 | tf_op jit(solution)/shard_map/all_gather | solution.py:93
  75.4 9.5 %all_gather.60 = bf16[1152,256]{1,0:T(8,128)(2,1)S(1)} all-gather(bf16[144,256]{1,0:T(8,128)(2,1)S(1)} %copy-done.46), channel_id=1, replica_groups=mesh['wide'=8,'narrow'=4] {'wide'}, dimensions={0}, use_global_device_ids=true | all-gather | bytes 663552 | tf_op jit(solution)/shard_map/all_gather | solution.py:95
  84.9 9.5 %all_gather.65 = bf16[1152,256]{1,0:T(8,128)(2,1)S(1)} all-gather(bf16[144,256]{1,0:T(8,128)(2,1)S(1)} %copy-done.47), channel_id=1, replica_groups=mesh['wide'=8,'narrow'=4] {'wide'}, dimensions={0}, use_global_device_ids=true | all-gather | bytes 663552 | tf_op jit(solution)/shard_map/all_gather | solution.py:96
  99.2 1.9 multiply_cosine_fusion.1
  108.4 3.4 all-to-all-start.2
  112.6 6.5 all-to-all-done.2
  120.3 43.4 %all-reduce.26.cloned.1.call-done = bf16[512,1152]{0,1:T(8,128)(2,1)} async-done(((bf16[512,1152]{0,1:T(8,128)(2,1)}), bf16[512,1152]{0,1:T(8,128)(2,1)}) %all-reduce.26.cloned.1.call-update) | async-done | bytes 1179664 | tf_op jit(solution)/shard_map/psum | solution.py:128
  165.8 1.9 multiply_reduce_fusion.4
  169.1 6.9 fusion.72
  176.0 8.3 %all-gather.10.cloned.1.call-done = bf16[1152,1728]{1,0:T(8,128)(2,1)} async-done(((bf16[144,1728]{1,0:T(8,128)(2,1)}), bf16[1152,1728]{1,0:T(8,128)(2,1)}) %all-gather.10.cloned.1.call-update) | async-done | bytes 3981328 | tf_op jit(solution)/shard_map/all_gather | solution.py:98
  184.3 9.0 %multiply_convert_fusion.1 = (bf16[512,1728]{0,1:T(8,128)(2,1)}, f32[512,1728]{0,1:T(8,128)}) fusion(f32[512,1728]{0,1:T(8,128)} %fusion.72, bf16[512,1152]{0,1:T(8,128)(2,1)S(1)} %multiply_convert_fusion.2, bf16[1152,1728]{1,0:T(8,128)(2,1)} %all-gather.10.cloned.1.call-done), kind=kOutput, calls=%fused_computation.14 | convolution fusion | flops 2047279104 | bytes 14008320 | tf_op jit(solution)/shard_map/dot_general | solution.py:177
  193.3 29.1 %all-gather.12.cloned.1.call-done = bf16[1152,1728]{1,0:T(8,128)(2,1)} async-done(((bf16[144,1728]{1,0:T(8,128)(2,1)}), bf16[1152,1728]{1,0:T(8,128)(2,1)}) %all-gather.12.cloned.1.call-update) | async-done | bytes 3981328 | tf_op jit(solution)/shard_map/all_gather | solution.py:99
  222.4 6.1 convolution_convert_fusion.4
  230.7 37.3 %all-gather.14.cloned.1.call-done = bf16[512,1152]{0,1:T(8,128)(2,1)} async-done(((bf16[128,1152]{0,1:T(8,128)(2,1)}), bf16[512,1152]{0,1:T(8,128)(2,1)}) %all-gather.14.cloned.1.call-update) | async-done | bytes 1179664 | tf_op jit(solution)/shard_map/all_gather | solution.py:121
  268.1 34.1 %all-reduce.28.cloned.1.call-done = bf16[512,1152]{0,1:T(8,128)(2,1)} async-done(((bf16[512,1152]{0,1:T(8,128)(2,1)}), bf16[512,1152]{0,1:T(8,128)(2,1)}) %all-reduce.28.cloned.1.call-update) | async-done | bytes 1179664 | tf_op jit(solution)/shard_map/psum | solution.py:128
  302.2 2.3 multiply_reduce_fusion.2
  304.6 10.3 %multiply_convert_fusion = (bf16[512,1728]{0,1:T(8,128)(2,1)S(1)}, bf16[512,1728]{0,1:T(8,128)(2,1)S(1)}) fusion(f32[512,1728]{0,1:T(8,128)} %fusion.72, f32[512,1728]{0,1:T(8,128)} %get-tuple-element.184, bf16[1152,1728]{1,0:T(8,128)(2,1)} %all-gather.12.cloned.1.call-done, bf16[512,1152]{0,1:T(8,128)(2,1)S(1)} %copy-done.13, ...), kind=kOutput, calls=%fused_computation.13 | convolution fusion | flops 2068512768 | bytes 16968192 | tf_op jit(solution)/shard_map/dot_general | solution.py:205
  315.0 2.3 fusion.73
  318.4 3.4 fusion.6
  323.3 54.2 %all-reduce.30.cloned.1.call-done = bf16[512,1152]{0,1:T(8,128)(2,1)} async-done(((bf16[512,1152]{0,1:T(8,128)(2,1)}), bf16[512,1152]{0,1:T(8,128)(2,1)}) %all-reduce.30.cloned.1.call-update) | async-done | bytes 1179664 | tf_op jit(solution)/shard_map/psum | solution.py:128
  379.5 2.4 multiply_reduce_fusion
  393.6 71.4 %all-reduce.32.cloned.1.call-done = bf16[512,1664]{0,1:T(8,128)(2,1)} async-done(((bf16[512,1664]{0,1:T(8,128)(2,1)}), bf16[512,1664]{0,1:T(8,128)(2,1)}) %all-reduce.32.cloned.1.call-update) | async-done | bytes 1703952 | tf_op jit(solution)/shard_map/psum | solution.py:128
  465.0 2.1 dynamic-slice_convert_fusion
  469.6 2.1 convolution_convert_fusion.9
  471.8 2.1 convolution_convert_fusion.8
  474.0 2.6 convolution_convert_fusion.6
  476.7 2.7 convolution_convert_fusion.7
  479.5 25.8 %reduce-scatter.10.cloned.1.call-done = bf16[144,256]{1,0:T(8,128)(2,1)} async-done(((bf16[1152,256]{1,0:T(8,128)(2,1)}), bf16[144,256]{1,0:T(8,128)(2,1)}) %reduce-scatter.10.cloned.1.call-update) | async-done | bytes 73744 | tf_op jit(solution)/shard_map/reduce_scatter | solution.py:283
  505.3 37.6 %reduce-scatter.12.cloned.1.call-done = bf16[144,256]{1,0:T(8,128)(2,1)} async-done(((bf16[1152,256]{1,0:T(8,128)(2,1)}), bf16[144,256]{1,0:T(8,128)(2,1)}) %reduce-scatter.12.cloned.1.call-update) | async-done | bytes 73744 | tf_op jit(solution)/shard_map/reduce_scatter | solution.py:286
  542.9 6.9 convolution_convert_fusion
  549.8 6.2 convolution_convert_fusion.2
  556.2 6.2 convolution_convert_fusion.1
  572.0 3.3 reduce.7
  576.2 3.8 all-to-all-start.1
  585.4 2.4 reduce.8
  588.6 4.2 all-to-all-start.3
  596.7 21.0 %reduce-scatter.8.cloned.1.call-done = bf16[144,256]{1,0:T(8,128)(2,1)} async-done(((bf16[1152,256]{1,0:T(8,128)(2,1)}), bf16[144,256]{1,0:T(8,128)(2,1)}) %reduce-scatter.8.cloned.1.call-update) | async-done | bytes 73744 | tf_op jit(solution)/shard_map/reduce_scatter | solution.py:280
  619.2 22.5 %all-reduce.16 = (bf16[1152]{0:T(1024)(128)(2,1)S(1)}, bf16[1152]{0:T(1024)(128)(2,1)S(1)}, bf16[1152]{0:T(1024)(128)(2,1)S(1)}, bf16[1152]{0:T(1024)(128)(2,1)S...) all-reduce(bf16[1152]{0:T(1024)(128)(2,1)S(1)} %get-tuple-element.1, ...), channel_id=9, replica_groups=mesh['wide'=8,'narrow'=4] {'wide'}, use_global_device_ids=true, to_apply=%region_31.32.clone | all-reduce | flops 5120 | bytes 20480
  642.2 11.7 %all-reduce.18 = (bf16[144]{0:T(256)(128)(2,1)S(1)}, bf16[144]{0:T(256)(128)(2,1)S(1)}, bf16[144]{0:T(256)(128)(2,1)S(1)}, bf16[144]{0:T(256)(128)(2,1)S(1)}, bf...) all-reduce(bf16[144]{0:T(256)(128)(2,1)S(1)} %dynamic-slice.7, ...), channel_id=1, replica_groups=mesh['wide'=8,'narrow'=4] {'narrow'}, use_global_device_ids=true, to_apply=%region_32.33 | all-reduce | flops 640 | bytes 2560 | tf_op jit(solution)/shard_map/psum | solution.py:325
  661.3 11.0 %reduce-scatter.20.cloned.1.call-done = bf16[144,1728]{1,0:T(8,128)(2,1)} async-done(((bf16[1152,1728]{1,0:T(8,128)(2,1)}), bf16[144,1728]{1,0:T(8,128)(2,1)}) %reduce-scatter.20.cloned.1.call-update) | async-done | bytes 497680 | tf_op jit(solution)/shard_map/reduce_scatter | solution.py:298
  672.3 2.1 convert_element_type.304
  674.3 52.7 %reduce-scatter.16.cloned.1.call-done = bf16[144,1728]{1,0:T(8,128)(2,1)} async-done(((bf16[1152,1728]{1,0:T(8,128)(2,1)}), bf16[144,1728]{1,0:T(8,128)(2,1)}) %reduce-scatter.16.cloned.1.call-update) | async-done | bytes 497680 | tf_op jit(solution)/shard_map/reduce_scatter | solution.py:292
  727.0 2.1 convert_element_type.300
  729.1 52.5 %reduce-scatter.18.cloned.1.call-done = bf16[144,1728]{1,0:T(8,128)(2,1)} async-done(((bf16[1152,1728]{1,0:T(8,128)(2,1)}), bf16[144,1728]{1,0:T(8,128)(2,1)}) %reduce-scatter.18.cloned.1.call-update) | async-done | bytes 497680 | tf_op jit(solution)/shard_map/reduce_scatter | solution.py:295
  781.6 2.1 convert_element_type.302
  (332 shorter events, 76.2 us)
Async XLA Ops:
  8.0 67.4 %copy-start.46 = (bf16[144,256]{1,0:T(8,128)(2,1)S(1)}, bf16[144,256]{1,0:T(8,128)(2,1)}, u32[]{:S(2)}) copy-start(bf16[144,256]{1,0:T(8,128)(2,1)} %param.21) | copy-start | bytes 221188
  8.0 76.9 %copy-start.47 = (bf16[144,256]{1,0:T(8,128)(2,1)S(1)}, bf16[144,256]{1,0:T(8,128)(2,1)}, u32[]{:S(2)}) copy-start(bf16[144,256]{1,0:T(8,128)(2,1)} %param.22) | copy-start | bytes 221188
  8.0 86.5 %all-gather.6.cloned.1.call-start = ((), (), s32[]{:S(2)}) async-start(), calls=%async_computation.11 | async-start | bytes 1474560 | tf_op jit(solution)/shard_map/all_gather | solution.py:120
  21.5 142.2 %all-reduce.26.cloned.1.call-start = ((), (), s32[]{:S(2)}) async-start(), calls=%async_computation.12 | async-start | bytes 2359296 | tf_op jit(solution)/shard_map/psum | solution.py:128
  55.8 45.5 %copy-start.71 = (f32[128]{0:T(128)}, f32[128]{0:T(128)S(1)}, u32[]{:S(2)}) copy-start(f32[128]{0:T(128)S(1)} %multiply_exponential_fusion) | copy-start | bytes 1540
  56.4 44.8 %copy-start.49 = (f32[512]{0:T(512)}, f32[512]{0:T(512)S(1)}, u32[]{:S(2)}) copy-start(f32[512]{0:T(512)S(1)} %get-tuple-element.188) | copy-start | bytes 6148
  66.0 31.9 %copy-start.20 = (bf16[1152,256]{1,0:T(8,128)(2,1)}, bf16[1152,256]{1,0:T(8,128)(2,1)S(1)}, u32[]{:S(2)}) copy-start(bf16[1152,256]{1,0:T(8,128)(2,1)S(1)} %all_gather.61) | copy-start | bytes 1769476
  75.4 23.1 %copy-start.21 = (bf16[1152,256]{1,0:T(8,128)(2,1)}, bf16[1152,256]{1,0:T(8,128)(2,1)S(1)}, u32[]{:S(2)}) copy-start(bf16[1152,256]{1,0:T(8,128)(2,1)S(1)} %all_gather.63) | copy-start | bytes 1769476
  84.9 17.5 %copy-start.19 = (bf16[1152,256]{1,0:T(8,128)(2,1)}, bf16[1152,256]{1,0:T(8,128)(2,1)S(1)}, u32[]{:S(2)}) copy-start(bf16[1152,256]{1,0:T(8,128)(2,1)S(1)} %all_gather.60) | copy-start | bytes 1769476
  94.4 9.6 %copy-start.23 = (bf16[1152,256]{1,0:T(8,128)(2,1)}, bf16[1152,256]{1,0:T(8,128)(2,1)S(1)}, u32[]{:S(2)}) copy-start(bf16[1152,256]{1,0:T(8,128)(2,1)S(1)} %all_gather.65) | copy-start | bytes 1769476
  94.4 4.7 copy-start.63
  94.5 6.7 copy-start.65
  105.2 6.8 copy-start.75
  105.2 6.8 copy-start.74
  106.7 59.1 %copy-start.1 = (bf16[512,1152]{0,1:T(8,128)(2,1)S(1)}, bf16[512,1152]{0,1:T(8,128)(2,1)}, u32[]{:S(2)}) copy-start(bf16[512,1152]{0,1:T(8,128)(2,1)} %all-gather.6.cloned.1.call-done) | copy-start | bytes 3538948
  106.7 62.4 %all-gather.8.cloned.1.call-start = ((), (), s32[]{:S(2)}) async-start(), calls=%async_computation.13 | async-start | bytes 4644864 | tf_op jit(solution)/shard_map/all_gather | solution.py:97
  107.3 77.0 %all-gather.10.cloned.1.call-start = ((), (), s32[]{:S(2)}) async-start(), calls=%async_computation.14 | async-start | bytes 4644864 | tf_op jit(solution)/shard_map/all_gather | solution.py:98
  107.9 114.5 %all-gather.12.cloned.1.call-start = ((), (), s32[]{:S(2)}) async-start(), calls=%async_computation.15 | async-start | bytes 4644864 | tf_op jit(solution)/shard_map/all_gather | solution.py:99
  108.4 10.7 %all-to-all-start.2 = ((bf16[8,1,16,1152]{3,2,1,0:T(8,128)(2,1)}), bf16[8,1,16,1152]{3,2,1,0:T(8,128)(2,1)S(1)}, u32[]{:S(2)}, u32[]{:S(2)}) async-start(bf16[8,1,16,1152]{3,2,1,0:T(8,128)(2,1)} %param.17), calls=%async_computation.2 | async-start | bytes 589824 | tf_op jit(solution)/shard_map/all_to_all | solution.py:85
  111.9 156.2 %all-gather.14.cloned.1.call-start = ((), (), s32[]{:S(2)}) async-start(), calls=%async_computation.17 | async-start | bytes 1474560 | tf_op jit(solution)/shard_map/all_gather | solution.py:121
  120.0 182.2 %all-reduce.28.cloned.1.call-start = ((), (), s32[]{:S(2)}) async-start(), calls=%async_computation.16 | async-start | bytes 2359296 | tf_op jit(solution)/shard_map/psum | solution.py:128
  169.0 15.3 %copy-start.28 = (bf16[512,1152]{0,1:T(8,128)(2,1)}, bf16[512,1152]{0,1:T(8,128)(2,1)S(1)}, u32[]{:S(2)}) copy-start(bf16[512,1152]{0,1:T(8,128)(2,1)S(1)} %multiply_convert_fusion.2) | copy-start | bytes 3538948
  222.4 7.8 copy-start.73
  228.5 149.0 %all-reduce.30.cloned.1.call-start = ((), (), s32[]{:S(2)}) async-start(), calls=%async_computation.18 | async-start | bytes 2359296 | tf_op jit(solution)/shard_map/psum | solution.py:128
  268.1 36.5 %copy-start.11 = (bf16[512,1152]{0,1:T(8,128)(2,1)S(1)}, bf16[512,1152]{0,1:T(8,128)(2,1)}, u32[]{:S(2)}) copy-start(bf16[512,1152]{0,1:T(8,128)(2,1)} %all-gather.14.cloned.1.call-done) | copy-start | bytes 3538948
  304.6 10.4 %copy-start.79 = (f32[512]{0:T(512)}, f32[512]{0:T(512)S(1)}, u32[]{:S(2)}) copy-start(f32[512]{0:T(512)S(1)} %get-tuple-element.172) | copy-start | bytes 6148
  304.6 10.4 %copy-start.80 = (f32[512]{0:T(512)}, f32[512]{0:T(512)S(1)}, u32[]{:S(2)}) copy-start(f32[512]{0:T(512)S(1)} %get-tuple-element.171) | copy-start | bytes 6148
  304.6 10.3 %copy-start.85 = (bf16[1152,1728]{1,0:T(8,128)(2,1)S(1)}, bf16[1152,1728]{1,0:T(8,128)(2,1)}, u32[]{:S(2)}) copy-start(bf16[1152,1728]{1,0:T(8,128)(2,1)} %all-gather.8.cloned.1.call-done) | copy-start | bytes 11943940
  321.9 57.5 %copy-start = (bf16[512,1152]{0,1:T(8,128)(2,1)S(1)}, bf16[512,1152]{0,1:T(8,128)(2,1)}, u32[]{:S(2)}) copy-start(bf16[512,1152]{0,1:T(8,128)(2,1)} %all-reduce.26.cloned.1.call-done) | copy-start | bytes 3538948
  321.9 143.1 %all-reduce.32.cloned.1.call-start = ((), (), s32[]{:S(2)}) async-start(), calls=%async_computation.19 | async-start | bytes 3407872 | tf_op jit(solution)/shard_map/psum | solution.py:128
  391.9 76.3 %copy-start.64 = (f32[256]{0:T(256)S(1)}, f32[256]{0:T(256)}, u32[]{:S(2)}) copy-start(f32[256]{0:T(256)} %copy-done.63) | copy-start | bytes 3076
  391.9 113.3 %reduce-scatter.10.cloned.1.call-start = ((), (), s32[]{:S(2)}) async-start(), calls=%async_computation.21 | async-start | bytes 663552 | tf_op jit(solution)/shard_map/reduce_scatter | solution.py:283
  471.8 71.1 %reduce-scatter.12.cloned.1.call-start = ((), (), s32[]{:S(2)}) async-start(), calls=%async_computation.22 | async-start | bytes 663552 | tf_op jit(solution)/shard_map/reduce_scatter | solution.py:286
  473.9 69.0 %copy-start.45 = (f32[1152]{0:T(1024)S(1)}, f32[1152]{0:T(1024)}, u32[]{:S(2)}) copy-start(f32[1152]{0:T(1024)} %convert_add_fusion) | copy-start | bytes 13828
  474.0 121.2 %reduce-scatter.14.cloned.1.call-start = ((), (), s32[]{:S(2)}) async-start(), calls=%async_computation.23 | async-start | bytes 663552 | tf_op jit(solution)/shard_map/reduce_scatter | solution.py:289
  476.6 141.0 %reduce-scatter.8.cloned.1.call-start = ((), (), s32[]{:S(2)}) async-start(), calls=%async_computation.20 | async-start | bytes 663552 | tf_op jit(solution)/shard_map/reduce_scatter | solution.py:280
  479.4 178.7 %all-reduce.34.cloned.1.call-start = ((), (), s32[]{:S(2)}) async-start(), calls=%async_computation.27 | async-start | bytes 294912 | tf_op jit(solution)/shard_map/psum | solution.py:323
  542.8 129.4 %reduce-scatter.20.cloned.1.call-start = ((), (), s32[]{:S(2)}) async-start(), calls=%async_computation.26 | async-start | bytes 4644864 | tf_op jit(solution)/shard_map/reduce_scatter | solution.py:298
  549.8 177.2 %reduce-scatter.16.cloned.1.call-start = ((), (), s32[]{:S(2)}) async-start(), calls=%async_computation.24 | async-start | bytes 4644864 | tf_op jit(solution)/shard_map/reduce_scatter | solution.py:292
  556.1 225.5 %reduce-scatter.18.cloned.1.call-start = ((), (), s32[]{:S(2)}) async-start(), calls=%async_computation.25 | async-start | bytes 4644864 | tf_op jit(solution)/shard_map/reduce_scatter | solution.py:295
  568.4 11.5 %copy-start.18 = (f32[128,1664]{0,1:T(8,128)S(1)}, f32[128,1664]{0,1:T(8,128)}, u32[]{:S(2)}) copy-start(f32[128,1664]{0,1:T(8,128)} %get-tuple-element.156) | copy-start | bytes 2555908
  570.2 11.1 %copy-start.9 = (f32[512,1152]{0,1:T(8,128)S(1)}, f32[512,1152]{0,1:T(8,128)}, u32[]{:S(2)}) copy-start(f32[512,1152]{0,1:T(8,128)} %copy-done.8) | copy-start | bytes 7077892
  570.2 11.1 %copy-start.76 = (f32[128]{0:T(128)S(1)}, f32[128]{0:T(128)}, u32[]{:S(2)}) copy-start(f32[128]{0:T(128)} %fusion.61) | copy-start | bytes 1540
  576.2 6.7 copy-start.82
  576.2 12.4 %all-to-all-start.1 = ((bf16[8,2,9216]{2,1,0:T(2,128)(2,1)}), bf16[8,2,9216]{2,1,0:T(2,128)(2,1)S(1)}, u32[]{:S(2)}, u32[]{:S(2)}) async-start(bf16[8,2,9216]{2,1,0:T(2,128)(2,1)} %reshape.545), calls=%async_computation.1 | async-start | bytes 589824 | tf_op jit(solution)/shard_map/all_to_all | solution.py:333
  585.4 33.8 %copy-start.77 = (bf16[256]{0:T(256)(128)(2,1)S(1)}, bf16[256]{0:T(256)(128)(2,1)}, u32[]{:S(2)}) copy-start(bf16[256]{0:T(256)(128)(2,1)} %get-tuple-element.121) | copy-start | bytes 1540
  585.4 33.8 %copy-start.78 = (bf16[256]{0:T(256)(128)(2,1)S(1)}, bf16[256]{0:T(256)(128)(2,1)}, u32[]{:S(2)}) copy-start(bf16[256]{0:T(256)(128)(2,1)} %get-tuple-element.123) | copy-start | bytes 1540
  588.6 68.5 %all-to-all-start.3 = ((bf16[8,2,9216]{2,1,0:T(2,128)(2,1)}), bf16[8,2,9216]{2,1,0:T(2,128)(2,1)S(1)}, u32[]{:S(2)}, u32[]{:S(2)}) async-start(bf16[8,2,9216]{2,1,0:T(2,128)(2,1)} %reshape.547), calls=%async_computation.3 | async-start | bytes 589824 | tf_op jit(solution)/shard_map/all_to_all | solution.py:336
  (61 other events, 118.1 us)
Sparse Core Ops, SparseCore 0:
  21.6 31.1 all-gather.5
  106.8 56.8 all-reduce.25
  228.6 73.5 all-reduce.27
  322.0 55.4 all-reduce.29
  392.0 72.9 all-reduce.31
  543.0 34.4 all-reduce.33
Sparse Core Ops, SparseCore 1:
  109.1 37.1 all-gather.7
  148.0 36.2 all-gather.9
  186.1 36.2 all-gather.11
  224.5 43.5 all-gather.13
  471.8 33.4 reduce-scatter.9
  508.4 34.4 reduce-scatter.11
  545.8 34.4 reduce-scatter.13
  583.2 34.3 reduce-scatter.7
  621.3 50.9 reduce-scatter.19
  676.1 50.9 reduce-scatter.15
  730.7 50.9 reduce-scatter.17
where the time goes:
time: 801 us; the launch traced here: 792 us
  waiting for transfers between devices  487 us (61%)
  blocking collectives  109 us (14%)
  matrix products  76 us (9%)
  other arithmetic  59.4 us (7%)
  local copies, waits for them, and re-layouts  26.7 us (3%)
  between operations  21.2 us (3%)
  starting transfers between devices  12.9 us (2%)
    psum x4, waiting for transfers between devices, total(): return lax.psum(value.astype(jnp.bfloat16), 'narrow').astype(jnp.float32)  203 us
    reduce_scatter x1, waiting for transfers between devices, on_device(): lax.psum_scatter(grad_gate.astype(jnp.bfloat16), 'wide', scatter_dimensio...  52.7 us
    reduce_scatter x1, waiting for transfers between devices, on_device(): lax.psum_scatter(grad_up.astype(jnp.bfloat16), 'wide', scatter_dimension=...  52.5 us
    unnamed x2, blocking collectives  46.4 us
    reduce_scatter x1, waiting for transfers between devices, on_device(): lax.psum_scatter(grad_value.astype(jnp.bfloat16), 'wide', scatter_dimensi...  37.6 us
    all_gather x1, waiting for transfers between devices, on_device(): lax.all_gather(own_dy, 'narrow', axis=0, tiled=True)  37.3 us
    all_gather x1, waiting for transfers between devices, on_device(): lax.all_gather(down_weight, 'wide', axis=0, tiled=True)  29.1 us
    reduce_scatter x1, waiting for transfers between devices, on_device(): lax.psum_scatter(grad_key.astype(jnp.bfloat16), 'wide', scatter_dimension...  25.8 us
  transfers between devices with their start and end apart: 20, of which 14 were waited for; matrix products, arithmetic and copies ran while one was open for 13% of the time, Pallas kernels for 0%

commit v1 on v0

v1 whole, which is shorter than its diff:
```python
import functools
import math

import jax
import jax.numpy as jnp
from jax import lax
from jax.experimental import pallas as pl
from jax.experimental.pallas import tpu as pltpu
from jax.sharding import PartitionSpec as P

EPS = 1e-06
SCALE = 0.0625
LOGBASE = math.log(1000000.0)
GELU_C = 0.7978845608028654
GELU_A = 0.044715
F32, BF16 = jnp.float32, jnp.bfloat16
VMEM_LIMIT = 60 * 1024 * 1024


def call(kernel, outs, scratch=(), anys=(), smem=(), count=0, flops=0, moved=0):
    def place(index):
        if index in anys:
            return pl.BlockSpec(memory_space=pl.ANY)
        if index in smem:
            return pl.BlockSpec(memory_space=pltpu.SMEM)
        return pl.BlockSpec(memory_space=pltpu.VMEM)

    return pl.pallas_call(
        kernel,
        out_shape=[jax.ShapeDtypeStruct(s, d) for s, d in outs],
        in_specs=[place(i) for i in range(count)],
        out_specs=[pl.BlockSpec(memory_space=pltpu.VMEM)] * len(outs),
        scratch_shapes=list(scratch),
        compiler_params=pltpu.CompilerParams(vmem_limit_bytes=VMEM_LIMIT),
        cost_estimate=pl.CostEstimate(flops=flops, bytes_accessed=moved, transcendentals=0),
    )


def mm(a, b):
    return lax.dot_general(a, b, (((1,), (0,)), ((), ())), preferred_element_type=F32)


def mm_nt(a, b):
    return lax.dot_general(a, b, (((1,), (1,)), ((), ())), preferred_element_type=F32)


def mm_tn(a, b):
    return lax.dot_general(a, b, (((0,), (0,)), ((), ())), preferred_element_type=F32)


def root(v):
    return lax.rsqrt(jnp.mean(v * v, axis=-1, keepdims=True) + EPS)


def norm(v, gain):
    return v * root(v) * (1.0 + gain)


def norm_back(v, grad, gain):
    r = root(v)
    e = grad * (1.0 + gain)
    return r * e - v * (r * r * r * jnp.mean(e * v, axis=-1, keepdims=True))


def norm_term(v, grad):
    return jnp.sum(grad * v * root(v), axis=0, keepdims=True)


def rotate(v, cosine, sine):
    half = v.shape[-1] // 2
    a, b = v[:, :half], v[:, half:]
    return jnp.concatenate([a * cosine - b * sine, b * cosine + a * sine], axis=-1)


def rotate_back(v, cosine, sine):
    half = v.shape[-1] // 2
    a, b = v[:, :half], v[:, half:]
    return jnp.concatenate([a * cosine + b * sine, b * cosine - a * sine], axis=-1)


def tiles(extent, size):
    return [(i, min(size, extent - i)) for i in range(0, extent, size)]


def packing(q_ref, k_ref, v_ref, o_ref, g0_ref, g1_ref, g2_ref, g3_ref, g4_ref, g5_ref, out_ref):
    rows, head = q_ref.shape
    for i, ref in enumerate((q_ref, k_ref, v_ref, o_ref)):
        out_ref[:, i * head : (i + 1) * head] = ref[...]
    lane = lax.broadcasted_iota(jnp.int32, (rows, 128), 1)
    columns = jnp.zeros((rows, 128), F32)
    for i, ref in enumerate((g0_ref, g1_ref, g2_ref, g3_ref, g4_ref, g5_ref)):
        n = ref.shape[0]
        same = lax.broadcasted_iota(jnp.int32, (rows, n), 0) == lax.broadcasted_iota(
            jnp.int32, (rows, n), 1
        )
        column = jnp.sum(jnp.where(same, ref[...].astype(F32)[None, :], 0.0), axis=1, keepdims=True)
        columns = jnp.where(lane == i, column, columns)
    out_ref[:, 4 * head :] = columns.astype(BF16)


def one_hot(order_ref, rows):
    index = lax.broadcasted_iota(jnp.int32, (rows, order_ref.shape[1]), 0)
    return jnp.where(index == order_ref[...], 1.0, 0.0).astype(BF16)


def fetch(pieces, slot, target, sem):
    own, below, above = pieces
    n, count = own.shape[0], len(below) + 1

    def copy(ref, at, i):
        at = pl.multiple_of(at * n, n)
        return pltpu.make_async_copy(ref, target.at[pl.ds(at, n)], sem.at[i])

    def each(act):
        act(copy(own, slot, 0))
        for s in range(1, count):

            @pl.when(slot >= s)
            def _(s=s):
                act(copy(below[s - 1], slot - s, 2 * s - 1))

            @pl.when(slot + s < count)
            def _(s=s):
                act(copy(above[s - 1], slot + s, 2 * s))

    each(lambda c: c.start())
    return lambda: each(lambda c: c.wait())


def attention_forward(
    own_ref, b1_ref, b2_ref, b3_ref, a1_ref, a2_ref, a3_ref,
    order_ref, pick_ref, wm_ref, wo_ref, cos_ref, sin_ref, segc_ref, segr_ref, slot_ref,
    xp_ref, xn1_ref, qraw_ref, kraw_ref, q_ref, k_ref, v_ref, probs_ref, att_ref, part_ref,
    gains_ref, hgain_ref,
    x_ref, w_ref, sem, xsem,
):
    half, head = wm_ref.shape[0], q_ref.shape[1]
    rows, width = x_ref.shape
    arrived = fetch(
        (own_ref, (b1_ref, b2_ref, b3_ref), (a1_ref, a2_ref, a3_ref)), slot_ref[0], x_ref, xsem
    )
    low = pltpu.make_async_copy(wm_ref, w_ref.at[pl.ds(0, half)], sem.at[0])
    high = pltpu.make_async_copy(wo_ref, w_ref.at[pl.ds(half, half)], sem.at[1])
    low.start()
    high.start()
    choose = one_hot(order_ref, width)
    low.wait()
    high.wait()
    columns = w_ref[:, 4 * head :].T
    gains_ref[...] = columns[:8].astype(F32)
    hgain_ref[...] = mm(columns[:8], one_hot(pick_ref, width))
    arrived()
    step = 128
    for r, n in tiles(rows, step):
        x = mm(x_ref[pl.ds(r, n), :], choose)
        xp_ref[pl.ds(r, n), :] = x.astype(BF16)
        xn1_ref[pl.ds(r, n), :] = norm(x, gains_ref[0:1, :]).astype(BF16)
    gq, gk = hgain_ref[4:5, :], hgain_ref[5:6, :]
    raw = mm(xn1_ref[...], w_ref[:, : 3 * head])
    qraw_ref[...] = raw[:, :head]
    kraw_ref[...] = raw[:, head : 2 * head]
    v_ref[...] = raw[:, 2 * head :].astype(BF16)
    cosine, sine = cos_ref[...], sin_ref[...]
    q_ref[...] = rotate(norm(raw[:, :head], gq), cosine, sine).astype(BF16)
    k_ref[...] = rotate(norm(raw[:, head : 2 * head], gk), cosine, sine).astype(BF16)
    for r, n in tiles(rows, step):
        s = mm_nt(q_ref[pl.ds(r, n), :], k_ref[...]) * SCALE
        row = lax.broadcasted_iota(jnp.int32, s.shape, 0) + r
        col = lax.broadcasted_iota(jnp.int32, s.shape, 1)
        keep = (segc_ref[pl.ds(r, n), :] == segr_ref[...]) & (col <= row)
        s = jnp.where(keep, s, -1e30)
        e = jnp.exp(s - jnp.max(s, axis=-1, keepdims=True))
        p = e / jnp.sum(e, axis=-1, keepdims=True)
        probs_ref[pl.ds(r, n), :] = p
        att_ref[pl.ds(r, n), :] = mm(p.astype(BF16), v_ref[...]).astype(BF16)
    part_ref[...] = mm_nt(att_ref[...], w_ref[:, 3 * head : 4 * head]).astype(BF16)


def total(ref):
    out = ref[0].astype(F32)
    for i in range(1, ref.shape[0]):
        out = out + ref[i].astype(F32)
    return out


def middle_forward(z_ref, xp_ref, gains_ref, slot_ref, mixed_ref, h_ref, xn2_ref):
    n = h_ref.shape[0]
    x = xp_ref[pl.ds(pl.multiple_of(slot_ref[0] * n, n), n), :].astype(F32)
    z = total(z_ref)
    h = x + norm(z, gains_ref[1:2, :])
    mixed_ref[...] = z
    h_ref[...] = h
    xn2_ref[...] = norm(h, gains_ref[2:3, :]).astype(BF16)


def ffn_forward(
    own_ref, b1_ref, b2_ref, b3_ref, a1_ref, a2_ref, a3_ref, wm_ref, wo_ref, slot_ref,
    xn2_ref, act_ref, fa_ref, fb_ref, part_ref, w_ref, sem, xsem,
):
    half = wm_ref.shape[1]
    arrived = fetch(
        (own_ref, (b1_ref, b2_ref, b3_ref), (a1_ref, a2_ref, a3_ref)), slot_ref[0], xn2_ref, xsem
    )
    copies = []
    for i in range(3):
        for j, ref in enumerate((wm_ref, wo_ref)):
            c = pltpu.make_async_copy(
                ref.at[i], w_ref.at[i, pl.ds(j * half, half)], sem.at[2 * i + j]
            )
            c.start()
            copies.append(c)
    for c in copies[:4]:
        c.wait()
    arrived()
    x = xn2_ref[...]
    for f, n in tiles(act_ref.shape[1], 256):
        gate = mm(x, w_ref[0, :, pl.ds(f, n)])
        up = mm(x, w_ref[1, :, pl.ds(f, n)])
        square = gate * gate
        t = jnp.tanh(GELU_C * (gate + GELU_A * (gate * square)))
        bell = 0.5 * (1.0 + t)
        g = gate * bell
        slope = bell + 0.5 * gate * (1.0 - t * t) * (GELU_C * (1.0 + 3.0 * GELU_A * square))
        act_ref[:, pl.ds(f, n)] = (g * up).astype(BF16)
        fa_ref[:, pl.ds(f, n)] = (slope * up).astype(BF16)
        fb_ref[:, pl.ds(f, n)] = g.astype(BF16)
    for c in copies[4:]:
        c.wait()
    for d, n in tiles(part_ref.shape[1], 384):
        part_ref[:, pl.ds(d, n)] = mm_nt(act_ref[...], w_ref[2, pl.ds(d, n), :]).astype(BF16)


def middle_turn(
    m_ref, h_ref, dy_ref, order_ref, valid_ref, gains_ref, out_ref, dout_ref, dm_ref, term_ref
):
    choose = one_hot(order_ref, h_ref.shape[1])
    m = total(m_ref)
    gain = gains_ref[3:4, :]
    out = (h_ref[...] + norm(m, gain)).astype(BF16)
    out_ref[...] = mm_nt(out, choose).astype(BF16)
    dy = mm(dy_ref[...], choose) * valid_ref[...]
    dout_ref[...] = dy
    dm_ref[...] = norm_back(m, dy, gain).astype(BF16)
    term_ref[...] = norm_term(m, dy)


def ffn_backward(
    own_ref, b1_ref, b2_ref, b3_ref, a1_ref, a2_ref, a3_ref, fa_ref, fb_ref, wm_ref, wo_ref, slot_ref,
    dm_ref, dg_ref, du_ref, part_ref, w_ref, sem, xsem,
):
    half = wm_ref.shape[1]
    arrived = fetch(
        (own_ref, (b1_ref, b2_ref, b3_ref), (a1_ref, a2_ref, a3_ref)), slot_ref[0], dm_ref, xsem
    )
    copies = []
    for i in (2, 0, 1):
        for j, ref in enumerate((wm_ref, wo_ref)):
            c = pltpu.make_async_copy(
                ref.at[i], w_ref.at[i, pl.ds(j * half, half)], sem.at[2 * i + j]
            )
            c.start()
            copies.append(c)
    for c in copies[:2]:
        c.wait()
    arrived()
    dm = dm_ref[...]
    for f, n in tiles(dg_ref.shape[1], 256):
        d = mm(dm, w_ref[2, :, pl.ds(f, n)])
        dg_ref[:, pl.ds(f, n)] = (d * fa_ref[:, pl.ds(f, n)].astype(F32)).astype(BF16)
        du_ref[:, pl.ds(f, n)] = (d * fb_ref[:, pl.ds(f, n)].astype(F32)).astype(BF16)
    for c in copies[2:]:
        c.wait()
    for d, n in tiles(part_ref.shape[1], 384):
        part_ref[:, pl.ds(d, n)] = (
            mm_nt(dg_ref[...], w_ref[0, pl.ds(d, n), :])
            + mm_nt(du_ref[...], w_ref[1, pl.ds(d, n), :])
        ).astype(BF16)


def weight_grad(left_ref, right_ref, own_ref, other_ref, turned_ref):
    turned_ref[...] = left_ref[...].T
    half = own_ref.shape[0]
    for r, n in tiles(half, 192):
        for at, out in ((r, own_ref), (half + r, other_ref)):
            out[pl.ds(r, n), :] = mm(turned_ref[pl.ds(at, n), :], right_ref[...]).astype(BF16)


def ffn_weight_grads(
    dm_ref, xn2_ref, act_ref, dg_ref, du_ref, own_ref, other_ref, turned_ref, sem
):
    half = own_ref.shape[1]
    for i, (left, right) in enumerate(((xn2_ref, dg_ref), (xn2_ref, du_ref), (dm_ref, act_ref))):
        if i != 1:
            turned_ref[...] = left[...].T
        for r, n in tiles(half, 192):
            for at, out in ((r, own_ref), (half + r, other_ref)):
                out[i, pl.ds(r, n), :] = mm(turned_ref[pl.ds(at, n), :], right[...]).astype(BF16)


def middle_backward(
    g_ref, dout_ref, h_ref, mixed_ref, gains_ref, dh_ref, dz_ref, ffn_term_ref, att_term_ref
):
    dxn2 = total(g_ref)
    h = h_ref[...]
    dh = dout_ref[...] + norm_back(h, dxn2, gains_ref[2:3, :])
    mixed = mixed_ref[...]
    dh_ref[...] = dh
    dz_ref[...] = norm_back(mixed, dh, gains_ref[1:2, :]).astype(BF16)
    ffn_term_ref[...] = norm_term(h, dxn2)
    att_term_ref[...] = norm_term(mixed, dh)


def attention_backward(
    own_ref, b1_ref, b2_ref, b3_ref, a1_ref, a2_ref, a3_ref, slot_ref, wm_ref, wo_ref, qraw_ref, q_ref, k_ref, v_ref, probs_ref, hgain_ref, cos_ref, sin_ref,
    dz_ref, part_ref, dq_ref, term_ref,
    w_ref, datt_ref, ds_ref, sem, xsem,
):
    half, head = wm_ref.shape[0], q_ref.shape[1]
    rows, width = dz_ref.shape
    arrived = fetch(
        (own_ref, (b1_ref, b2_ref, b3_ref), (a1_ref, a2_ref, a3_ref)), slot_ref[0], dz_ref, xsem
    )
    low = pltpu.make_async_copy(wm_ref, w_ref.at[pl.ds(0, half)], sem.at[0])
    high = pltpu.make_async_copy(wo_ref, w_ref.at[pl.ds(half, half)], sem.at[1])
    low.start()
    high.start()
    low.wait()
    high.wait()
    arrived()
    datt_ref[...] = mm(dz_ref[...], w_ref[:, 3 * head : 4 * head]).astype(BF16)
    term = jnp.zeros((1, head), F32)
    for r, n in tiles(rows, 128):
        p = probs_ref[pl.ds(r, n), :]
        dp = mm_nt(datt_ref[pl.ds(r, n), :], v_ref[...])
        ds = (p * (dp - jnp.sum(dp * p, axis=-1, keepdims=True))).astype(BF16)
        ds_ref[pl.ds(r, n), :] = ds
        dq = (mm(ds, k_ref[...]) * SCALE).astype(BF16).astype(F32)
        cosine, sine = cos_ref[pl.ds(r, n), :], sin_ref[pl.ds(r, n), :]
        e = rotate_back(dq, cosine, sine)
        raw = qraw_ref[pl.ds(r, n), :]
        term = term + norm_term(raw, e)
        dq_ref[pl.ds(r, n), :] = norm_back(raw, e, hgain_ref[4:5, :]).astype(BF16)
    term_ref[...] = term
    part_ref[:, :width] = mm_nt(dq_ref[...], w_ref[:, :head]).astype(BF16)
    part_ref[:, width : width + head] = (mm_tn(ds_ref[...], q_ref[...]) * SCALE).astype(BF16)
    part_ref[:, width + head :] = mm_tn(probs_ref[...].astype(BF16), datt_ref[...]).astype(BF16)


def last_rows(
    g_ref, xp_ref, xn1_ref, dh_ref, kraw_ref, cos_ref, sin_ref, hgain_ref, gains_ref, order_ref,
    pick_ref, slot_ref, t1_ref, t2_ref, t3_ref, qterm_ref, wm_ref, wo_ref,
    out_ref, own_ref, other_ref,
    w_ref, sem,
):
    half, head = wm_ref.shape[0], kraw_ref.shape[1]
    n, width = dh_ref.shape
    low = pltpu.make_async_copy(wm_ref, w_ref.at[pl.ds(0, half)], sem.at[0])
    high = pltpu.make_async_copy(wo_ref, w_ref.at[pl.ds(half, half)], sem.at[1])
    low.start()
    high.start()
    here = pl.ds(pl.multiple_of(slot_ref[0] * n, n), n)
    joined = total(g_ref)
    dk = joined[:, width : width + head].astype(BF16).astype(F32)
    e = rotate_back(dk, cos_ref[here, :], sin_ref[here, :])
    raw = kraw_ref[here, :]
    kterm = norm_term(raw, e)
    dkr = norm_back(raw, e, hgain_ref[5:6, :]).astype(BF16)
    dkv = jnp.concatenate([dkr, joined[:, width + head :].astype(BF16)], axis=1)
    low.wait()
    high.wait()
    dxn1 = joined[:, :width] + mm_nt(dkv, w_ref[:, head : 3 * head])
    x = xp_ref[here, :].astype(F32)
    dx = (dh_ref[...] + norm_back(x, dxn1, gains_ref[0:1, :])).astype(BF16)
    term = norm_term(x, dxn1)
    choose = one_hot(order_ref, width)
    out_ref[...] = mm_nt(dx, choose).astype(BF16)
    grad = mm_tn(xn1_ref[here, :], dkv)
    own_ref[:, : 2 * head] = grad[:half].astype(BF16)
    other_ref[:, : 2 * head] = grad[half:].astype(BF16)
    small = jnp.concatenate([qterm_ref[...], kterm, jnp.zeros((6, head), F32)], axis=0)
    small = mm_nt(small.astype(BF16), one_hot(pick_ref, width))
    terms = [term, t1_ref[...], t2_ref[...], t3_ref[...], small[0:2], jnp.zeros((122, width), F32)]
    terms = jnp.concatenate(terms, axis=0).T
    own_ref[:, 2 * head :] = terms[:half].astype(BF16)
    other_ref[:, 2 * head :] = terms[half:].astype(BF16)


def rope_tables(place, width):
    half = width // 2
    expo = jnp.arange(half, dtype=jnp.float32) * (-2.0 / width)
    freqs = jnp.exp(expo * LOGBASE)
    angle = place.astype(jnp.float32)[:, None] * freqs[None, :]
    return (jnp.cos(angle), jnp.sin(angle))


def bucket_layout(lengths, rows):
    position = jnp.arange(rows, dtype=jnp.int32)
    first = lengths[0]
    ends = lengths[0] + lengths[1]
    segment = jnp.where(position < first, 0, jnp.where(position < ends, 1, 2)).astype(jnp.int32)
    begin = jnp.where(segment == 0, 0, jnp.where(segment == 1, first, ends))
    return (segment, position - begin)


def on_device(
    tokens,
    cotangent,
    seq_lengths,
    query_weight,
    key_weight,
    value_weight,
    outproj_weight,
    gate_weight,
    up_weight,
    down_weight,
    attn_gain,
    attnout_gain,
    ffn_gain,
    ffnout_gain,
    query_gain,
    key_gain,
):
    width = tokens.shape[3]
    wide, narrow = lax.axis_size("wide"), lax.axis_size("narrow")
    chips = wide // 2
    core = lax.axis_index("wide") % 2
    slot = lax.axis_index("narrow")
    slots = jnp.reshape(slot, (1,)).astype(jnp.int32)
    same_core = [[i for i in range(wide) if i % 2 == c] for c in range(2)]
    swap = [(i, i ^ 1) for i in range(wide)]
    upward = [(i, i + 1) for i in range(narrow - 1)]
    downward = [(i + 1, i) for i in range(narrow - 1)]
    dw = width // wide
    dh = query_gain.shape[0]
    head = key_weight.shape[1]
    units = gate_weight.shape[1]
    half = width // 2

    j = jnp.arange(width, dtype=jnp.int32)
    chip, side, rest = (j % half) // dw, j // half, j % dw
    order = ((2 * chip + (core + side) % 2) * dw + rest)[None, :]

    def gather_wide(value, axis):
        return lax.all_gather(
            value, "wide", axis=axis, tiled=True, axis_index_groups=same_core
        )

    def sibling(value):
        return lax.ppermute(value, "wide", swap)

    def pair_sum(own, other):
        return (own.astype(F32) + sibling(other).astype(F32)).astype(BF16)

    def scatter_wide(value, axis):
        return lax.psum_scatter(
            value, "wide", scatter_dimension=axis, tiled=True, axis_index_groups=same_core
        )

    def after(value, *others):
        return lax.optimization_barrier((value, *others))[0]

    def gather_z(value, hook=None):
        up = down = value
        below, above = [], []
        for s in range(1, narrow):
            up = lax.ppermute(up, "narrow", upward)
            down = lax.ppermute(down, "narrow", downward)
            below.append(up)
            above.append(down)
            if hook is not None:
                hook((up, down), s)
        return [value] + below + above

    def exchange_z(value):
        parts = value.reshape(narrow, -1, value.shape[1])
        return lax.all_to_all(parts, "narrow", split_axis=0, concat_axis=0, tiled=True)

    def enter(value):
        value = value.reshape(value.shape[0], value.shape[2], width)
        value = lax.all_to_all(value, "wide", split_axis=0, concat_axis=0, tiled=True)
        return value.reshape(-1, width)

    def leave(value):
        value = value.reshape(wide, -1, width)
        value = lax.all_to_all(value, "wide", split_axis=0, concat_axis=0, tiled=True)
        return value.reshape(wide, 1, -1, width)

    bf, ff = BF16, F32
    pack = call(packing, [((dw, 4 * head + 128), bf)], count=10, flops=10**6, moved=10**6)(
        query_weight, key_weight, value_weight, outproj_weight,
        attn_gain, attnout_gain, ffn_gain, ffnout_gain, query_gain, key_gain,
    )[0]
    own_x = enter(tokens)
    quarter = own_x.shape[0]
    rows = quarter * narrow
    wa_mine = gather_wide(pack, 0)
    held = {}

    def swap_attention(piece, step):
        if step == 1:
            parts = after(jnp.stack([gate_weight, up_weight, down_weight]), *piece)
            held["wf"] = gather_wide(parts, 1)
        if step == narrow - 1:
            held["wa"] = sibling(after(wa_mine, *piece))

    x_all = gather_z(own_x, swap_attention)
    wa_other, wf_mine = held["wa"], held["wf"]
    own_dy = enter(after(cotangent, own_x))
    segment, place = bucket_layout(seq_lengths[0], rows)
    cosine, sine = rope_tables(place, head)
    valid = lax.dynamic_slice_in_dim((segment < 2).astype(F32), slot * quarter, quarter)[:, None]
    t = jnp.arange(head, dtype=jnp.int32)
    owner = t // dh
    pick = (((owner % 2 + core) % 2) * half + (owner // 2) * dw + t % dh)[None, :]

    w_scratch = pltpu.VMEM((width, wa_mine.shape[1]), bf)
    f_scratch = pltpu.VMEM((3, width, units), bf)
    sem = pltpu.SemaphoreType.DMA
    xsem = sem((2 * narrow - 1,))
    seven = tuple(range(2 * narrow - 1))
    k0 = len(seven)
    xp, xn1, qraw, kraw, q, k, v, probs, attended, z_part, gains, hgain = call(
        attention_forward,
        [
            ((rows, width), bf), ((rows, width), bf), ((rows, head), ff), ((rows, head), ff),
            ((rows, head), bf), ((rows, head), bf), ((rows, head), bf), ((rows, rows), ff),
            ((rows, head), bf), ((rows, width), bf), ((8, width), ff), ((8, head), ff),
        ],
        scratch=[pltpu.VMEM((rows, width), bf), w_scratch, sem((2,)), xsem],
        anys=seven + (k0 + 2, k0 + 3), smem=(k0 + 8,), count=k0 + 9, flops=3 * 10**9, moved=8 * 10**6,
    )(*x_all, order, pick, wa_mine, wa_other, cosine, sine, segment[:, None], segment[None, :], slots)
    z = exchange_z(z_part)
    mixed, h, xn2_own = call(
        middle_forward,
        [((quarter, width), ff), ((quarter, width), ff), ((quarter, width), bf)],
        smem=(3,), count=4, flops=10**7, moved=3 * 10**6,
    )(z, xp, gains, slots)
    def swap_ffn(piece, step):
        if step == narrow - 2:
            held["wf"] = sibling(after(wf_mine, *piece))

    xn2_all = gather_z(xn2_own, swap_ffn)
    wf_other = held["wf"]
    xn2, act, fa, fb, m_part = call(
        ffn_forward,
        [((rows, width), bf)] + [((rows, units), bf)] * 3 + [((rows, width), bf)],
        scratch=[f_scratch, sem((6,)), xsem],
        anys=seven + (k0, k0 + 1), smem=(k0 + 2,), count=k0 + 3, flops=6 * 10**9, moved=20 * 10**6,
    )(*xn2_all, wf_mine, wf_other, slots)
    m = exchange_z(m_part)
    out_own, d_out, dm_own, ffnout_term = call(
        middle_turn,
        [((quarter, width), bf), ((quarter, width), ff), ((quarter, width), bf), ((1, width), ff)],
        count=6, flops=10**8, moved=4 * 10**6,
    )(m, h, own_dy, order, valid, gains)
    dm_all = gather_z(dm_own)
    dm, d_gate, d_up, dxn2_part = call(
        ffn_backward,
        [((rows, width), bf)] + [((rows, units), bf)] * 2 + [((rows, width), bf)],
        scratch=[f_scratch, sem((6,)), xsem],
        anys=seven + (k0 + 2, k0 + 3), smem=(k0 + 4,), count=k0 + 5, flops=6 * 10**9, moved=20 * 10**6,
    )(*dm_all, fa, fb, wf_mine, wf_other, slots)
    dxn2 = lax.psum_scatter(
        dxn2_part.reshape(narrow, quarter, width), "narrow", scatter_dimension=0, tiled=True
    )

    def outer(left, right):
        own, other = call(
            weight_grad,
            [((half, right.shape[1]), bf)] * 2,
            scratch=[pltpu.VMEM((width, left.shape[0]), bf)],
            count=2, flops=2 * width * left.shape[0] * right.shape[1], moved=8 * 10**6,
        )(left, right)
        return own, other

    ffn_own, ffn_other = call(
        ffn_weight_grads,
        [((3, half, units), bf)] * 2,
        scratch=[pltpu.VMEM((width, rows), bf), sem((2,))],
        count=5, flops=10**6, moved=10**6,
    )(dm, xn2, act, d_gate, d_up)
    ffn_sum = pair_sum(ffn_own, ffn_other)
    dxn2 = after(dxn2, ffn_sum)
    s_ffn = scatter_wide(ffn_sum, 1)
    left_out = leave(out_own)
    d_resid, dz_own, ffn_term, attnout_term = call(
        middle_backward,
        [((quarter, width), ff), ((quarter, width), bf), ((1, width), ff), ((1, width), ff)],
        count=5, flops=10**7, moved=4 * 10**6,
    )(dxn2, d_out, h, mixed, gains)
    dz_all = gather_z(dz_own)
    dz, joined_part, dq_raw, query_term = call(
        attention_backward,
        [((rows, width), bf), ((rows, width + 2 * head), bf), ((rows, head), bf), ((1, head), ff)],
        scratch=[
            w_scratch, pltpu.VMEM((rows, head), bf), pltpu.VMEM((rows, rows), bf), sem((2,)), xsem,
        ],
        smem=(k0,), anys=seven + (k0 + 1, k0 + 2), count=k0 + 11, flops=3 * 10**9, moved=8 * 10**6,
    )(*dz_all, slots, wa_mine, wa_other, qraw, q, k, v, probs, hgain, cosine, sine)
    joined = exchange_z(joined_part)
    g_outproj = outer(dz, attended)
    g_query = outer(xn1, dq_raw)
    s_ffn = s_ffn.astype(F32)
    joined = after(joined, left_out, s_ffn, *g_outproj, *g_query)
    s_outproj = scatter_wide(pair_sum(*g_outproj), 0)
    dx_own, own, other = call(
        last_rows,
        [((quarter, width), bf)] + [((half, 2 * head + 128), bf)] * 2,
        scratch=[w_scratch, sem((2,))],
        smem=(11,), anys=(16, 17), count=18, flops=10**9, moved=8 * 10**6,
    )(
        joined, xp, xn1, d_resid, kraw, cosine, sine, hgain, gains, order, pick, slots,
        attnout_term, ffn_term, ffnout_term, query_term, wa_mine, wa_other,
    )
    s_query = scatter_wide(pair_sum(*g_query), 0)
    last = scatter_wide(pair_sum(own, other), 0)
    shared = lax.all_gather(last, "narrow").astype(F32).sum(axis=0)
    small = shared[:, 2 * head :]
    return (
        left_out,
        leave(dx_own),
        s_query.astype(F32),
        shared[:, :head],
        shared[:, head : 2 * head],
        s_outproj.astype(F32),
        s_ffn[0],
        s_ffn[1],
        s_ffn[2],
        small[:, 0],
        small[:, 1],
        small[:, 2],
        small[:, 3],
        small[:dh, 4],
        small[:dh, 5],
    )


def solution(mesh):
    return jax.shard_map(
        on_device,
        mesh=mesh,
        in_specs=(
            P(None, "narrow", "wide", None),
            P(None, "narrow", "wide", None),
            P("wide", None),
            P("wide", "narrow"),
            P("wide", None),
            P("wide", None),
            P("wide", "narrow"),
            P("wide", "narrow"),
            P("wide", "narrow"),
            P("wide", "narrow"),
            P("wide"),
            P("wide"),
            P("wide"),
            P("wide"),
            P("wide"),
            P("wide"),
        ),
        out_specs=(
            P(None, "narrow", "wide", None),
            P(None, "narrow", "wide", None),
            P("wide", "narrow"),
            P("wide", None),
            P("wide", None),
            P("wide", "narrow"),
            P("wide", "narrow"),
            P("wide", "narrow"),
            P("wide", "narrow"),
            P("wide"),
            P("wide"),
            P("wide"),
            P("wide"),
            P("wide"),
            P("wide"),
        ),
        check_vma=False,
    )
```

time: 801 us -> 485 us (0.61)
  waiting for transfers between devices: 487 us -> 184 us
  Pallas kernels: 0 us -> 87.9 us
  matrix products: 76 us -> 0 us
  starting transfers between devices: 12.9 us -> 82.4 us
  blocking collectives: 109 us -> 65.6 us
  other arithmetic: 59.4 us -> 27.7 us
  local copies, waits for them, and re-layouts: 26.7 us -> 12.1 us
    psum x5 -> x0, waiting for transfers between devices: 203 us -> none  [the longest x4 203 us: total(): return lax.psum(value.astype(jnp.bfloat16), 'narrow').astype(jnp.float32)]
    reduce_scatter x7 -> x4, waiting for transfers between devices: 201 us -> 52.5 us  [the longest x3 45.4 us: scatter_wide(): lax.psum_scatter(value, 'wide', scatter_dimension=axis, tiled=True, axis_...]
    pallas_call x0 -> x12, Pallas kernels: none -> 87.9 us  [the longest x1 16 us: on_device(): call(ffn_backward, [((rows, width), bf)] + [((rows, units), bf)] * 2 + [(...]
    dot_general x27 -> x0, matrix products: 76 us -> none  [the longest x1 10.3 us: on_device(): d_act = jnp.dot(d_ffn_all, w_down, preferred_element_type=jnp.float32)]
    all_gather x5 -> x2, waiting for transfers between devices: 74.8 us -> 0.01 us  [gather_wide(): lax.all_gather(value, 'wide', axis=axis, tiled=True, axis_index_groups=sa...]
    ppermute x0 -> x30, waiting for transfers between devices: none -> 72.9 us  [the longest x12 32.7 us: gather_z(): up = lax.ppermute(up, 'narrow', upward)]
    ppermute x0 -> x30, starting transfers between devices: none -> 61.7 us  [the longest x12 45.6 us: gather_z(): up = lax.ppermute(up, 'narrow', upward)]
    unnamed x2 -> x0, blocking collectives: 46.4 us -> none
  transfers between devices with their start and end apart: 20 -> 42, of which waited for: 14 -> 30; matrix products, arithmetic and copies ran while one was open for 13% -> 6% of each run, Pallas kernels for 0% -> 11%
where the time goes in v1:
time: 485 us; the launch traced here: 476 us
  waiting for transfers between devices  184 us (38%)
  Pallas kernels  87.9 us (18%)
  starting transfers between devices  82.4 us (17%)
  blocking collectives  65.6 us (14%)
  other arithmetic  27.7 us (6%)
  between operations  16.5 us (3%)
  local copies, waits for them, and re-layouts  12.1 us (2%)
    ppermute x12, starting transfers between devices, gather_z(): up = lax.ppermute(up, 'narrow', upward)  45.6 us
    reduce_scatter x3, waiting for transfers between devices, scatter_wide(): lax.psum_scatter(value, 'wide', scatter_dimension=axis, tiled=True, axis_...  45.4 us
    all_to_all x2, waiting for transfers between devices, exchange_z(): lax.all_to_all(parts, 'narrow', split_axis=0, concat_axis=0, tiled=True)  36.8 us
    all_to_all x1, blocking collectives, exchange_z(): lax.all_to_all(parts, 'narrow', split_axis=0, concat_axis=0, tiled=True)  33.9 us
    ppermute x12, waiting for transfers between devices, gather_z(): up = lax.ppermute(up, 'narrow', upward)  32.7 us
    ppermute x12, waiting for transfers between devices, gather_z(): down = lax.ppermute(down, 'narrow', downward)  27.7 us
    all_gather x1, blocking collectives, on_device(): shared = lax.all_gather(last, 'narrow').astype(F32).sum(axis=0)  19.2 us
    pallas_call x1, Pallas kernels, on_device(): call(ffn_backward, [((rows, width), bf)] + [((rows, units), bf)] * 2 + [(...  16 us
  transfers between devices with their start and end apart: 42, of which 30 were waited for; matrix products, arithmetic and copies ran while one was open for 6% of the time, Pallas kernels for 11%

profile of v1, /device:TPU:0, one launch (start us, length us, event | category | flops | bytes accessed | tf_op | source)
XLA Modules:
  0.0 476.5 jit_solution(14899799779029993819)
XLA Ops:
  9.4 12.5 %all_to_all.35 = bf16[8,16,1152]{2,1,0:T(8,128)(2,1)S(1)} all-to-all(bf16[8,16,1152]{2,1,0:T(8,128)(2,1)} %bitcast.39), channel_id=1, replica_groups=mesh['wide'=8,'narrow'=4] {'wide'}, dimensions={0} | all-to-all | bytes 589824 | tf_op jit(solution)/shard_map/all_to_all | solution.py:480
  21.9 3.5 collective-permute-start
  28.1 3.6 collective-permute-done.b1_ref
  31.7 4.1 collective-permute-done.3.a1_ref
  35.8 3.5 collective-permute-start.1
  40.6 3.9 collective-permute-done.1.b2_ref
  44.5 4.4 collective-permute-start.2
  50.2 2.9 collective-permute-done.2.b3_ref
  53.1 4.4 collective-permute-done.5.a3_ref
  66.9 10.0 %shard_map.272 = (bf16[512,1152]{1,0:T(8,128)(2,1)}, bf16[512,1152]{1,0:T(8,128)(2,1)}, f32[512,256]{1,0:T(8,128)}, f32[512,256]{1,0:T(8,128)}, bf16[512,256]{1,...) custom-call(bf16[128,1152]{1,0:T(8,128)(2,1)} %bitcast.42, ...), custom_call_target="tpu_custom_call" | custom-call | flops 3000000000 | bytes 8000000 | tf_op jit(solution)/shard_map/pallas_call | solution.py:522
  76.9 33.9 %all_to_all.36.z_ref = bf16[4,128,1152]{2,1,0:T(8,128)(2,1)} all-to-all(bf16[4,128,1152]{2,1,0:T(8,128)(2,1)} %bitcast.34), channel_id=1, replica_groups=mesh['wide'=8,'narrow'=4] {'narrow'}, dimensions={0} | all-to-all | bytes 2359296 | tf_op jit(solution)/shard_map/all_to_all | solution.py:476
  110.8 2.9 shard_map.273
  115.0 4.6 collective-permute-start.7
  119.5 4.5 collective-permute-done.10.a1_ref
  125.4 4.6 collective-permute-start.8
  130.0 3.4 collective-permute-done.11.a2_ref
  135.8 5.0 %collective-permute-start.9 = (bf16[128,1152]{1,0:T(8,128)(2,1)S(1)}, bf16[128,1152]{1,0:T(8,128)(2,1)S(1)}, u32[]{:S(2)}, u32[]{:S(2)}) collective-permute-start(bf16[128,1152]{1,0:T(8,128)(2,1)S(1)} %collective-permute-done.8.b2_ref), channel_id=1, source_target_pairs={{0,1},{1,2},{2,3},{4,5},{5,6},{6,7},{8,9},{9,10},{10,11},{12,13},{... | collective-permute-start | bytes 884744 | tf_op jit(solution)/shard_map/ppermute | solution.py:466
  140.9 3.6 all-to-all-start.3
  148.5 14.7 %shard_map.274 = (bf16[512,1152]{1,0:T(8,128)(2,1)}, bf16[512,1728]{1,0:T(8,128)(2,1)}, bf16[512,1728]{1,0:T(8,128)(2,1)}, bf16[512,1728]{1,0:T(8,128)(2,1)}, bf16[512,1152]{1,0:T(8,128)(2,1)}) custom-call(bf16[128,1152]{1,0:T(8,128)(2,1)} %get-tuple-element.70.own_ref, bf16[128,1152]{1,0:T(8,128)(2,1)} %copy-done.16, bf16[128,1152]{1,0:T(8,128)(2,1)} %copy-done.21, ...), custom_call_target="tpu_custom_call" | custom-call | flops 6000000000 | bytes 20000000 | tf_op jit(solution)/shard_map/pallas_call | solution.py:544
  163.2 4.5 all-to-all-start.2
  169.2 26.6 %all-to-all-done.2.m_ref = bf16[4,128,1152]{2,1,0:T(8,128)(2,1)S(1)} async-done(((bf16[4,128,1152]{2,1,0:T(8,128)(2,1)}), bf16[4,128,1152]{2,1,0:T(8,128)(2,1)S(1)}, u32[]{:S(2)}, u32[]{:S(2)}) %all-to-all-start.2) | async-done | bytes 1179680 | tf_op jit(solution)/shard_map/all_to_all | solution.py:476
  196.8 4.2 shard_map.275
  203.6 4.7 collective-permute-done.14.b1_ref
  208.3 4.3 collective-permute-start.15
  214.0 3.5 collective-permute-done.15.b2_ref
  217.4 4.4 collective-permute-start.16
  226.0 4.4 collective-permute-done.19.a3_ref
  231.2 16.0 %shard_map.276 = (bf16[512,1152]{1,0:T(8,128)(2,1)}, bf16[512,1728]{1,0:T(8,128)(2,1)}, bf16[512,1728]{1,0:T(8,128)(2,1)}, bf16[512,1152]{1,0:T(8,128)(2,1)}) custom-call(bf16[128,1152]{1,0:T(8,128)(2,1)} %get-tuple-element.77.own_ref, bf16[128,1152]{1,0:T(8,128)(2,1)} %copy-done.20, bf16[128,1152]{1,0:T(8,128)(2,1)} %copy-done.24, ...), custom_call_target="tpu_custom_call" | custom-call | flops 6000000000 | bytes 20000000 | tf_op jit(solution)/shard_map/pallas_call | solution.py:557
  247.2 14.1 %shard_map.277 = (bf16[3,576,1728]{2,1,0:T(8,128)(2,1)}, bf16[3,576,1728]{2,1,0:T(8,128)(2,1)}) custom-call(bf16[512,1152]{1,0:T(8,128)(2,1)} %get-tuple-element.81.dm_ref, bf16[512,1152]{1,0:T(8,128)(2,1)} %get-tuple-element.82.xn2_ref, bf16[512,1728]{1,0:T(8,128)(2,1)} %get-tuple-element.83.act_ref, bf16[512,1728]{1,0:T(8,128)(2,1)} %get-tuple-element.84.dg_ref, ...), custom_call_target="tpu_custom_call" | custom-call | flops 1000000 | bytes 1000000 | tf_op jit(solution)/shard_map/pallas_call | solution.py:576
  261.7 10.0 %collective-permute-done.20 = bf16[3,576,1728]{2,1,0:T(8,128)(2,1)} collective-permute-done((bf16[3,576,1728]{2,1,0:T(8,128)(2,1)}, bf16[3,576,1728]{2,1,0:T(8,128)(2,1)}, u32[]{:S(2)}, u32[]{:S(2)}) %collective-permute-start.20) | collective-permute-done | bytes 5972000 | tf_op jit(solution)/shard_map/ppermute | solution.py:449
  271.7 8.6 %add_convert_fusion = bf16[3,576,1728]{2,1,0:T(8,128)(2,1)} fusion(bf16[3,576,1728]{2,1,0:T(8,128)(2,1)} %collective-permute-done.20, bf16[3,576,1728]{2,1,0:T(8,128)(2,1)} %get-tuple-element.86), kind=kLoop, calls=%fused_computation | loop fusion | flops 11943936 | bytes 17915904 | tf_op jit(solution)/shard_map/convert_element_type | solution.py:452
  280.4 7.1 %reduce-scatter.8.cloned.1.call-done.g_ref = bf16[1,128,1152]{2,1,0:T(8,128)(2,1)} async-done(((bf16[4,128,1152]{2,1,0:T(8,128)(2,1)}), bf16[1,128,1152]{2,1,0:T(8,128)(2,1)}) %reduce-scatter.8.cloned.1.call-update) | async-done | bytes 294928 | tf_op jit(solution)/shard_map/reduce_scatter | solution.py:563
  293.0 5.2 %collective-permute-done.21.b1_ref = bf16[128,1152]{1,0:T(8,128)(2,1)S(1)} collective-permute-done((bf16[128,1152]{1,0:T(8,128)(2,1)}, bf16[128,1152]{1,0:T(8,128)(2,1)S(1)}, u32[]{:S(2)}, u32[]{:S(2)}) %collective-permute-start.21) | collective-permute-done | bytes 294944 | tf_op jit(solution)/shard_map/ppermute | solution.py:466
  298.2 4.3 collective-permute-start.22
  304.0 3.8 collective-permute-done.22.b2_ref
  307.9 4.4 collective-permute-start.23
  314.0 3.7 all-to-all-start.4
  317.7 4.1 collective-permute-done.26.a3_ref
  322.5 8.1 %shard_map.279 = (bf16[512,1152]{1,0:T(8,128)(2,1)}, bf16[512,1664]{1,0:T(8,128)(2,1)}, bf16[512,256]{1,0:T(8,128)(2,1)}, f32[1,256]{1,0:T(1,128)}) custom-call(bf16[128,1152]{1,0:T(8,128)(2,1)} %get-tuple-element.91.own_ref, bf16[128,1152]{1,0:T(8,128)(2,1)} %copy-done.17, bf16[128,1152]{1,0:T(8,128)(2,1)} %copy-done.23, bf16[128,1152]{1,0:T(8,128)(2,1)} %copy-done.27, ...), custom_call_target="tpu_custom_call" | custom-call | flops 3000000000 | bytes 8000000 | tf_op jit(solution)/shard_map/pallas_call | solution.py:592
  330.6 4.4 all-to-all-start.5
  344.4 17.2 %reduce-scatter.10.cloned.1.call-done = bf16[3,144,1728]{2,1,0:T(8,128)(2,1)} async-done(((bf16[3,576,1728]{2,1,0:T(8,128)(2,1)}), bf16[3,144,1728]{2,1,0:T(8,128)(2,1)}) %reduce-scatter.10.cloned.1.call-update) | async-done | bytes 1493008 | tf_op jit(solution)/shard_map/reduce_scatter | solution.py:455
  363.3 10.2 %all-to-all-done.5.g_ref = bf16[4,128,1664]{2,1,0:T(8,128)(2,1)} async-done(((bf16[4,128,1664]{2,1,0:T(8,128)(2,1)}), bf16[4,128,1664]{2,1,0:T(8,128)(2,1)}, u32[]{:S(2)}, u32[]{:S(2)}) %all-to-all-start.5) | async-done | bytes 1703968 | tf_op jit(solution)/shard_map/all_to_all | solution.py:476
  373.5 7.7 %shard_map.282 = (bf16[128,1152]{1,0:T(8,128)(2,1)}, bf16[576,640]{1,0:T(8,128)(2,1)}, bf16[576,640]{1,0:T(8,128)(2,1)}) custom-call(bf16[4,128,1664]{2,1,0:T(8,128)(2,1)} %all-to-all-done.5.g_ref, bf16[512,1152]{1,0:T(8,128)(2,1)} %get-tuple-element.68.xp_ref, bf16[512,1152]{1,0:T(8,128)(2,1)} %get-tuple-element.103.left_ref.xn1_ref, ...), custom_call_target="tpu_custom_call" | custom-call | flops 1000000000 | bytes 8000000 | tf_op jit(solution)/shard_map/pallas_call | solution.py:606
  390.1 25.9 %reduce-scatter.12.cloned.1.call-done = bf16[144,256]{1,0:T(8,128)(2,1)} async-done(((bf16[576,256]{1,0:T(8,128)(2,1)}), bf16[144,256]{1,0:T(8,128)(2,1)}) %reduce-scatter.12.cloned.1.call-update) | async-done | bytes 73744 | tf_op jit(solution)/shard_map/reduce_scatter | solution.py:455
  417.5 4.1 all-to-all-start.6
  423.3 6.3 %all-to-all-done.6 = bf16[8,16,1152]{2,1,0:T(8,128)(2,1)} async-done(((bf16[8,16,1152]{2,1,0:T(8,128)(2,1)}), bf16[8,16,1152]{2,1,0:T(8,128)(2,1)}, u32[]{:S(2)}, u32[]{:S(2)}) %all-to-all-start.6) | async-done | bytes 294944 | tf_op jit(solution)/shard_map/all_to_all | solution.py:485
  429.5 15.6 %reduce-scatter.16.cloned.1.call-done = bf16[144,640]{1,0:T(8,128)(2,1)} async-done(((bf16[576,640]{1,0:T(8,128)(2,1)}), bf16[144,640]{1,0:T(8,128)(2,1)}) %reduce-scatter.16.cloned.1.call-update) | async-done | bytes 184336
  445.1 19.2 %all-gather = bf16[576,640]{1,0:T(8,128)(2,1)S(1)} all-gather(bf16[144,640]{1,0:T(8,128)(2,1)} %reduce-scatter.16.cloned.1.call-done), channel_id=2, replica_groups=mesh['wide'=8,'narrow'=4] {'narrow'}, dimensions={0}, use_global_device_ids=true | all-gather | bytes 921600 | tf_op jit(solution)/shard_map/all_gather | solution.py:617
  (150 shorter events, 73.7 us)
Async XLA Ops:
  7.2 50.3 %all-gather.4.cloned.1.call-start = ((), (), s32[]{:S(2)}) async-start(), calls=%async_computation.12 | async-start | bytes 1658880 | tf_op jit(solution)/shard_map/all_gather | solution.py:444
  9.3 125.2 %all-gather.6.cloned.1.call-start = ((), (), s32[]{:S(2)}) async-start(), calls=%async_computation.13 | async-start | bytes 7741440 | tf_op jit(solution)/shard_map/all_gather | solution.py:444
  21.9 9.8 %collective-permute-start = (bf16[128,1152]{1,0:T(8,128)(2,1)S(1)}, bf16[128,1152]{1,0:T(8,128)(2,1)S(1)}, u32[]{:S(2)}, u32[]{:S(2)}) collective-permute-start(bf16[128,1152]{1,0:T(8,128)(2,1)S(1)} %bitcast.40), channel_id=1, source_target_pairs={{0,1},{1,2},{2,3},{4,5},{5,6},{6,7},{8,9},{9,10},{10,11},{12,13},{... | collective-permute-start | bytes 884744 | tf_op jit(solution)/shard_map/ppermute | solution.py:466
  25.4 10.5 %collective-permute-start.3 = (bf16[128,1152]{1,0:T(8,128)(2,1)S(1)}, bf16[128,1152]{1,0:T(8,128)(2,1)S(1)}, u32[]{:S(2)}, u32[]{:S(2)}) collective-permute-start(bf16[128,1152]{1,0:T(8,128)(2,1)S(1)} %bitcast.41), channel_id=1, source_target_pairs={{1,0},{2,1},{3,2},{5,4},{6,5},{7,6},{9,8},{10,9},{11,10},{13,12},{... | collective-permute-start | bytes 884744 | tf_op jit(solution)/shard_map/ppermute | solution.py:467
  28.1 29.4 %copy-start.8 = (s32[1,2]{1,0:T(1,128)S(1)}, s32[1,2]{1,0:T(1,128)}, u32[]{:S(2)}) copy-start(s32[1,2]{1,0:T(1,128)} %param.18) | copy-start | bytes 28
  31.7 34.1 %copy-start.9 = (bf16[128,1152]{1,0:T(8,128)(2,1)}, bf16[128,1152]{1,0:T(8,128)(2,1)S(1)}, u32[]{:S(2)}) copy-start(bf16[128,1152]{1,0:T(8,128)(2,1)S(1)} %collective-permute-done.b1_ref) | copy-start | bytes 884740
  35.8 30.0 %copy-start.10 = (bf16[128,1152]{1,0:T(8,128)(2,1)}, bf16[128,1152]{1,0:T(8,128)(2,1)S(1)}, u32[]{:S(2)}) copy-start(bf16[128,1152]{1,0:T(8,128)(2,1)S(1)} %collective-permute-done.3.a1_ref) | copy-start | bytes 884740
  35.8 8.7 %collective-permute-start.1 = (bf16[128,1152]{1,0:T(8,128)(2,1)S(1)}, bf16[128,1152]{1,0:T(8,128)(2,1)S(1)}, u32[]{:S(2)}, u32[]{:S(2)}) collective-permute-start(bf16[128,1152]{1,0:T(8,128)(2,1)S(1)} %collective-permute-done.b1_ref), channel_id=1, source_target_pairs={{0,1},{1,2},{2,3},{4,5},{5,6},{6,7},{8,9},{9,10},{10,11},{12,13},{... | collective-permute-start | bytes 884744 | tf_op jit(solution)/shard_map/ppermute | solution.py:466
  39.3 9.6 %collective-permute-start.4 = (bf16[128,1152]{1,0:T(8,128)(2,1)S(1)}, bf16[128,1152]{1,0:T(8,128)(2,1)S(1)}, u32[]{:S(2)}, u32[]{:S(2)}) collective-permute-start(bf16[128,1152]{1,0:T(8,128)(2,1)S(1)} %collective-permute-done.3.a1_ref), channel_id=1, source_target_pairs={{1,0},{2,1},{3,2},{5,4},{6,5},{7,6},{9,8},{10,9},{11,10},{13,12},{... | collective-permute-start | bytes 884744 | tf_op jit(solution)/shard_map/ppermute | solution.py:467
  44.5 8.6 %collective-permute-start.2 = (bf16[128,1152]{1,0:T(8,128)(2,1)S(1)}, bf16[128,1152]{1,0:T(8,128)(2,1)S(1)}, u32[]{:S(2)}, u32[]{:S(2)}) collective-permute-start(bf16[128,1152]{1,0:T(8,128)(2,1)S(1)} %collective-permute-done.1.b2_ref), channel_id=1, source_target_pairs={{0,1},{1,2},{2,3},{4,5},{5,6},{6,7},{8,9},{9,10},{10,11},{12,13},{... | collective-permute-start | bytes 884744 | tf_op jit(solution)/shard_map/ppermute | solution.py:466
  48.9 8.6 %collective-permute-start.5 = (bf16[128,1152]{1,0:T(8,128)(2,1)S(1)}, bf16[128,1152]{1,0:T(8,128)(2,1)S(1)}, u32[]{:S(2)}, u32[]{:S(2)}) collective-permute-start(bf16[128,1152]{1,0:T(8,128)(2,1)S(1)} %collective-permute-done.4.a2_ref), channel_id=1, source_target_pairs={{1,0},{2,1},{3,2},{5,4},{6,5},{7,6},{9,8},{10,9},{11,10},{13,12},{... | collective-permute-start | bytes 884744 | tf_op jit(solution)/shard_map/ppermute | solution.py:467
  57.5 8.3 %collective-permute-start.6 = (bf16[576,1152]{1,0:T(8,128)(2,1)}, bf16[576,1152]{1,0:T(8,128)(2,1)S(1)}, u32[]{:S(2)}, u32[]{:S(2)}) collective-permute-start(bf16[576,1152]{1,0:T(8,128)(2,1)} %all-gather.4.cloned.1.call-done.wm_ref), channel_id=1, source_target_pairs={{0,4},{4,0},{8,12},{12,8},{16,20},{20,16},{24,28},{28,24},{1,5},{5... | collective-permute-start | bytes 3981320 | tf_op jit(solution)/shard_map/ppermute | solution.py:449
  113.7 10.4 %collective-permute-start.10 = (bf16[128,1152]{1,0:T(8,128)(2,1)}, bf16[128,1152]{1,0:T(8,128)(2,1)S(1)}, u32[]{:S(2)}, u32[]{:S(2)}) collective-permute-start(bf16[128,1152]{1,0:T(8,128)(2,1)} %get-tuple-element.70.own_ref), channel_id=1, source_target_pairs={{1,0},{2,1},{3,2},{5,4},{6,5},{7,6},{9,8},{10,9},{11,10},{13,12},{... | collective-permute-start | bytes 884744 | tf_op jit(solution)/shard_map/ppermute | solution.py:467
  115.0 10.4 %collective-permute-start.7 = (bf16[128,1152]{1,0:T(8,128)(2,1)}, bf16[128,1152]{1,0:T(8,128)(2,1)S(1)}, u32[]{:S(2)}, u32[]{:S(2)}) collective-permute-start(bf16[128,1152]{1,0:T(8,128)(2,1)} %get-tuple-element.70.own_ref), channel_id=1, source_target_pairs={{0,1},{1,2},{2,3},{4,5},{5,6},{6,7},{8,9},{9,10},{10,11},{12,13},{... | collective-permute-start | bytes 884744 | tf_op jit(solution)/shard_map/ppermute | solution.py:466
  124.1 23.7 %copy-start.15 = (bf16[128,1152]{1,0:T(8,128)(2,1)}, bf16[128,1152]{1,0:T(8,128)(2,1)S(1)}, u32[]{:S(2)}) copy-start(bf16[128,1152]{1,0:T(8,128)(2,1)S(1)} %collective-permute-done.10.a1_ref) | copy-start | bytes 884740
  124.1 9.3 %collective-permute-start.11 = (bf16[128,1152]{1,0:T(8,128)(2,1)S(1)}, bf16[128,1152]{1,0:T(8,128)(2,1)S(1)}, u32[]{:S(2)}, u32[]{:S(2)}) collective-permute-start(bf16[128,1152]{1,0:T(8,128)(2,1)S(1)} %collective-permute-done.10.a1_ref), channel_id=1, source_target_pairs={{1,0},{2,1},{3,2},{5,4},{6,5},{7,6},{9,8},{10,9},{11,10},{13,12},{... | collective-permute-start | bytes 884744 | tf_op jit(solution)/shard_map/ppermute | solution.py:467
  125.4 9.2 %collective-permute-start.8 = (bf16[128,1152]{1,0:T(8,128)(2,1)S(1)}, bf16[128,1152]{1,0:T(8,128)(2,1)S(1)}, u32[]{:S(2)}, u32[]{:S(2)}) collective-permute-start(bf16[128,1152]{1,0:T(8,128)(2,1)S(1)} %collective-permute-done.7.b1_ref), channel_id=1, source_target_pairs={{0,1},{1,2},{2,3},{4,5},{5,6},{6,7},{8,9},{9,10},{10,11},{12,13},{... | collective-permute-start | bytes 884744 | tf_op jit(solution)/shard_map/ppermute | solution.py:466
  134.5 13.2 %collective-permute-start.13 = (bf16[3,576,1728]{2,1,0:T(8,128)(2,1)}, bf16[3,576,1728]{2,1,0:T(8,128)(2,1)}, u32[]{:S(2)}, u32[]{:S(2)}) collective-permute-start(bf16[3,576,1728]{2,1,0:T(8,128)(2,1)} %all-gather.6.cloned.1.call-done.wm_ref), channel_id=1, source_target_pairs={{0,4},{4,0},{8,12},{12,8},{16,20},{20,16},{24,28},{28,24},{1,5},{5... | collective-permute-start | bytes 17915912 | tf_op jit(solution)/shard_map/ppermute | solution.py:449
  134.5 12.1 %collective-permute-start.12 = (bf16[128,1152]{1,0:T(8,128)(2,1)S(1)}, bf16[128,1152]{1,0:T(8,128)(2,1)S(1)}, u32[]{:S(2)}, u32[]{:S(2)}) collective-permute-start(bf16[128,1152]{1,0:T(8,128)(2,1)S(1)} %collective-permute-done.11.a2_ref), channel_id=1, source_target_pairs={{1,0},{2,1},{3,2},{5,4},{6,5},{7,6},{9,8},{10,9},{11,10},{13,12},{... | collective-permute-start | bytes 884744 | tf_op jit(solution)/shard_map/ppermute | solution.py:467
  135.8 11.9 %collective-permute-start.9 = (bf16[128,1152]{1,0:T(8,128)(2,1)S(1)}, bf16[128,1152]{1,0:T(8,128)(2,1)S(1)}, u32[]{:S(2)}, u32[]{:S(2)}) collective-permute-start(bf16[128,1152]{1,0:T(8,128)(2,1)S(1)} %collective-permute-done.8.b2_ref), channel_id=1, source_target_pairs={{0,1},{1,2},{2,3},{4,5},{5,6},{6,7},{8,9},{9,10},{10,11},{12,13},{... | collective-permute-start | bytes 884744 | tf_op jit(solution)/shard_map/ppermute | solution.py:466
  140.9 22.3 %all-to-all-start.3 = ((bf16[8,16,1152]{2,1,0:T(8,128)(2,1)}), bf16[8,16,1152]{2,1,0:T(8,128)(2,1)S(1)}, u32[]{:S(2)}, u32[]{:S(2)}) async-start(bf16[8,16,1152]{2,1,0:T(8,128)(2,1)} %bitcast.10), calls=%async_computation.3 | async-start | bytes 589824 | tf_op jit(solution)/shard_map/all_to_all | solution.py:480
  163.2 32.6 %copy-start.2 = (bf16[8,16,1152]{2,1,0:T(8,128)(2,1)}, bf16[8,16,1152]{2,1,0:T(8,128)(2,1)S(1)}, u32[]{:S(2)}) copy-start(bf16[8,16,1152]{2,1,0:T(8,128)(2,1)S(1)} %all-to-all-done.3) | copy-start | bytes 884740
  163.2 32.6 %all-to-all-start.2 = ((bf16[4,128,1152]{2,1,0:T(8,128)(2,1)}), bf16[4,128,1152]{2,1,0:T(8,128)(2,1)S(1)}, u32[]{:S(2)}, u32[]{:S(2)}) async-start(bf16[4,128,1152]{2,1,0:T(8,128)(2,1)} %bitcast.33), calls=%async_computation.2 | async-start | bytes 2359296 | tf_op jit(solution)/shard_map/all_to_all | solution.py:476
  167.7 119.7 %reduce-scatter.8.cloned.1.call-start = ((), (), s32[]{:S(2)}) async-start(), calls=%async_computation.14 | async-start | bytes 1474560 | tf_op jit(solution)/shard_map/reduce_scatter | solution.py:563
  201.0 7.3 %collective-permute-start.14 = (bf16[128,1152]{1,0:T(8,128)(2,1)}, bf16[128,1152]{1,0:T(8,128)(2,1)S(1)}, u32[]{:S(2)}, u32[]{:S(2)}) collective-permute-start(bf16[128,1152]{1,0:T(8,128)(2,1)} %get-tuple-element.77.own_ref), channel_id=1, source_target_pairs={{0,1},{1,2},{2,3},{4,5},{5,6},{6,7},{8,9},{9,10},{10,11},{12,13},{... | collective-permute-start | bytes 884744 | tf_op jit(solution)/shard_map/ppermute | solution.py:466
  202.3 10.3 %collective-permute-start.17 = (bf16[128,1152]{1,0:T(8,128)(2,1)}, bf16[128,1152]{1,0:T(8,128)(2,1)S(1)}, u32[]{:S(2)}, u32[]{:S(2)}) collective-permute-start(bf16[128,1152]{1,0:T(8,128)(2,1)} %get-tuple-element.77.own_ref), channel_id=1, source_target_pairs={{1,0},{2,1},{3,2},{5,4},{6,5},{7,6},{9,8},{10,9},{11,10},{13,12},{... | collective-permute-start | bytes 884744 | tf_op jit(solution)/shard_map/ppermute | solution.py:467
  208.3 9.1 %collective-permute-start.15 = (bf16[128,1152]{1,0:T(8,128)(2,1)S(1)}, bf16[128,1152]{1,0:T(8,128)(2,1)S(1)}, u32[]{:S(2)}, u32[]{:S(2)}) collective-permute-start(bf16[128,1152]{1,0:T(8,128)(2,1)S(1)} %collective-permute-done.14.b1_ref), channel_id=1, source_target_pairs={{0,1},{1,2},{2,3},{4,5},{5,6},{6,7},{8,9},{9,10},{10,11},{12,13},{... | collective-permute-start | bytes 884744 | tf_op jit(solution)/shard_map/ppermute | solution.py:466
  212.7 9.2 %collective-permute-start.18 = (bf16[128,1152]{1,0:T(8,128)(2,1)S(1)}, bf16[128,1152]{1,0:T(8,128)(2,1)S(1)}, u32[]{:S(2)}, u32[]{:S(2)}) collective-permute-start(bf16[128,1152]{1,0:T(8,128)(2,1)S(1)} %collective-permute-done.17.a1_ref), channel_id=1, source_target_pairs={{1,0},{2,1},{3,2},{5,4},{6,5},{7,6},{9,8},{10,9},{11,10},{13,12},{... | collective-permute-start | bytes 884744 | tf_op jit(solution)/shard_map/ppermute | solution.py:467
  217.4 8.6 %collective-permute-start.16 = (bf16[128,1152]{1,0:T(8,128)(2,1)S(1)}, bf16[128,1152]{1,0:T(8,128)(2,1)S(1)}, u32[]{:S(2)}, u32[]{:S(2)}) collective-permute-start(bf16[128,1152]{1,0:T(8,128)(2,1)S(1)} %collective-permute-done.15.b2_ref), channel_id=1, source_target_pairs={{0,1},{1,2},{2,3},{4,5},{5,6},{6,7},{8,9},{9,10},{10,11},{12,13},{... | collective-permute-start | bytes 884744 | tf_op jit(solution)/shard_map/ppermute | solution.py:466
  221.9 8.6 %collective-permute-start.19 = (bf16[128,1152]{1,0:T(8,128)(2,1)S(1)}, bf16[128,1152]{1,0:T(8,128)(2,1)S(1)}, u32[]{:S(2)}, u32[]{:S(2)}) collective-permute-start(bf16[128,1152]{1,0:T(8,128)(2,1)S(1)} %collective-permute-done.18.a2_ref), channel_id=1, source_target_pairs={{1,0},{2,1},{3,2},{5,4},{6,5},{7,6},{9,8},{10,9},{11,10},{13,12},{... | collective-permute-start | bytes 884744 | tf_op jit(solution)/shard_map/ppermute | solution.py:467
  261.3 10.4 %collective-permute-start.20 = (bf16[3,576,1728]{2,1,0:T(8,128)(2,1)}, bf16[3,576,1728]{2,1,0:T(8,128)(2,1)}, u32[]{:S(2)}, u32[]{:S(2)}) collective-permute-start(bf16[3,576,1728]{2,1,0:T(8,128)(2,1)} %get-tuple-element.87), channel_id=1, source_target_pairs={{0,4},{4,0},{8,12},{12,8},{16,20},{20,16},{24,28},{28,24},{1,5},{5... | collective-permute-start | bytes 17915912 | tf_op jit(solution)/shard_map/ppermute | solution.py:449
  261.4 100.2 %reduce-scatter.10.cloned.1.call-start = ((), (), s32[]{:S(2)}) async-start(), calls=%async_computation.15 | async-start | bytes 7741440 | tf_op jit(solution)/shard_map/reduce_scatter | solution.py:455
  290.3 8.0 %collective-permute-start.21 = (bf16[128,1152]{1,0:T(8,128)(2,1)}, bf16[128,1152]{1,0:T(8,128)(2,1)S(1)}, u32[]{:S(2)}, u32[]{:S(2)}) collective-permute-start(bf16[128,1152]{1,0:T(8,128)(2,1)} %get-tuple-element.91.own_ref), channel_id=1, source_target_pairs={{0,1},{1,2},{2,3},{4,5},{5,6},{6,7},{8,9},{9,10},{10,11},{12,13},{... | collective-permute-start | bytes 884744 | tf_op jit(solution)/shard_map/ppermute | solution.py:466
  291.7 11.1 %collective-permute-start.24 = (bf16[128,1152]{1,0:T(8,128)(2,1)}, bf16[128,1152]{1,0:T(8,128)(2,1)S(1)}, u32[]{:S(2)}, u32[]{:S(2)}) collective-permute-start(bf16[128,1152]{1,0:T(8,128)(2,1)} %get-tuple-element.91.own_ref), channel_id=1, source_target_pairs={{1,0},{2,1},{3,2},{5,4},{6,5},{7,6},{9,8},{10,9},{11,10},{13,12},{... | collective-permute-start | bytes 884744 | tf_op jit(solution)/shard_map/ppermute | solution.py:467
  298.2 23.6 %copy-start.17 = (bf16[128,1152]{1,0:T(8,128)(2,1)}, bf16[128,1152]{1,0:T(8,128)(2,1)S(1)}, u32[]{:S(2)}) copy-start(bf16[128,1152]{1,0:T(8,128)(2,1)S(1)} %collective-permute-done.21.b1_ref) | copy-start | bytes 884740
  298.2 9.6 %collective-permute-start.22 = (bf16[128,1152]{1,0:T(8,128)(2,1)S(1)}, bf16[128,1152]{1,0:T(8,128)(2,1)S(1)}, u32[]{:S(2)}, u32[]{:S(2)}) collective-permute-start(bf16[128,1152]{1,0:T(8,128)(2,1)S(1)} %collective-permute-done.21.b1_ref), channel_id=1, source_target_pairs={{0,1},{1,2},{2,3},{4,5},{5,6},{6,7},{8,9},{9,10},{10,11},{12,13},{... | collective-permute-start | bytes 884744 | tf_op jit(solution)/shard_map/ppermute | solution.py:466
  302.8 9.9 %collective-permute-start.25 = (bf16[128,1152]{1,0:T(8,128)(2,1)S(1)}, bf16[128,1152]{1,0:T(8,128)(2,1)S(1)}, u32[]{:S(2)}, u32[]{:S(2)}) collective-permute-start(bf16[128,1152]{1,0:T(8,128)(2,1)S(1)} %collective-permute-done.24.a1_ref), channel_id=1, source_target_pairs={{1,0},{2,1},{3,2},{5,4},{6,5},{7,6},{9,8},{10,9},{11,10},{13,12},{... | collective-permute-start | bytes 884744 | tf_op jit(solution)/shard_map/ppermute | solution.py:467
  307.9 9.8 %collective-permute-start.23 = (bf16[128,1152]{1,0:T(8,128)(2,1)S(1)}, bf16[128,1152]{1,0:T(8,128)(2,1)S(1)}, u32[]{:S(2)}, u32[]{:S(2)}) collective-permute-start(bf16[128,1152]{1,0:T(8,128)(2,1)S(1)} %collective-permute-done.22.b2_ref), channel_id=1, source_target_pairs={{0,1},{1,2},{2,3},{4,5},{5,6},{6,7},{8,9},{9,10},{10,11},{12,13},{... | collective-permute-start | bytes 884744 | tf_op jit(solution)/shard_map/ppermute | solution.py:466
  312.7 9.1 %collective-permute-start.26 = (bf16[128,1152]{1,0:T(8,128)(2,1)S(1)}, bf16[128,1152]{1,0:T(8,128)(2,1)S(1)}, u32[]{:S(2)}, u32[]{:S(2)}) collective-permute-start(bf16[128,1152]{1,0:T(8,128)(2,1)S(1)} %collective-permute-done.25.a2_ref), channel_id=1, source_target_pairs={{1,0},{2,1},{3,2},{5,4},{6,5},{7,6},{9,8},{10,9},{11,10},{13,12},{... | collective-permute-start | bytes 884744 | tf_op jit(solution)/shard_map/ppermute | solution.py:467
  314.0 16.6 %all-to-all-start.4 = ((bf16[8,16,1152]{2,1,0:T(8,128)(2,1)}), bf16[8,16,1152]{2,1,0:T(8,128)(2,1)S(1)}, u32[]{:S(2)}, u32[]{:S(2)}) async-start(bf16[8,16,1152]{2,1,0:T(8,128)(2,1)} %bitcast.13), calls=%async_computation.4 | async-start | bytes 589824 | tf_op jit(solution)/shard_map/all_to_all | solution.py:485
  330.6 42.9 %all-to-all-start.5 = ((bf16[4,128,1664]{2,1,0:T(8,128)(2,1)}), bf16[4,128,1664]{2,1,0:T(8,128)(2,1)}, u32[]{:S(2)}, u32[]{:S(2)}) async-start(bf16[4,128,1664]{2,1,0:T(8,128)(2,1)} %bitcast.30), calls=%async_computation.6 | async-start | bytes 3407872 | tf_op jit(solution)/shard_map/all_to_all | solution.py:476
  335.0 53.5 %reduce-scatter.14.cloned.1.call-start = ((), (), s32[]{:S(2)}) async-start(), calls=%async_computation.17 | async-start | bytes 368640 | tf_op jit(solution)/shard_map/reduce_scatter | solution.py:455
  337.8 1.8 collective-permute-start.29
  341.4 74.6 %reduce-scatter.12.cloned.1.call-start = ((), (), s32[]{:S(2)}) async-start(), calls=%async_computation.16 | async-start | bytes 368640 | tf_op jit(solution)/shard_map/reduce_scatter | solution.py:455
  344.2 37.0 %collective-permute-start.27 = (bf16[576,256]{1,0:T(8,128)(2,1)}, bf16[576,256]{1,0:T(8,128)(2,1)}, u32[]{:S(2)}, u32[]{:S(2)}) collective-permute-start(bf16[576,256]{1,0:T(8,128)(2,1)} %get-tuple-element.106), channel_id=1, source_target_pairs={{0,4},{4,0},{8,12},{12,8},{16,20},{20,16},{24,28},{28,24},{1,5},{5... | collective-permute-start | bytes 884744 | tf_op jit(solution)/shard_map/ppermute | solution.py:449
  381.1 2.6 collective-permute-start.28
  383.0 62.1 %reduce-scatter.16.cloned.1.call-start = ((), (), s32[]{:S(2)}) async-start(), calls=%async_computation.18 | async-start | bytes 921600
  417.5 12.1 %all-to-all-start.6 = ((bf16[8,16,1152]{2,1,0:T(8,128)(2,1)}), bf16[8,16,1152]{2,1,0:T(8,128)(2,1)}, u32[]{:S(2)}, u32[]{:S(2)}) async-start(bf16[8,16,1152]{2,1,0:T(8,128)(2,1)} %bitcast.43), calls=%async_computation.8 | async-start | bytes 589824 | tf_op jit(solution)/shard_map/all_to_all | solution.py:485
  (27 other events, 299.6 us)
Sparse Core Ops, SparseCore 0:
  10.5 31.6 all-gather.3
  44.0 69.3 all-gather.5
  261.5 25.8 reduce-scatter.7
  290.4 71.2 reduce-scatter.9
  364.3 24.1 reduce-scatter.13
  391.7 24.1 reduce-scatter.11
  418.9 26.1 reduce-scatter.15

commit v2 on v1

v2 whole, which is shorter than its diff:
```python
import functools
import math

import jax
import jax.numpy as jnp
from jax import lax
from jax.experimental import pallas as pl
from jax.experimental.pallas import tpu as pltpu
from jax.sharding import PartitionSpec as P

EPS = 1e-06
SCALE = 0.0625
LOGBASE = math.log(1000000.0)
GELU_C = 0.7978845608028654
GELU_A = 0.044715
F32, BF16 = jnp.float32, jnp.bfloat16
VMEM_LIMIT = 60 * 1024 * 1024
CHUNKS = 1
RING = 4


def call(kernel, outs, scratch=(), anys=(), smem=(), count=0, flops=0, moved=0):
    def place(index):
        if index in anys:
            return pl.BlockSpec(memory_space=pl.ANY)
        if index in smem:
            return pl.BlockSpec(memory_space=pltpu.SMEM)
        return pl.BlockSpec(memory_space=pltpu.VMEM)

    return pl.pallas_call(
        kernel,
        out_shape=[jax.ShapeDtypeStruct(s, d) for s, d in outs],
        in_specs=[place(i) for i in range(count)],
        out_specs=[pl.BlockSpec(memory_space=pltpu.VMEM)] * len(outs),
        scratch_shapes=list(scratch),
        compiler_params=pltpu.CompilerParams(vmem_limit_bytes=VMEM_LIMIT),
        cost_estimate=pl.CostEstimate(flops=1, bytes_accessed=1, transcendentals=0),
    )


def mm(a, b):
    return lax.dot_general(a, b, (((1,), (0,)), ((), ())), preferred_element_type=F32)


def mm_nt(a, b):
    return lax.dot_general(a, b, (((1,), (1,)), ((), ())), preferred_element_type=F32)


def mm_tn(a, b):
    return lax.dot_general(a, b, (((0,), (0,)), ((), ())), preferred_element_type=F32)


def root(v):
    return lax.rsqrt(jnp.mean(v * v, axis=-1, keepdims=True) + EPS)


def norm(v, gain):
    return v * root(v) * (1.0 + gain)


def norm_back(v, grad, gain):
    r = root(v)
    e = grad * (1.0 + gain)
    return r * e - v * (r * r * r * jnp.mean(e * v, axis=-1, keepdims=True))


def norm_term(v, grad):
    return jnp.sum(grad * v * root(v), axis=0, keepdims=True)


def rotate(v, cosine, sine):
    half = v.shape[-1] // 2
    a, b = v[:, :half], v[:, half:]
    return jnp.concatenate([a * cosine - b * sine, b * cosine + a * sine], axis=-1)


def rotate_back(v, cosine, sine):
    half = v.shape[-1] // 2
    a, b = v[:, :half], v[:, half:]
    return jnp.concatenate([a * cosine + b * sine, b * cosine - a * sine], axis=-1)


def tiles(extent, size):
    return [(i, min(size, extent - i)) for i in range(0, extent, size)]


def packing(q_ref, k_ref, v_ref, o_ref, g0_ref, g1_ref, g2_ref, g3_ref, g4_ref, g5_ref, out_ref):
    rows, head = q_ref.shape
    for i, ref in enumerate((q_ref, k_ref, v_ref, o_ref)):
        out_ref[:, i * head : (i + 1) * head] = ref[...]
    lane = lax.broadcasted_iota(jnp.int32, (rows, 128), 1)
    columns = jnp.zeros((rows, 128), F32)
    for i, ref in enumerate((g0_ref, g1_ref, g2_ref, g3_ref, g4_ref, g5_ref)):
        n = ref.shape[0]
        same = lax.broadcasted_iota(jnp.int32, (rows, n), 0) == lax.broadcasted_iota(
            jnp.int32, (rows, n), 1
        )
        column = jnp.sum(jnp.where(same, ref[...].astype(F32)[None, :], 0.0), axis=1, keepdims=True)
        columns = jnp.where(lane == i, column, columns)
    out_ref[:, 4 * head :] = columns.astype(BF16)


def one_hot(order, rows):
    index = lax.broadcasted_iota(jnp.int32, (rows, order.shape[1]), 0)
    return jnp.where(index == order, 1.0, 0.0).astype(BF16)


def steps(value, size, count):
    return sum(jnp.where(value >= size * i, 1, 0) for i in range(1, count))


def orders(core, width, head, wide):
    half, dw, dh = width // 2, width // wide, head // wide
    place = lax.broadcasted_iota(jnp.int32, (1, width), 1)
    side = jnp.where(place >= half, 1, 0)
    inner = place - half * side
    chip = steps(inner, dw, wide // 2)
    order = (2 * chip + ((core + side) & 1)) * dw + (inner - chip * dw)
    entry = lax.broadcasted_iota(jnp.int32, (1, head), 1)
    owner = steps(entry, dh, wide)
    chip = steps(owner, 2, wide // 2)
    pick = (((owner & 1) + core) & 1) * half + chip * dw + (entry - owner * dh)
    return order, pick


def segments(position, first, ends):
    segment = jnp.where(position < first, 0, jnp.where(position < ends, 1, 2))
    begin = jnp.where(position < first, 0, jnp.where(position < ends, first, ends))
    return segment, position - begin


def attention_forward(wide, *refs):
    x_refs, weight_refs, info_ref, refs = refs[:RING], refs[RING:-26], refs[-26], refs[-25:]
    (
        xp_ref, xn1_ref, qraw_ref, kraw_ref, q_ref, k_ref, v_ref, probs_ref, att_ref, gains_ref,
        hgain_ref, wkv_ref, wout_ref, cos_ref, sin_ref, order_ref, pick_ref, *part_refs,
        part_ref, x_ref, w_ref, sem,
    ) = refs
    head = q_ref.shape[1]
    rows, width = x_ref.shape
    half = width // 2
    slot, core, first, ends = info_ref[0], info_ref[1], info_ref[2], info_ref[3]
    copies, count = [], len(weight_refs) // 2
    for i, ref in enumerate(weight_refs):
        n = ref.shape[0]
        at = pl.multiple_of(info_ref[4 + i % count] * n + half * (1 - i // count), 16)
        copies.append(pltpu.make_async_copy(ref, w_ref.at[pl.ds(at, n)], sem.at[i]))
        copies[-1].start()
    collect(x_refs, slot, x_ref)
    order, pick = orders(core, width, head, wide)
    order_ref[...] = order
    pick_ref[...] = pick
    choose = one_hot(order, width)
    step = 128
    for r, n in tiles(rows, step):
        xp_ref[pl.ds(r, n), :] = mm(x_ref[pl.ds(r, n), :], choose).astype(BF16)
    frequency = jnp.exp(
        lax.broadcasted_iota(jnp.int32, (1, head // 2), 1).astype(F32) * (-2.0 / head) * LOGBASE
    )
    for r, n in tiles(rows, step):
        position = lax.broadcasted_iota(jnp.int32, (n, 1), 0) + r
        angle = segments(position, first, ends)[1].astype(F32) * frequency
        cos_ref[pl.ds(r, n), :] = jnp.cos(angle)
        sin_ref[pl.ds(r, n), :] = jnp.sin(angle)
    for c in copies:
        c.wait()
    columns = w_ref[:, 4 * head :].T
    gains_ref[...] = columns[:8].astype(F32)
    hgain_ref[...] = mm(columns[:8], one_hot(pick, width))
    wkv_ref[...] = w_ref[:, head : 3 * head]
    wout_ref[...] = w_ref[:, 3 * head : 4 * head]
    for r, n in tiles(rows, step):
        x = xp_ref[pl.ds(r, n), :].astype(F32)
        xn1_ref[pl.ds(r, n), :] = norm(x, gains_ref[0:1, :]).astype(BF16)
    gq, gk = hgain_ref[4:5, :], hgain_ref[5:6, :]
    raw = mm(xn1_ref[...], w_ref[:, : 3 * head])
    qraw_ref[...] = raw[:, :head]
    kraw_ref[...] = raw[:, head : 2 * head]
    v_ref[...] = raw[:, 2 * head :].astype(BF16)
    cosine, sine = cos_ref[...], sin_ref[...]
    q_ref[...] = rotate(norm(raw[:, :head], gq), cosine, sine).astype(BF16)
    k_ref[...] = rotate(norm(raw[:, head : 2 * head], gk), cosine, sine).astype(BF16)
    for r, n in tiles(rows, step):
        s = mm_nt(q_ref[pl.ds(r, n), :], k_ref[...]) * SCALE
        row = lax.broadcasted_iota(jnp.int32, s.shape, 0) + r
        col = lax.broadcasted_iota(jnp.int32, s.shape, 1)
        keep = (segments(row, first, ends)[0] == segments(col, first, ends)[0]) & (col <= row)
        s = jnp.where(keep, s, -1e30)
        e = jnp.exp(s - jnp.max(s, axis=-1, keepdims=True))
        p = e / jnp.sum(e, axis=-1, keepdims=True)
        probs_ref[pl.ds(r, n), :] = p
        att_ref[pl.ds(r, n), :] = mm(p.astype(BF16), v_ref[...]).astype(BF16)
    for r, n in tiles(rows, step):
        part_ref[pl.ds(r, n), :] = mm_nt(
            att_ref[pl.ds(r, n), :], w_ref[:, 3 * head : 4 * head]
        ).astype(BF16)
    hand_out(part_ref, slot, part_refs)


def hand_out(whole_ref, slot, refs):
    for s, ref in enumerate(refs):
        n = ref.shape[0]
        at = lax.rem(slot + s, len(refs)) * n
        ref[...] = whole_ref[pl.ds(pl.multiple_of(at, n), n), :]


def spread(whole_ref, refs):
    for s, ref in enumerate(refs):
        n = ref.shape[0]
        ref[...] = whole_ref[pl.ds((len(refs) - s) % len(refs) * n, n), :]


def collect(refs, slot, target):
    for s, ref in enumerate(refs):
        n = ref.shape[0]
        at = pl.multiple_of(lax.rem(slot + len(refs) - s, len(refs)) * n, n)
        target[pl.ds(at, n), :] = ref[...]


def total(refs):
    out = refs[0][...].astype(F32)
    for ref in refs[1:]:
        out = out + ref[...].astype(F32)
    return out


def middle_forward(*refs):
    *z_refs, xp_ref, gains_ref, slot_ref, mixed_ref, h_ref = refs[:-CHUNKS]
    n = h_ref.shape[0]
    x = xp_ref[pl.ds(pl.multiple_of(slot_ref[0] * n, n), n), :].astype(F32)
    z = total(z_refs)
    h = x + norm(z, gains_ref[1:2, :])
    mixed_ref[...] = z
    h_ref[...] = h
    xn2 = norm(h, gains_ref[2:3, :]).astype(BF16)
    for c, ref in enumerate(refs[-CHUNKS:]):
        ref[...] = xn2[c * ref.shape[0] : (c + 1) * ref.shape[0]]


def load_weights(sources, target, sem, order):
    half = sources[0].shape[1]
    waits = []
    for i in order:
        pair = [
            pltpu.make_async_copy(
                ref.at[i], target.at[i, pl.ds(j * half, half)], sem.at[2 * i + j]
            )
            for j, ref in enumerate(sources)
        ]
        for c in pair:
            c.start()
        waits.append(lambda pair=pair: [c.wait() for c in pair])
    return waits


def ffn_forward(*refs):
    wm_ref, wo_ref = refs[RING : RING + 2]
    x_ref, act_ref, fa_ref, fb_ref, *part_refs = refs[RING + 2 : -3]
    part_ref, w_ref, sem = refs[-3:]
    waits = load_weights((wm_ref, wo_ref), w_ref, sem, (0, 1, 2))
    for s in range(RING):
        n = refs[s].shape[0]
        x_ref[s * n : (s + 1) * n] = refs[s][...]
    waits[0]()
    waits[1]()
    x = x_ref[...]
    for f, n in tiles(act_ref.shape[1], 256):
        gate = mm(x, w_ref[0, :, pl.ds(f, n)])
        up = mm(x, w_ref[1, :, pl.ds(f, n)])
        square = gate * gate
        t = jnp.tanh(GELU_C * (gate + GELU_A * (gate * square)))
        bell = 0.5 * (1.0 + t)
        g = gate * bell
        slope = bell + 0.5 * gate * (1.0 - t * t) * (GELU_C * (1.0 + 3.0 * GELU_A * square))
        act_ref[:, pl.ds(f, n)] = (g * up).astype(BF16)
        fa_ref[:, pl.ds(f, n)] = (slope * up).astype(BF16)
        fb_ref[:, pl.ds(f, n)] = g.astype(BF16)
    waits[2]()
    for d, n in tiles(part_ref.shape[1], 384):
        part_ref[:, pl.ds(d, n)] = mm_nt(act_ref[...], w_ref[2, pl.ds(d, n), :]).astype(BF16)
    spread(part_ref, part_refs)


def middle_turn(chunk, *refs):
    *m_refs, h_ref, dy_ref, order_ref, info_ref, gains_ref = refs[:-4]
    out_ref, dout_ref, dm_ref, term_ref = refs[-4:]
    n = dm_ref.shape[0]
    choose = one_hot(order_ref[...], h_ref.shape[1])
    m = total(m_refs)
    gain = gains_ref[3:4, :]
    here = pl.ds(chunk * n, n)
    out = (h_ref[here, :] + norm(m, gain)).astype(BF16)
    out_ref[...] = mm_nt(out, choose).astype(BF16)
    position = lax.broadcasted_iota(jnp.int32, (n, 1), 0) + (info_ref[0] * CHUNKS + chunk) * n
    dy = mm(dy_ref[here, :], choose) * jnp.where(position < info_ref[3], 1.0, 0.0)
    dout_ref[...] = dy
    dm_ref[...] = norm_back(m, dy, gain).astype(BF16)
    term_ref[...] = norm_term(m, dy)


def ffn_backward(*refs):
    fa_ref, fb_ref, wm_ref, wo_ref = refs[RING : RING + 4]
    slot_ref, dm_ref, dg_ref, du_ref, part_ref, w_ref, sem = refs[RING + 4 :]
    waits = load_weights((wm_ref, wo_ref), w_ref, sem, (2, 0, 1))
    for s in range(RING):
        n = refs[s].shape[0]
        dm_ref[s * n : (s + 1) * n] = refs[s][...]
    waits[0]()
    dm = dm_ref[...]
    for f, n in tiles(dg_ref.shape[1], 256):
        d = mm(dm, w_ref[2, :, pl.ds(f, n)])
        dg_ref[:, pl.ds(f, n)] = (d * fa_ref[:, pl.ds(f, n)].astype(F32)).astype(BF16)
        du_ref[:, pl.ds(f, n)] = (d * fb_ref[:, pl.ds(f, n)].astype(F32)).astype(BF16)
    waits[1]()
    waits[2]()
    for d, n in tiles(part_ref.shape[1], 384):
        part = mm_nt(dg_ref[...], w_ref[0, pl.ds(d, n), :])
        part = (part + mm_nt(du_ref[...], w_ref[1, pl.ds(d, n), :])).astype(BF16)
        for s in range(RING):
            m = refs[s].shape[0]
            at = pl.multiple_of(lax.rem(slot_ref[0] + RING - s, RING) * m, m)
            part_ref[pl.ds(at, m), pl.ds(d, n)] = part[s * m : (s + 1) * m]


def weight_grad(left_ref, right_ref, own_ref, other_ref, turned_ref):
    turned_ref[...] = left_ref[...].T
    half, n_right = own_ref.shape
    for r, n in tiles(half, 192):
        for at, out in ((r, own_ref), (half + r, other_ref)):
            grad = mm(turned_ref[pl.ds(at, n), :], right_ref[:, :n_right])
            out[pl.ds(r, n), :] = grad.astype(BF16)


def ffn_weight_grads(first, *refs):
    groups = [refs[CHUNKS * i : CHUNKS * (i + 1)] for i in range(5)]
    dm, xn2, act, dg, du = groups
    *rest, turned_ref = refs[CHUNKS * 5 :]
    half, part = turned_ref.shape[0], dm[0].shape[0]
    received = rest[:3] if len(rest) == 4 else []
    outs = [rest[3].at[i] for i in range(3)] if received else rest
    for i, (left, right) in enumerate(((xn2, dg), (xn2, du), (dm, act))):
        if i != 1:
            for c, ref in enumerate(left):
                turned = ref[:, first : first + half].T
                turned_ref[:, c * part : (c + 1) * part] = turned
        for r, n in tiles(half, 192):
            grad = sum(
                mm(turned_ref[pl.ds(r, n), c * part : (c + 1) * part], right[c][...])
                for c in range(CHUNKS)
            )
            if received:
                grad = grad + received[i][pl.ds(r, n), :].astype(F32)
            outs[i][pl.ds(r, n), :] = grad.astype(BF16)


def load_heads(sources, target, sem):
    half = sources[0].shape[1]
    copies = [
        pltpu.make_async_copy(
            ref, target.at[:, pl.ds(j * half, half), :], sem.at[j]
        )
        for j, ref in enumerate(sources)
    ]
    for c in copies:
        c.start()
    return lambda: [c.wait() for c in copies]


def middle_backward(g_ref, dout_ref, h_ref, mixed_ref, gains_ref, dh_ref, dz_ref, fterm_ref, aterm_ref):
    dxn2 = g_ref[0].astype(F32)
    h, mixed = h_ref[...], mixed_ref[...]
    dh = dout_ref[...] + norm_back(h, dxn2, gains_ref[2:3, :])
    dh_ref[...] = dh
    dz_ref[...] = norm_back(mixed, dh, gains_ref[1:2, :]).astype(BF16)
    fterm_ref[...] = norm_term(h, dxn2)
    aterm_ref[...] = norm_term(mixed, dh)


def attention_backward(*refs):
    (
        slot_ref, wout_ref, qraw_ref, q_ref, k_ref, v_ref, probs_ref, hgain_ref, cos_ref, sin_ref,
        dz_ref, part_ref, term_ref, *out_refs, datt_ref, ds_ref,
    ) = refs[RING:]
    rows, head = q_ref.shape
    collect(refs[:RING], slot_ref[0], dz_ref)
    datt_ref[...] = mm(dz_ref[...], wout_ref[...]).astype(BF16)
    term = jnp.zeros((1, head), F32)
    for r, n in tiles(rows, 128):
        p = probs_ref[pl.ds(r, n), :]
        dp = mm_nt(datt_ref[pl.ds(r, n), :], v_ref[...])
        ds = (p * (dp - jnp.sum(dp * p, axis=-1, keepdims=True))).astype(BF16)
        ds_ref[pl.ds(r, n), :] = ds
        dq = (mm(ds, k_ref[...]) * SCALE).astype(BF16).astype(F32)
        cosine, sine = cos_ref[pl.ds(r, n), :], sin_ref[pl.ds(r, n), :]
        e = rotate_back(dq, cosine, sine)
        raw = qraw_ref[pl.ds(r, n), :]
        term = term + norm_term(raw, e)
        part_ref[pl.ds(r, n), :head] = norm_back(raw, e, hgain_ref[4:5, :]).astype(BF16)
    term_ref[...] = term
    part_ref[:, head : 2 * head] = (mm_tn(ds_ref[...], q_ref[...]) * SCALE).astype(BF16)
    part_ref[:, 2 * head :] = mm_tn(probs_ref[...].astype(BF16), datt_ref[...]).astype(BF16)
    hand_out(part_ref, slot_ref[0], out_refs)


def last_rows(
    g0_ref, g1_ref, g2_ref, g3_ref, xp_ref, xn1_ref, dh_ref, kraw_ref, cos_ref, sin_ref, hgain_ref, gains_ref, order_ref,
    pick_ref, slot_ref, t1_ref, t2_ref, t3_ref, qterm_ref, qm_ref, qo_ref, om_ref, oo_ref, w_ref, hm_ref, ho_ref,
    out_ref, own_ref, other_ref,
    wq_ref, hsem,
):
    head = kraw_ref.shape[1]
    n, width = dh_ref.shape
    half = width // 2
    arrived = load_heads((hm_ref, ho_ref), wq_ref, hsem)
    here = pl.ds(pl.multiple_of(slot_ref[0] * n, n), n)
    g_refs = (g0_ref, g1_ref, g2_ref, g3_ref)
    joined = sum(ref[:, head:].astype(F32) for ref in g_refs)
    dk = joined[:, :head].astype(BF16).astype(F32)
    e = rotate_back(dk, cos_ref[here, :], sin_ref[here, :])
    raw = kraw_ref[here, :]
    kterm = norm_term(raw, e)
    dkr = norm_back(raw, e, hgain_ref[5:6, :]).astype(BF16)
    dkv = jnp.concatenate([dkr, joined[:, head:].astype(BF16)], axis=1)
    dxn1 = mm_nt(dkv, w_ref[...])
    arrived()
    for i, ref in enumerate(g_refs):
        dxn1 = dxn1 + mm_nt(ref[:, :head], wq_ref[i])
    x = xp_ref[here, :].astype(F32)
    dx = (dh_ref[...] + norm_back(x, dxn1, gains_ref[0:1, :])).astype(BF16)
    term = norm_term(x, dxn1)
    choose = one_hot(order_ref[...], width)
    out_ref[...] = mm_nt(dx, choose).astype(BF16)
    grad = mm_tn(xn1_ref[here, :], dkv)
    for i, (mine, others) in enumerate(((qm_ref, qo_ref), (om_ref, oo_ref))):
        own_ref[:, i * head : (i + 1) * head] = mine[...]
        other_ref[:, i * head : (i + 1) * head] = others[...]
    own_ref[:, 2 * head : 4 * head] = grad[:half].astype(BF16)
    other_ref[:, 2 * head : 4 * head] = grad[half:].astype(BF16)
    small = jnp.concatenate([qterm_ref[...], kterm, jnp.zeros((6, head), F32)], axis=0)
    small = mm_nt(small.astype(BF16), one_hot(pick_ref[...], width))
    terms = [term, t1_ref[...], t2_ref[...], t3_ref[...], small[0:2], jnp.zeros((122, width), F32)]
    terms = jnp.concatenate(terms, axis=0).T
    own_ref[:, 4 * head :] = terms[:half].astype(BF16)
    other_ref[:, 4 * head :] = terms[half:].astype(BF16)


def on_device(
    tokens,
    cotangent,
    seq_lengths,
    query_weight,
    key_weight,
    value_weight,
    outproj_weight,
    gate_weight,
    up_weight,
    down_weight,
    attn_gain,
    attnout_gain,
    ffn_gain,
    ffnout_gain,
    query_gain,
    key_gain,
):
    width = tokens.shape[3]
    wide, narrow = lax.axis_size("wide"), lax.axis_size("narrow")
    chips = wide // 2
    core = lax.axis_index("wide") % 2
    slot = lax.axis_index("narrow")
    slots = jnp.reshape(slot, (1,)).astype(jnp.int32)
    same_core = [[i for i in range(wide) if i % 2 == c] for c in range(2)]
    swap = [(i, i ^ 1) for i in range(wide)]
    upward = [(i, i + 1) for i in range(narrow - 1)]
    downward = [(i + 1, i) for i in range(narrow - 1)]
    dw = width // wide
    dh = query_gain.shape[0]
    head = key_weight.shape[1]
    units = gate_weight.shape[1]
    half = width // 2

    def gather_wide(value, axis):
        return lax.all_gather(
            value, "wide", axis=axis, tiled=True, axis_index_groups=same_core
        )

    def sibling(value):
        return lax.ppermute(value, "wide", swap)

    def pair_sum(own, other):
        return (own.astype(F32) + sibling(other).astype(F32)).astype(BF16)

    def scatter_wide(value, axis):
        return lax.psum_scatter(
            value, "wide", scatter_dimension=axis, tiled=True, axis_index_groups=same_core
        )

    def after(value, *others):
        return lax.optimization_barrier((value, *others))[0]

    def gather_rows(value):
        return lax.all_gather(value, "narrow", axis=0, tiled=True)

    def gather_ring(value):
        return pass_on([value] * narrow)

    def pass_on(parts):
        got = [parts[0]]
        for s in range(1, narrow):
            shift = [(i, (i + s) % narrow) for i in range(narrow)]
            got.append(lax.ppermute(parts[s], "narrow", shift))
        return got

    def exchange_z(value):
        parts = value.reshape(narrow, -1, value.shape[-1])
        return lax.all_to_all(parts, "narrow", split_axis=0, concat_axis=0, tiled=True)

    def enter(value):
        value = value.reshape(value.shape[0], value.shape[2], width)
        value = lax.all_to_all(value, "wide", split_axis=0, concat_axis=0, tiled=True)
        return value.reshape(-1, width)

    def leave(value):
        value = value.reshape(wide, -1, width)
        value = lax.all_to_all(value, "wide", split_axis=0, concat_axis=0, tiled=True)
        return value.reshape(wide, 1, -1, width)

    bf, ff = BF16, F32
    pack = call(packing, [((dw, 4 * head + 128), bf)], count=10, flops=10**6, moved=10**6)(
        query_weight, key_weight, value_weight, outproj_weight,
        attn_gain, attnout_gain, ffn_gain, ffnout_gain, query_gain, key_gain,
    )[0]
    wa_mine = gather_wide(pack, 0)
    own_x = enter(tokens)
    quarter = own_x.shape[0]
    rows = quarter * narrow
    part = quarter // CHUNKS
    every = range(CHUNKS)
    sem = pltpu.SemaphoreType.DMA
    f_scratch = pltpu.VMEM((3, width, units), bf)
    x_all = gather_ring(own_x)
    wf_mine = gather_wide(after(jnp.stack([gate_weight, up_weight, down_weight]), own_x), 1)
    weights = [sibling(after(wa_mine, *x_all)), wa_mine]
    queries = gather_ring(after(query_weight, *x_all))
    wh_mine = gather_wide(after(jnp.stack(queries), wf_mine), 1)
    lengths = seq_lengths[0]
    info = [slot, core, lengths[0], lengths[0] + lengths[1], 0]
    info = jnp.stack([jnp.asarray(v, jnp.int32) for v in info])
    own_dy = enter(after(cotangent, own_x))
    many = len(x_all) + len(weights)
    (
        xp, xn1, qraw, kraw, q, k, v, probs, attended, gains, hgain, wkv, wout, cosine, sine, order, pick,
        *z_parts,
    ) = call(
        functools.partial(attention_forward, wide),
        [
            ((rows, width), bf), ((rows, width), bf), ((rows, head), ff), ((rows, head), ff),
            ((rows, head), bf), ((rows, head), bf), ((rows, head), bf), ((rows, rows), ff),
            ((rows, head), bf), ((8, width), ff), ((8, head), ff), ((width, 2 * head), bf), ((width, head), bf),
            ((rows, head // 2), ff), ((rows, head // 2), ff), ((1, width), jnp.int32),
            ((1, head), jnp.int32),
        ]
        + [((quarter, width), bf)] * narrow,
        scratch=[
            pltpu.VMEM((rows, width), bf), pltpu.VMEM((rows, width), bf),
            pltpu.VMEM((width, 4 * head + 128), bf), sem((len(weights),)),
        ],
        anys=tuple(range(len(x_all), many)), smem=(many,), count=many + 1,
        flops=3 * 10**9, moved=8 * 10**6,
    )(*x_all, *weights, info)
    z_parts = [after(p, *queries) for p in z_parts]
    z = pass_on(z_parts)
    mixed, h, *xn2_own = call(
        middle_forward,
        [((quarter, width), ff)] * 2 + [((part, width), bf)] * CHUNKS,
        smem=(narrow + 2,), count=narrow + 3, flops=10**7, moved=2 * 10**6,
    )(*z, xp, gains, slots)
    xn2 = [gather_ring(xn2_own[c]) for c in every]
    wf_other = sibling(after(wf_mine, *xn2[0]))
    def ffn_ahead(c):
        return call(
            ffn_forward,
            [((narrow * part, width), bf)] + [((narrow * part, units), bf)] * 3
            + [((part, width), bf)] * narrow,
            scratch=[pltpu.VMEM((narrow * part, width), bf), f_scratch, sem((6,))],
            anys=(narrow, narrow + 1), count=narrow + 2, flops=3 * 10**9, moved=16 * 10**6,
        )(*xn2[c], wf_mine, wf_other)

    ahead = []
    for c in every:
        if c:
            xn2[c][0] = after(xn2[c][0], ahead[-1][1])
        ahead.append(ffn_ahead(c))
    xn2_all, act, fa, fb, *m_part = zip(*ahead)
    m = [pass_on([p[c] for p in m_part]) for c in every]
    out_own, d_out, dm_own, turn_term = zip(*[
        call(
            functools.partial(middle_turn, c),
            [((part, width), bf), ((part, width), ff), ((part, width), bf), ((1, width), ff)],
            smem=(narrow + 3,), count=narrow + 5, flops=10**8, moved=4 * 10**6,
        )(*m[c], h, own_dy, order, info, gains)
        for c in every
    ])
    dm = [gather_ring(dm_own[c]) for c in every]

    dm[0][0] = after(dm[0][0], wh_mine)

    def ffn_back(c):
        return call(
            ffn_backward,
            [((narrow * part, width), bf)] + [((narrow * part, units), bf)] * 2
            + [((narrow * part, width), bf)],
            scratch=[f_scratch, sem((6,))],
            anys=(narrow + 2, narrow + 3), smem=(narrow + 4,), count=narrow + 5,
            flops=3 * 10**9, moved=16 * 10**6,
        )(*dm[c], fa[c], fb[c], wf_mine, wf_other, slots)

    back = []
    for c in every:
        if c:
            dm[c][0] = after(dm[c][0], back[-1][1])
        back.append(ffn_back(c))
    dm_all, d_gate, d_up, dxn2_part = zip(*back)
    dxn2 = lax.psum_scatter(
        dxn2_part[0].reshape(narrow, quarter, width), "narrow", scatter_dimension=0, tiled=True
    )
    saved = (*dm_all, *xn2_all, *act, *d_gate, *d_up)

    def ffn_grads(first, *received):
        outs = [((3, half, units), bf)] if received else [((half, units), bf)] * 3
        return call(
            functools.partial(ffn_weight_grads, first),
            outs,
            scratch=[pltpu.VMEM((half, rows), bf)],
            count=5 * CHUNKS + len(received), flops=10**6, moved=10**6,
        )(*saved, *received)

    ffn_other = [sibling(g) for g in ffn_grads(half)]
    ffn_sum = ffn_grads(0, *ffn_other)[0]
    dxn2 = after(dxn2, ffn_sum)
    s_ffn = scatter_wide(ffn_sum, 1)
    left_out = leave(out_own[0])
    d_resid, dz_own, ffn_term, attnout_term = call(
        middle_backward,
        [((quarter, width), ff), ((quarter, width), bf), ((1, width), ff), ((1, width), ff)],
        count=5, flops=10**7, moved=3 * 10**6,
    )(dxn2, d_out[0], h, mixed, gains)
    dz = gather_ring(dz_own)
    wh_other = sibling(after(wh_mine, dz_own))
    dz_all, joined_part, query_term, *joined = call(
        attention_backward,
        [((rows, width), bf), ((rows, 3 * head), bf), ((1, head), ff)]
        + [((quarter, 3 * head), bf)] * narrow,
        scratch=[pltpu.VMEM((rows, head), bf), pltpu.VMEM((rows, rows), bf)],
        smem=(narrow,), count=narrow + 10, flops=2 * 10**9, moved=6 * 10**6,
    )(*dz, slots, wout, qraw, q, k, v, probs, hgain, cosine, sine)
    joined = pass_on(joined)

    def outer(left, right, columns):
        return call(
            weight_grad,
            [((half, columns), bf)] * 2,
            scratch=[pltpu.VMEM((width, left.shape[0]), bf)],
            count=2, flops=2 * width * left.shape[0] * columns, moved=3 * 10**6,
        )(left, right)

    g_query = outer(xn1, joined_part, head)
    g_outproj = outer(dz_all, attended, head)
    joined[0] = after(joined[0], left_out, *g_query, *g_outproj)
    heads = wh_mine.shape[0]
    dx_own, own, other = call(
        last_rows,
        [((quarter, width), bf)] + [((half, 4 * head + 128), bf)] * 2,
        scratch=[pltpu.VMEM((heads, width, head), bf), sem((2,))],
        smem=(14,), anys=(24, 25), count=26, flops=10**9, moved=8 * 10**6,
    )(
        *joined, xp, xn1, d_resid, kraw, cosine, sine, hgain, gains, order, pick, slots,
        attnout_term, ffn_term, *turn_term, query_term, *g_query, *g_outproj, wkv,
        wh_mine, wh_other,
    )

    def scatter_chips(value):
        parts = value.reshape(chips, dw, value.shape[1])
        parts = lax.all_to_all(
            parts, "wide", split_axis=0, concat_axis=0, tiled=True, axis_index_groups=same_core
        )
        return parts.astype(F32).sum(axis=0)

    left_dx = leave(dx_own)
    last = scatter_chips(after(pair_sum(own, other), left_dx))
    s_query, s_outproj = last[:, :head], last[:, head : 2 * head]
    last = last[:, 2 * head :].astype(BF16)
    last, s_ffn = lax.optimization_barrier((last, s_ffn))
    s_ffn = s_ffn.astype(F32)
    shared = lax.all_gather(last, "narrow").astype(F32).sum(axis=0)
    small = shared[:, 2 * head :]
    return (
        left_out,
        left_dx,
        s_query,
        shared[:, :head],
        shared[:, head : 2 * head],
        s_outproj,
        s_ffn[0],
        s_ffn[1],
        s_ffn[2],
        small[:, 0],
        small[:, 1],
        small[:, 2],
        small[:, 3],
        small[:dh, 4],
        small[:dh, 5],
    )


def solution(mesh):
    return jax.shard_map(
        on_device,
        mesh=mesh,
        in_specs=(
            P(None, "narrow", "wide", None),
            P(None, "narrow", "wide", None),
            P("wide", None),
            P("wide", "narrow"),
            P("wide", None),
            P("wide", None),
            P("wide", "narrow"),
            P("wide", "narrow"),
            P("wide", "narrow"),
            P("wide", "narrow"),
            P("wide"),
            P("wide"),
            P("wide"),
            P("wide"),
            P("wide"),
            P("wide"),
        ),
        out_specs=(
            P(None, "narrow", "wide", None),
            P(None, "narrow", "wide", None),
            P("wide", "narrow"),
            P("wide", None),
            P("wide", None),
            P("wide", "narrow"),
            P("wide", "narrow"),
            P("wide", "narrow"),
            P("wide", "narrow"),
            P("wide"),
            P("wide"),
            P("wide"),
            P("wide"),
            P("wide"),
            P("wide"),
        ),
        check_vma=False,
    )
```

time: 485 us -> 397 us (0.82)
  waiting for transfers between devices: 184 us -> 143 us
  other arithmetic: 27.7 us -> 4.4 us
  starting transfers between devices: 82.4 us -> 68.1 us
  blocking collectives: 65.6 us -> 51.6 us
  Pallas kernels: 87.9 us -> 92.9 us
    ppermute x24, waiting for transfers between devices: 60.4 us -> 109 us  [pass_on(): got.append(lax.ppermute(parts[s], 'narrow', shift))]
    reduce_scatter x3 -> x1, waiting for transfers between devices: 45.4 us -> 0.02 us  [scatter_wide(): lax.psum_scatter(value, 'wide', scatter_dimension=axis, tiled=True, axis_...]
    all_to_all x2 -> x0, waiting for transfers between devices: 36.8 us -> none  [exchange_z(): lax.all_to_all(parts, 'narrow', split_axis=0, concat_axis=0, tiled=True)]
    unnamed x8 -> x5, waiting for transfers between devices: 15.7 us -> 0.08 us
    all_to_all x1, blocking collectives: 33.9 us -> 19.3 us  [scatter_chips(): lax.all_to_all(parts, 'wide', split_axis=0, concat_axis=0, tiled=True, ax...]
    convert_element_type x4 -> x1, other arithmetic: 14.5 us -> 1.71 us  [pair_sum(): return (own.astype(F32) + sibling(other).astype(F32)).astype(BF16)]
    all_to_all x2 -> x0, starting transfers between devices: 8.87 us -> none  [exchange_z(): lax.all_to_all(parts, 'narrow', split_axis=0, concat_axis=0, tiled=True)]
    ppermute x6 -> x7, waiting for transfers between devices: 12.5 us -> 19.1 us  [sibling(): return lax.ppermute(value, 'wide', swap)]
  transfers between devices with their start and end apart: 42 -> 39, of which waited for: 30 -> 19; matrix products, arithmetic and copies ran while one was open for 6% -> 2% of each run, Pallas kernels for 11% -> 19%
where the time goes in v2:
time: 397 us; the launch traced here: 390 us
  waiting for transfers between devices  143 us (36%)
  Pallas kernels  92.9 us (23%)
  starting transfers between devices  68.1 us (17%)
  blocking collectives  51.6 us (13%)
  between operations  15.9 us (4%)
  local copies, waits for them, and re-layouts  14.2 us (4%)
  other arithmetic  4.4 us (1%)
    ppermute x24, waiting for transfers between devices, pass_on(): got.append(lax.ppermute(parts[s], 'narrow', shift))  109 us
    ppermute x24, starting transfers between devices, pass_on(): got.append(lax.ppermute(parts[s], 'narrow', shift))  54.7 us
    all_gather x1, blocking collectives, on_device(): shared = lax.all_gather(last, 'narrow').astype(F32).sum(axis=0)  21.9 us
    pallas_call x2, Pallas kernels, ffn_grads(): call(functools.partial(ffn_weight_grads, first), outs, scratch=[pltpu.VME...  19.4 us
    all_to_all x1, blocking collectives, scatter_chips(): lax.all_to_all(parts, 'wide', split_axis=0, concat_axis=0, tiled=True, ax...  19.3 us
    ppermute x7, waiting for transfers between devices, sibling(): return lax.ppermute(value, 'wide', swap)  19.1 us
    pallas_call x1, Pallas kernels, ffn_ahead(): call(ffn_forward, [((narrow * part, width), bf)] + [((narrow * part, unit...  15.3 us
    pallas_call x1, Pallas kernels, ffn_back(): call(ffn_backward, [((narrow * part, width), bf)] + [((narrow * part, uni...  15.3 us
  transfers between devices with their start and end apart: 39, of which 19 were waited for; matrix products, arithmetic and copies ran while one was open for 2% of the time, Pallas kernels for 19%

profile of v2, /device:TPU:0, one launch (start us, length us, event | category | flops | bytes accessed | tf_op | source)
XLA Modules:
  0.0 389.9 jit_solution(4182615888131246953)
XLA Ops:
  7.3 2.1 shard_map.271
  9.3 5.2 %all-to-all-start = ((bf16[8,16,1152]{2,1,0:T(8,128)(2,1)}), bf16[8,16,1152]{2,1,0:T(8,128)(2,1)S(1)}, u32[]{:S(2)}, u32[]{:S(2)}) async-start(bf16[8,16,1152]{2,1,0:T(8,128)(2,1)} %bitcast.43), calls=%async_computation | async-start | bytes 589824 | tf_op jit(solution)/shard_map/all_to_all | solution.py:519
  16.0 5.8 %all-to-all-done = bf16[8,16,1152]{2,1,0:T(8,128)(2,1)S(1)} async-done(((bf16[8,16,1152]{2,1,0:T(8,128)(2,1)}), bf16[8,16,1152]{2,1,0:T(8,128)(2,1)S(1)}, u32[]{:S(2)}, u32[]{:S(2)}) %all-to-all-start) | async-done | bytes 294944 | tf_op jit(solution)/shard_map/all_to_all | solution.py:519
  23.5 2.6 collective-permute-start.1
  27.5 6.4 %collective-permute-done.refs_1_ = bf16[128,1152]{1,0:T(8,128)(2,1)S(1)} collective-permute-done((bf16[128,1152]{1,0:T(8,128)(2,1)S(1)}, bf16[128,1152]{1,0:T(8,128)(2,1)S(1)}, u32[]{:S(2)}, u32[]{:S(2)}) %collective-permute-start) | collective-permute-done | bytes 294944 | tf_op jit(solution)/shard_map/ppermute | solution.py:510
  33.8 10.7 %collective-permute-done.1.refs_2_ = bf16[128,1152]{1,0:T(8,128)(2,1)S(1)} collective-permute-done((bf16[128,1152]{1,0:T(8,128)(2,1)S(1)}, bf16[128,1152]{1,0:T(8,128)(2,1)S(1)}, u32[]{:S(2)}, u32[]{:S(2)}) %collective-permute-start.1) | collective-permute-done | bytes 294944 | tf_op jit(solution)/shard_map/ppermute | solution.py:510
  44.6 6.7 %collective-permute-start.4 = (bf16[144,256]{1,0:T(8,128)(2,1)S(1)}, bf16[144,256]{1,0:T(8,128)(2,1)S(1)}, u32[]{:S(2)}, u32[]{:S(2)}) collective-permute-start(bf16[144,256]{1,0:T(8,128)(2,1)S(1)} %copy-done.19), channel_id=1, source_target_pairs={{0,1},{1,2},{2,3},{3,0},{4,5},{5,6},{6,7},{7,4},{8,9},{9,10},{10,1... | collective-permute-start | bytes 221192 | tf_op jit(solution)/shard_map/ppermute | solution.py:510
  58.0 10.1 %shard_map.272 = (bf16[512,1152]{1,0:T(8,128)(2,1)}, bf16[512,1152]{1,0:T(8,128)(2,1)}, f32[512,256]{1,0:T(8,128)}, f32[512,256]{1,0:T(8,128)}, bf16[512,256]{1,...) custom-call(bf16[128,1152]{1,0:T(8,128)(2,1)} %bitcast.34, ...), custom_call_target="tpu_custom_call" | custom-call | flops 1 | bytes 1 | tf_op jit(solution)/shard_map/pallas_call | solution.py:553
  68.2 2.0 collective-permute-start.9
  71.1 6.9 %collective-permute-done.9.refs_3_ = bf16[128,1152]{1,0:T(8,128)(2,1)S(1)} collective-permute-done((bf16[128,1152]{1,0:T(8,128)(2,1)}, bf16[128,1152]{1,0:T(8,128)(2,1)S(1)}, u32[]{:S(2)}, u32[]{:S(2)}) %collective-permute-start.9) | collective-permute-done | bytes 294944 | tf_op jit(solution)/shard_map/ppermute | solution.py:510
  78.0 18.6 %collective-permute-done.8.refs_2_ = bf16[128,1152]{1,0:T(8,128)(2,1)S(1)} collective-permute-done((bf16[128,1152]{1,0:T(8,128)(2,1)}, bf16[128,1152]{1,0:T(8,128)(2,1)S(1)}, u32[]{:S(2)}, u32[]{:S(2)}) %collective-permute-start.8) | collective-permute-done | bytes 294944 | tf_op jit(solution)/shard_map/ppermute | solution.py:510
  97.4 2.9 shard_map.273
  101.8 2.9 collective-permute-start.12
  104.7 7.7 %collective-permute-done.10.refs_1_ = bf16[128,1152]{1,0:T(8,128)(2,1)S(1)} collective-permute-done((bf16[128,1152]{1,0:T(8,128)(2,1)}, bf16[128,1152]{1,0:T(8,128)(2,1)S(1)}, u32[]{:S(2)}, u32[]{:S(2)}) %collective-permute-start.10) | collective-permute-done | bytes 294944 | tf_op jit(solution)/shard_map/ppermute | solution.py:510
  112.4 10.4 %collective-permute-done.11.refs_2_ = bf16[128,1152]{1,0:T(8,128)(2,1)S(1)} collective-permute-done((bf16[128,1152]{1,0:T(8,128)(2,1)}, bf16[128,1152]{1,0:T(8,128)(2,1)S(1)}, u32[]{:S(2)}, u32[]{:S(2)}) %collective-permute-start.11) | collective-permute-done | bytes 294944 | tf_op jit(solution)/shard_map/ppermute | solution.py:510
  124.0 9.3 %collective-permute-done.13.refs_5_.refs_7_ = bf16[3,576,1728]{2,1,0:T(8,128)(2,1)} collective-permute-done((bf16[3,576,1728]{2,1,0:T(8,128)(2,1)}, bf16[3,576,1728]{2,1,0:T(8,128)(2,1)}, u32[]{:S(2)}, u32[]{:S(2)}) %collective-permute-start.13) | collective-permute-done | bytes 5972000 | tf_op jit(solution)/shard_map/ppermute | solution.py:487
  133.3 15.3 %shard_map.274 = (bf16[512,1152]{1,0:T(8,128)(2,1)}, bf16[512,1728]{1,0:T(8,128)(2,1)}, bf16[512,1728]{1,0:T(8,128)(2,1)}, bf16[512,1728]{1,0:T(8,128)(2,1)}, bf...) custom-call(bf16[128,1152]{1,0:T(8,128)(2,1)} %get-tuple-element.105, ...), custom_call_target="tpu_custom_call" | custom-call | flops 1 | bytes 1 | tf_op jit(solution)/shard_map/pallas_call | solution.py:580
  148.6 5.6 %collective-permute-start.14 = (bf16[128,1152]{1,0:T(8,128)(2,1)}, bf16[128,1152]{1,0:T(8,128)(2,1)S(1)}, u32[]{:S(2)}, u32[]{:S(2)}) collective-permute-start(bf16[128,1152]{1,0:T(8,128)(2,1)} %get-tuple-element.109), channel_id=1, source_target_pairs={{0,1},{1,2},{2,3},{3,0},{4,5},{5,6},{6,7},{7,4},{8,9},{9,10},{10,1... | collective-permute-start | bytes 884744 | tf_op jit(solution)/shard_map/ppermute | solution.py:510
  154.2 2.1 collective-permute-start.15
  156.6 10.4 %all_to_all.25 = bf16[8,16,1152]{2,1,0:T(8,128)(2,1)} all-to-all(bf16[8,16,1152]{2,1,0:T(8,128)(2,1)S(1)} %bitcast.44), channel_id=1, replica_groups=mesh['wide'=8,'narrow'=4] {'wide'}, dimensions={0} | all-to-all | bytes 589824 | tf_op jit(solution)/shard_map/all_to_all | solution.py:519
  167.0 9.1 %collective-permute-done.15.refs_2_ = bf16[128,1152]{1,0:T(8,128)(2,1)S(1)} collective-permute-done((bf16[128,1152]{1,0:T(8,128)(2,1)}, bf16[128,1152]{1,0:T(8,128)(2,1)S(1)}, u32[]{:S(2)}, u32[]{:S(2)}) %collective-permute-start.15) | collective-permute-done | bytes 294944 | tf_op jit(solution)/shard_map/ppermute | solution.py:510
  176.8 4.1 %shard_map.275 = (bf16[128,1152]{1,0:T(8,128)(2,1)}, f32[128,1152]{1,0:T(8,128)}, bf16[128,1152]{1,0:T(8,128)(2,1)}, f32[1,1152]{1,0:T(1,128)}) custom-call(bf16[128,1152]{1,0:T(8,128)(2,1)} %get-tuple-element.108.refs_0_, bf16[128,1152]{1,0:T(8,128)(2,1)} %copy-done.21, bf16[128,1152]{1,0:T(8,128)(2,1)} %copy-done.23, bf16[128,1152]{1,0:T(8,128)(2,1)} %copy-done.25, ...), custom_call_target="tpu_custom_call" | custom-call | flops 1 | bytes 1 | tf_op jit(solution)/shard_map/pallas_call | solution.py:596
  181.0 6.7 %collective-permute-start.17 = (bf16[128,1152]{1,0:T(8,128)(2,1)}, bf16[128,1152]{1,0:T(8,128)(2,1)S(1)}, u32[]{:S(2)}, u32[]{:S(2)}) collective-permute-start(bf16[128,1152]{1,0:T(8,128)(2,1)} %get-tuple-element.118.refs_0_), channel_id=1, source_target_pairs={{0,1},{1,2},{2,3},{3,0},{4,5},{5,6},{6,7},{7,4},{8,9},{9,10},{10,1... | collective-permute-start | bytes 884744 | tf_op jit(solution)/shard_map/ppermute | solution.py:510
  190.1 6.1 %collective-permute-done.17.refs_1_ = bf16[128,1152]{1,0:T(8,128)(2,1)S(1)} collective-permute-done((bf16[128,1152]{1,0:T(8,128)(2,1)}, bf16[128,1152]{1,0:T(8,128)(2,1)S(1)}, u32[]{:S(2)}, u32[]{:S(2)}) %collective-permute-start.17) | collective-permute-done | bytes 294944 | tf_op jit(solution)/shard_map/ppermute | solution.py:510
  196.2 11.6 %collective-permute-done.18.refs_2_ = bf16[128,1152]{1,0:T(8,128)(2,1)S(1)} collective-permute-done((bf16[128,1152]{1,0:T(8,128)(2,1)}, bf16[128,1152]{1,0:T(8,128)(2,1)S(1)}, u32[]{:S(2)}, u32[]{:S(2)}) %collective-permute-start.18) | collective-permute-done | bytes 294944 | tf_op jit(solution)/shard_map/ppermute | solution.py:510
  208.6 15.3 %shard_map.276 = (bf16[512,1152]{1,0:T(8,128)(2,1)}, bf16[512,1728]{1,0:T(8,128)(2,1)}, bf16[512,1728]{1,0:T(8,128)(2,1)}, bf16[512,1152]{1,0:T(8,128)(2,1)}) custom-call(bf16[128,1152]{1,0:T(8,128)(2,1)} %get-tuple-element.118.refs_0_, bf16[128,1152]{1,0:T(8,128)(2,1)} %copy-done.27, bf16[128,1152]{1,0:T(8,128)(2,1)} %copy-done.28, ...), custom_call_target="tpu_custom_call" | custom-call | flops 1 | bytes 1 | tf_op jit(solution)/shard_map/pallas_call | solution.py:608
  224.1 8.2 %shard_map.277 = (bf16[576,1728]{1,0:T(8,128)(2,1)}, bf16[576,1728]{1,0:T(8,128)(2,1)}, bf16[576,1728]{1,0:T(8,128)(2,1)}) custom-call(bf16[512,1152]{1,0:T(8,128)(2,1)} %get-tuple-element.122.refs_0_, bf16[512,1152]{1,0:T(8,128)(2,1)} %get-tuple-element.123.refs_1_, bf16[512,1728]{1,0:T(8,128)(2,1)} %get-tuple-element.124.refs_2_, ...), custom_call_target="tpu_custom_call" | custom-call | flops 1 | bytes 1 | tf_op jit(solution)/shard_map/pallas_call | solution.py:630
  232.8 3.8 collective-permute-done.20.refs_5_
  236.6 5.9 %collective-permute-done.21.refs_6_ = bf16[576,1728]{1,0:T(8,128)(2,1)S(1)} collective-permute-done((bf16[576,1728]{1,0:T(8,128)(2,1)}, bf16[576,1728]{1,0:T(8,128)(2,1)S(1)}, u32[]{:S(2)}, u32[]{:S(2)}) %collective-permute-start.21) | collective-permute-done | bytes 1990688 | tf_op jit(solution)/shard_map/ppermute | solution.py:487
  244.0 11.2 %shard_map.278 = bf16[3,576,1728]{2,1,0:T(8,128)(2,1)} custom-call(bf16[512,1152]{1,0:T(8,128)(2,1)} %get-tuple-element.122.refs_0_, bf16[512,1152]{1,0:T(8,128)(2,1)} %get-tuple-element.123.refs_1_, bf16[512,1728]{1,0:T(8,128)(2,1)} %get-tuple-element.124.refs_2_, bf16[512,1728]{1,0:T(8,128)(2,1)} %get-tuple-element.125.refs_3_, ...), custom_call_target="tpu_custom_call" | custom-call | flops 1 | bytes 1 | tf_op jit(solution)/shard_map/pallas_call | solution.py:630
  255.2 3.4 reduce-scatter.3.cloned.1.call-done.g_ref
  258.6 2.8 shard_map.279
  261.4 3.6 collective-permute-start.23
  265.0 2.5 collective-permute-start.24
  267.5 3.4 all-to-all-start.2
  270.9 4.2 %collective-permute-done.23.refs_1_ = bf16[128,1152]{1,0:T(8,128)(2,1)S(1)} collective-permute-done((bf16[128,1152]{1,0:T(8,128)(2,1)}, bf16[128,1152]{1,0:T(8,128)(2,1)S(1)}, u32[]{:S(2)}, u32[]{:S(2)}) %collective-permute-start.23) | collective-permute-done | bytes 294944 | tf_op jit(solution)/shard_map/ppermute | solution.py:510
  275.1 12.3 %collective-permute-done.24.refs_2_ = bf16[128,1152]{1,0:T(8,128)(2,1)S(1)} collective-permute-done((bf16[128,1152]{1,0:T(8,128)(2,1)}, bf16[128,1152]{1,0:T(8,128)(2,1)S(1)}, u32[]{:S(2)}, u32[]{:S(2)}) %collective-permute-start.24) | collective-permute-done | bytes 294944 | tf_op jit(solution)/shard_map/ppermute | solution.py:510
  288.3 6.1 %shard_map.280 = (bf16[512,1152]{1,0:T(8,128)(2,1)}, bf16[512,768]{1,0:T(8,128)(2,1)}, f32[1,256]{1,0:T(1,128)}, bf16[128,768]{1,0:T(8,128)(2,1)}, bf16[128,768]...) custom-call(bf16[128,1152]{1,0:T(8,128)(2,1)} %get-tuple-element.133.refs_0_, ...), custom_call_target="tpu_custom_call" | custom-call | flops 1 | bytes 1 | tf_op jit(solution)/shard_map/pallas_call | solution.py:649
  294.4 6.8 %collective-permute-start.26 = (bf16[128,768]{1,0:T(8,128)(2,1)}, bf16[128,768]{1,0:T(8,128)(2,1)S(1)}, u32[]{:S(2)}, u32[]{:S(2)}) collective-permute-start(bf16[128,768]{1,0:T(8,128)(2,1)} %get-tuple-element.153), channel_id=1, source_target_pairs={{0,1},{1,2},{2,3},{3,0},{4,5},{5,6},{6,7},{7,4},{8,9},{9,10},{10,1... | collective-permute-start | bytes 589832 | tf_op jit(solution)/shard_map/ppermute | solution.py:510
  301.5 2.4 collective-permute-start.28
  303.9 2.7 shard_map.282
  306.5 2.9 shard_map.281
  309.5 5.0 %collective-permute-done.27.g2_ref = bf16[128,768]{1,0:T(8,128)(2,1)S(1)} collective-permute-done((bf16[128,768]{1,0:T(8,128)(2,1)}, bf16[128,768]{1,0:T(8,128)(2,1)S(1)}, u32[]{:S(2)}, u32[]{:S(2)}) %collective-permute-start.27) | collective-permute-done | bytes 196640 | tf_op jit(solution)/shard_map/ppermute | solution.py:510
  315.7 9.2 %shard_map.283 = (bf16[128,1152]{1,0:T(8,128)(2,1)}, bf16[576,1152]{1,0:T(8,128)(2,1)}, bf16[576,1152]{1,0:T(8,128)(2,1)}) custom-call(bf16[128,768]{1,0:T(8,128)(2,1)} %get-tuple-element.152.g0_ref, bf16[128,768]{1,0:T(8,128)(2,1)} %copy-done.30, bf16[128,768]{1,0:T(8,128)(2,1)} %copy-done.31, bf16[128,768]{1,0:T(8,128)(2,1)} %copy-done.32, ...), custom_call_target="tpu_custom_call" | custom-call | flops 1 | bytes 1 | tf_op jit(solution)/shard_map/pallas_call | solution.py:670
  324.9 3.4 all-to-all-start.3
  330.1 5.5 %all-to-all-done.3 = bf16[8,16,1152]{2,1,0:T(8,128)(2,1)S(1)} async-done(((bf16[8,16,1152]{2,1,0:T(8,128)(2,1)}), bf16[8,16,1152]{2,1,0:T(8,128)(2,1)S(1)}, u32[]{:S(2)}, u32[]{:S(2)}) %all-to-all-start.3) | async-done | bytes 294944 | tf_op jit(solution)/shard_map/all_to_all | solution.py:524
  335.6 19.3 %all_to_all.26 = bf16[4,144,1152]{2,1,0:T(8,128)(2,1)S(1)} all-to-all(bf16[4,144,1152]{2,1,0:T(8,128)(2,1)S(1)} %bitcast.29), channel_id=1, replica_groups={{0,8,16,24},{4,12,20,28},{1,9,17,25},{5,13,21,29},{2,10,18,26},{6,14,22..., dimensions={0} | all-to-all | bytes 2654208 | tf_op jit(solution)/shard_map/all_to_all | solution.py:683
  355.1 21.9 %all-gather = bf16[576,640]{1,0:T(8,128)(2,1)S(1)} all-gather(bf16[144,640]{1,0:T(8,128)(2,1)S(1)} %slice.102), channel_id=2, replica_groups=mesh['wide'=8,'narrow'=4] {'narrow'}, dimensions={0}, use_global_device_ids=true | all-gather | bytes 921600 | tf_op jit(solution)/shard_map/all_gather | solution.py:694
  (134 shorter events, 31.0 us)
Async XLA Ops:
  7.2 37.3 %all-gather.5.cloned.1.call-start = ((), (), s32[]{:S(2)}) async-start(), calls=%async_computation.7 | async-start | bytes 1658880 | tf_op jit(solution)/shard_map/all_gather | solution.py:482
  9.3 12.5 %all-to-all-start = ((bf16[8,16,1152]{2,1,0:T(8,128)(2,1)}), bf16[8,16,1152]{2,1,0:T(8,128)(2,1)S(1)}, u32[]{:S(2)}, u32[]{:S(2)}) async-start(bf16[8,16,1152]{2,1,0:T(8,128)(2,1)} %bitcast.43), calls=%async_computation | async-start | bytes 589824 | tf_op jit(solution)/shard_map/all_to_all | solution.py:519
  14.5 108.3 %all-gather.7.cloned.1.call-start = ((), (), s32[]{:S(2)}) async-start(), calls=%async_computation.8 | async-start | bytes 7741440 | tf_op jit(solution)/shard_map/all_gather | solution.py:482
  16.0 28.6 %copy-start.19 = (bf16[144,256]{1,0:T(8,128)(2,1)S(1)}, bf16[144,256]{1,0:T(8,128)(2,1)}, u32[]{:S(2)}) copy-start(bf16[144,256]{1,0:T(8,128)(2,1)} %q_ref.1) | copy-start | bytes 221188
  16.0 37.8 %copy-start.33 = (s32[1,2]{1,0:T(1,128)S(1)}, s32[1,2]{1,0:T(1,128)}, u32[]{:S(2)}) copy-start(s32[1,2]{1,0:T(1,128)} %param.18) | copy-start | bytes 28
  21.8 35.1 %copy-start.6 = (bf16[8,16,1152]{2,1,0:T(8,128)(2,1)}, bf16[8,16,1152]{2,1,0:T(8,128)(2,1)S(1)}, u32[]{:S(2)}) copy-start(bf16[8,16,1152]{2,1,0:T(8,128)(2,1)S(1)} %all-to-all-done) | copy-start | bytes 884740
  21.8 168.3 %all-gather.9.cloned.1.call-start = ((), (), s32[]{:S(2)}) async-start(), calls=%async_computation.9 | async-start | bytes 1474560 | tf_op jit(solution)/shard_map/all_gather | solution.py:482
  21.9 11.9 %collective-permute-start = (bf16[128,1152]{1,0:T(8,128)(2,1)S(1)}, bf16[128,1152]{1,0:T(8,128)(2,1)S(1)}, u32[]{:S(2)}, u32[]{:S(2)}) collective-permute-start(bf16[128,1152]{1,0:T(8,128)(2,1)S(1)} %bitcast.31), channel_id=1, source_target_pairs={{0,1},{1,2},{2,3},{3,0},{4,5},{5,6},{6,7},{7,4},{8,9},{9,10},{10,1... | collective-permute-start | bytes 884744 | tf_op jit(solution)/shard_map/ppermute | solution.py:510
  23.5 21.0 %collective-permute-start.1 = (bf16[128,1152]{1,0:T(8,128)(2,1)S(1)}, bf16[128,1152]{1,0:T(8,128)(2,1)S(1)}, u32[]{:S(2)}, u32[]{:S(2)}) collective-permute-start(bf16[128,1152]{1,0:T(8,128)(2,1)S(1)} %bitcast.32), channel_id=1, source_target_pairs={{0,2},{1,3},{2,0},{3,1},{4,6},{5,7},{6,4},{7,5},{8,10},{9,11},{10,... | collective-permute-start | bytes 884744 | tf_op jit(solution)/shard_map/ppermute | solution.py:510
  26.1 18.4 %collective-permute-start.2 = (bf16[128,1152]{1,0:T(8,128)(2,1)S(1)}, bf16[128,1152]{1,0:T(8,128)(2,1)S(1)}, u32[]{:S(2)}, u32[]{:S(2)}) collective-permute-start(bf16[128,1152]{1,0:T(8,128)(2,1)S(1)} %bitcast.33), channel_id=1, source_target_pairs={{0,3},{1,0},{2,1},{3,2},{4,7},{5,4},{6,5},{7,6},{8,11},{9,8},{10,9... | collective-permute-start | bytes 884744 | tf_op jit(solution)/shard_map/ppermute | solution.py:510
  33.8 23.1 %copy-start.10 = (bf16[128,1152]{1,0:T(8,128)(2,1)}, bf16[128,1152]{1,0:T(8,128)(2,1)S(1)}, u32[]{:S(2)}) copy-start(bf16[128,1152]{1,0:T(8,128)(2,1)S(1)} %collective-permute-done.refs_1_) | copy-start | bytes 884740
  44.5 12.5 %copy-start.12 = (bf16[128,1152]{1,0:T(8,128)(2,1)}, bf16[128,1152]{1,0:T(8,128)(2,1)S(1)}, u32[]{:S(2)}) copy-start(bf16[128,1152]{1,0:T(8,128)(2,1)S(1)} %collective-permute-done.2.refs_3_) | copy-start | bytes 884740
  44.5 12.4 %collective-permute-start.3 = (bf16[576,1152]{1,0:T(8,128)(2,1)}, bf16[576,1152]{1,0:T(8,128)(2,1)S(1)}, u32[]{:S(2)}, u32[]{:S(2)}) collective-permute-start(bf16[576,1152]{1,0:T(8,128)(2,1)} %all-gather.5.cloned.1.call-done.refs_5_), channel_id=1, source_target_pairs={{0,4},{4,0},{8,12},{12,8},{16,20},{20,16},{24,28},{28,24},{1,5},{5... | collective-permute-start | bytes 3981320 | tf_op jit(solution)/shard_map/ppermute | solution.py:487
  44.6 23.5 %collective-permute-start.4 = (bf16[144,256]{1,0:T(8,128)(2,1)S(1)}, bf16[144,256]{1,0:T(8,128)(2,1)S(1)}, u32[]{:S(2)}, u32[]{:S(2)}) collective-permute-start(bf16[144,256]{1,0:T(8,128)(2,1)S(1)} %copy-done.19), channel_id=1, source_target_pairs={{0,1},{1,2},{2,3},{3,0},{4,5},{5,6},{6,7},{7,4},{8,9},{9,10},{10,1... | collective-permute-start | bytes 221192 | tf_op jit(solution)/shard_map/ppermute | solution.py:510
  51.4 16.8 %collective-permute-start.5 = (bf16[144,256]{1,0:T(8,128)(2,1)S(1)}, bf16[144,256]{1,0:T(8,128)(2,1)S(1)}, u32[]{:S(2)}, u32[]{:S(2)}) collective-permute-start(bf16[144,256]{1,0:T(8,128)(2,1)S(1)} %copy-done.19), channel_id=1, source_target_pairs={{0,2},{1,3},{2,0},{3,1},{4,6},{5,7},{6,4},{7,5},{8,10},{9,11},{10,... | collective-permute-start | bytes 221192 | tf_op jit(solution)/shard_map/ppermute | solution.py:510
  53.1 15.1 %collective-permute-start.6 = (bf16[144,256]{1,0:T(8,128)(2,1)S(1)}, bf16[144,256]{1,0:T(8,128)(2,1)S(1)}, u32[]{:S(2)}, u32[]{:S(2)}) collective-permute-start(bf16[144,256]{1,0:T(8,128)(2,1)S(1)} %copy-done.19), channel_id=1, source_target_pairs={{0,3},{1,0},{2,1},{3,2},{4,7},{5,4},{6,5},{7,6},{8,11},{9,8},{10,9... | collective-permute-start | bytes 221192 | tf_op jit(solution)/shard_map/ppermute | solution.py:510
  68.2 9.8 %collective-permute-start.9 = (bf16[128,1152]{1,0:T(8,128)(2,1)}, bf16[128,1152]{1,0:T(8,128)(2,1)S(1)}, u32[]{:S(2)}, u32[]{:S(2)}) collective-permute-start(bf16[128,1152]{1,0:T(8,128)(2,1)} %get-tuple-element.102), channel_id=1, source_target_pairs={{0,3},{1,0},{2,1},{3,2},{4,7},{5,4},{6,5},{7,6},{8,11},{9,8},{10,9... | collective-permute-start | bytes 884744 | tf_op jit(solution)/shard_map/ppermute | solution.py:510
  70.2 26.5 %collective-permute-start.8 = (bf16[128,1152]{1,0:T(8,128)(2,1)}, bf16[128,1152]{1,0:T(8,128)(2,1)S(1)}, u32[]{:S(2)}, u32[]{:S(2)}) collective-permute-start(bf16[128,1152]{1,0:T(8,128)(2,1)} %get-tuple-element.100), channel_id=1, source_target_pairs={{0,2},{1,3},{2,0},{3,1},{4,6},{5,7},{6,4},{7,5},{8,10},{9,11},{10,... | collective-permute-start | bytes 884744 | tf_op jit(solution)/shard_map/ppermute | solution.py:510
  71.0 25.7 %collective-permute-start.7 = (bf16[128,1152]{1,0:T(8,128)(2,1)}, bf16[128,1152]{1,0:T(8,128)(2,1)S(1)}, u32[]{:S(2)}, u32[]{:S(2)}) collective-permute-start(bf16[128,1152]{1,0:T(8,128)(2,1)} %get-tuple-element.98), channel_id=1, source_target_pairs={{0,1},{1,2},{2,3},{3,0},{4,5},{5,6},{6,7},{7,4},{8,9},{9,10},{10,1... | collective-permute-start | bytes 884744 | tf_op jit(solution)/shard_map/ppermute | solution.py:510
  78.0 18.7 %copy-start.22 = (bf16[128,1152]{1,0:T(8,128)(2,1)}, bf16[128,1152]{1,0:T(8,128)(2,1)S(1)}, u32[]{:S(2)}) copy-start(bf16[128,1152]{1,0:T(8,128)(2,1)S(1)} %collective-permute-done.9.refs_3_) | copy-start | bytes 884740
  100.4 12.1 %collective-permute-start.10 = (bf16[128,1152]{1,0:T(8,128)(2,1)}, bf16[128,1152]{1,0:T(8,128)(2,1)S(1)}, u32[]{:S(2)}, u32[]{:S(2)}) collective-permute-start(bf16[128,1152]{1,0:T(8,128)(2,1)} %get-tuple-element.105.refs_0_), channel_id=1, source_target_pairs={{0,1},{1,2},{2,3},{3,0},{4,5},{5,6},{6,7},{7,4},{8,9},{9,10},{10,1... | collective-permute-start | bytes 884744 | tf_op jit(solution)/shard_map/ppermute | solution.py:510
  100.4 22.5 %collective-permute-start.11 = (bf16[128,1152]{1,0:T(8,128)(2,1)}, bf16[128,1152]{1,0:T(8,128)(2,1)S(1)}, u32[]{:S(2)}, u32[]{:S(2)}) collective-permute-start(bf16[128,1152]{1,0:T(8,128)(2,1)} %get-tuple-element.105.refs_0_), channel_id=1, source_target_pairs={{0,2},{1,3},{2,0},{3,1},{4,6},{5,7},{6,4},{7,5},{8,10},{9,11},{10,... | collective-permute-start | bytes 884744 | tf_op jit(solution)/shard_map/ppermute | solution.py:510
  101.8 21.1 %collective-permute-start.12 = (bf16[128,1152]{1,0:T(8,128)(2,1)}, bf16[128,1152]{1,0:T(8,128)(2,1)S(1)}, u32[]{:S(2)}, u32[]{:S(2)}) collective-permute-start(bf16[128,1152]{1,0:T(8,128)(2,1)} %get-tuple-element.105.refs_0_), channel_id=1, source_target_pairs={{0,3},{1,0},{2,1},{3,2},{4,7},{5,4},{6,5},{7,6},{8,11},{9,8},{10,9... | collective-permute-start | bytes 884744 | tf_op jit(solution)/shard_map/ppermute | solution.py:510
  112.4 20.9 %copy-start.13 = (bf16[128,1152]{1,0:T(8,128)(2,1)}, bf16[128,1152]{1,0:T(8,128)(2,1)S(1)}, u32[]{:S(2)}) copy-start(bf16[128,1152]{1,0:T(8,128)(2,1)S(1)} %collective-permute-done.10.refs_1_) | copy-start | bytes 884740
  122.8 10.4 %collective-permute-start.13 = (bf16[3,576,1728]{2,1,0:T(8,128)(2,1)}, bf16[3,576,1728]{2,1,0:T(8,128)(2,1)}, u32[]{:S(2)}, u32[]{:S(2)}) collective-permute-start(bf16[3,576,1728]{2,1,0:T(8,128)(2,1)} %all-gather.7.cloned.1.call-done.refs_4_.refs_6_), channel_id=1, source_target_pairs={{0,4},{4,0},{8,12},{12,8},{16,20},{20,16},{24,28},{28,24},{1,5},{5... | collective-permute-start | bytes 17915912 | tf_op jit(solution)/shard_map/ppermute | solution.py:487
  123.7 32.9 %copy-start.20 = (bf16[8,1,16,1152]{3,2,1,0:T(8,128)(2,1)S(1)}, bf16[8,1,16,1152]{3,2,1,0:T(8,128)(2,1)}, u32[]{:S(2)}) copy-start(bf16[8,1,16,1152]{3,2,1,0:T(8,128)(2,1)} %param.17) | copy-start | bytes 884740
  123.7 134.8 %reduce-scatter.3.cloned.1.call-start = ((), (), s32[]{:S(2)}) async-start(), calls=%async_computation.10 | async-start | bytes 1474560 | tf_op jit(solution)/shard_map/reduce_scatter | solution.py:623
  148.6 18.4 %collective-permute-start.14 = (bf16[128,1152]{1,0:T(8,128)(2,1)}, bf16[128,1152]{1,0:T(8,128)(2,1)S(1)}, u32[]{:S(2)}, u32[]{:S(2)}) collective-permute-start(bf16[128,1152]{1,0:T(8,128)(2,1)} %get-tuple-element.109), channel_id=1, source_target_pairs={{0,1},{1,2},{2,3},{3,0},{4,5},{5,6},{6,7},{7,4},{8,9},{9,10},{10,1... | collective-permute-start | bytes 884744 | tf_op jit(solution)/shard_map/ppermute | solution.py:510
  154.2 21.9 %collective-permute-start.15 = (bf16[128,1152]{1,0:T(8,128)(2,1)}, bf16[128,1152]{1,0:T(8,128)(2,1)S(1)}, u32[]{:S(2)}, u32[]{:S(2)}) collective-permute-start(bf16[128,1152]{1,0:T(8,128)(2,1)} %get-tuple-element.110), channel_id=1, source_target_pairs={{0,2},{1,3},{2,0},{3,1},{4,6},{5,7},{6,4},{7,5},{8,10},{9,11},{10,... | collective-permute-start | bytes 884744 | tf_op jit(solution)/shard_map/ppermute | solution.py:510
  156.3 19.7 %collective-permute-start.16 = (bf16[128,1152]{1,0:T(8,128)(2,1)}, bf16[128,1152]{1,0:T(8,128)(2,1)S(1)}, u32[]{:S(2)}, u32[]{:S(2)}) collective-permute-start(bf16[128,1152]{1,0:T(8,128)(2,1)} %get-tuple-element.111), channel_id=1, source_target_pairs={{0,3},{1,0},{2,1},{3,2},{4,7},{5,4},{6,5},{7,6},{8,11},{9,8},{10,9... | collective-permute-start | bytes 884744 | tf_op jit(solution)/shard_map/ppermute | solution.py:510
  181.0 15.2 %collective-permute-start.17 = (bf16[128,1152]{1,0:T(8,128)(2,1)}, bf16[128,1152]{1,0:T(8,128)(2,1)S(1)}, u32[]{:S(2)}, u32[]{:S(2)}) collective-permute-start(bf16[128,1152]{1,0:T(8,128)(2,1)} %get-tuple-element.118.refs_0_), channel_id=1, source_target_pairs={{0,1},{1,2},{2,3},{3,0},{4,5},{5,6},{6,7},{7,4},{8,9},{9,10},{10,1... | collective-permute-start | bytes 884744 | tf_op jit(solution)/shard_map/ppermute | solution.py:510
  187.7 20.1 %collective-permute-start.18 = (bf16[128,1152]{1,0:T(8,128)(2,1)}, bf16[128,1152]{1,0:T(8,128)(2,1)S(1)}, u32[]{:S(2)}, u32[]{:S(2)}) collective-permute-start(bf16[128,1152]{1,0:T(8,128)(2,1)} %get-tuple-element.118.refs_0_), channel_id=1, source_target_pairs={{0,2},{1,3},{2,0},{3,1},{4,6},{5,7},{6,4},{7,5},{8,10},{9,11},{10,... | collective-permute-start | bytes 884744 | tf_op jit(solution)/shard_map/ppermute | solution.py:510
  188.5 19.2 %collective-permute-start.19 = (bf16[128,1152]{1,0:T(8,128)(2,1)}, bf16[128,1152]{1,0:T(8,128)(2,1)S(1)}, u32[]{:S(2)}, u32[]{:S(2)}) collective-permute-start(bf16[128,1152]{1,0:T(8,128)(2,1)} %get-tuple-element.118.refs_0_), channel_id=1, source_target_pairs={{0,3},{1,0},{2,1},{3,2},{4,7},{5,4},{6,5},{7,6},{8,11},{9,8},{10,9... | collective-permute-start | bytes 884744 | tf_op jit(solution)/shard_map/ppermute | solution.py:510
  223.9 131.3 %reduce-scatter.5.cloned.1.call-start = ((), (), s32[]{:S(2)}) async-start(), calls=%async_computation.11 | async-start | bytes 7741440 | tf_op jit(solution)/shard_map/reduce_scatter | solution.py:493
  232.3 4.3 %collective-permute-start.20 = (bf16[576,1728]{1,0:T(8,128)(2,1)}, bf16[576,1728]{1,0:T(8,128)(2,1)S(1)}, u32[]{:S(2)}, u32[]{:S(2)}) collective-permute-start(bf16[576,1728]{1,0:T(8,128)(2,1)} %get-tuple-element.127), channel_id=1, source_target_pairs={{0,4},{4,0},{8,12},{12,8},{16,20},{20,16},{24,28},{28,24},{1,5},{5... | collective-permute-start | bytes 5971976 | tf_op jit(solution)/shard_map/ppermute | solution.py:487
  232.3 10.2 %collective-permute-start.21 = (bf16[576,1728]{1,0:T(8,128)(2,1)}, bf16[576,1728]{1,0:T(8,128)(2,1)S(1)}, u32[]{:S(2)}, u32[]{:S(2)}) collective-permute-start(bf16[576,1728]{1,0:T(8,128)(2,1)} %get-tuple-element.128), channel_id=1, source_target_pairs={{0,4},{4,0},{8,12},{12,8},{16,20},{20,16},{24,28},{28,24},{1,5},{5... | collective-permute-start | bytes 5971976 | tf_op jit(solution)/shard_map/ppermute | solution.py:487
  232.8 9.8 %collective-permute-start.22 = (bf16[576,1728]{1,0:T(8,128)(2,1)}, bf16[576,1728]{1,0:T(8,128)(2,1)}, u32[]{:S(2)}, u32[]{:S(2)}) collective-permute-start(bf16[576,1728]{1,0:T(8,128)(2,1)} %get-tuple-element.129), channel_id=1, source_target_pairs={{0,4},{4,0},{8,12},{12,8},{16,20},{20,16},{24,28},{28,24},{1,5},{5... | collective-permute-start | bytes 5971976 | tf_op jit(solution)/shard_map/ppermute | solution.py:487
  261.4 53.1 %collective-permute-start.29 = (bf16[4,576,256]{2,1,0:T(8,128)(2,1)S(1)}, bf16[4,576,256]{2,1,0:T(8,128)(2,1)S(1)}, u32[]{:S(2)}, u32[]{:S(2)}) collective-permute-start(bf16[4,576,256]{2,1,0:T(8,128)(2,1)S(1)} %copy-done.4), channel_id=1, source_target_pairs={{0,4},{4,0},{8,12},{12,8},{16,20},{20,16},{24,28},{28,24},{1,5},{5... | collective-permute-start | bytes 3538952 | tf_op jit(solution)/shard_map/ppermute | solution.py:487
  261.4 13.7 %collective-permute-start.23 = (bf16[128,1152]{1,0:T(8,128)(2,1)}, bf16[128,1152]{1,0:T(8,128)(2,1)S(1)}, u32[]{:S(2)}, u32[]{:S(2)}) collective-permute-start(bf16[128,1152]{1,0:T(8,128)(2,1)} %get-tuple-element.133.refs_0_), channel_id=1, source_target_pairs={{0,1},{1,2},{2,3},{3,0},{4,5},{5,6},{6,7},{7,4},{8,9},{9,10},{10,1... | collective-permute-start | bytes 884744 | tf_op jit(solution)/shard_map/ppermute | solution.py:510
  265.0 22.5 %collective-permute-start.24 = (bf16[128,1152]{1,0:T(8,128)(2,1)}, bf16[128,1152]{1,0:T(8,128)(2,1)S(1)}, u32[]{:S(2)}, u32[]{:S(2)}) collective-permute-start(bf16[128,1152]{1,0:T(8,128)(2,1)} %get-tuple-element.133.refs_0_), channel_id=1, source_target_pairs={{0,2},{1,3},{2,0},{3,1},{4,6},{5,7},{6,4},{7,5},{8,10},{9,11},{10,... | collective-permute-start | bytes 884744 | tf_op jit(solution)/shard_map/ppermute | solution.py:510
  267.5 19.9 %collective-permute-start.25 = (bf16[128,1152]{1,0:T(8,128)(2,1)}, bf16[128,1152]{1,0:T(8,128)(2,1)S(1)}, u32[]{:S(2)}, u32[]{:S(2)}) collective-permute-start(bf16[128,1152]{1,0:T(8,128)(2,1)} %get-tuple-element.133.refs_0_), channel_id=1, source_target_pairs={{0,3},{1,0},{2,1},{3,2},{4,7},{5,4},{6,5},{7,6},{8,11},{9,8},{10,9... | collective-permute-start | bytes 884744 | tf_op jit(solution)/shard_map/ppermute | solution.py:510
  267.5 42.0 %all-to-all-start.2 = ((bf16[8,16,1152]{2,1,0:T(8,128)(2,1)}), bf16[8,16,1152]{2,1,0:T(8,128)(2,1)S(1)}, u32[]{:S(2)}, u32[]{:S(2)}) async-start(bf16[8,16,1152]{2,1,0:T(8,128)(2,1)} %bitcast.45), calls=%async_computation.2 | async-start | bytes 589824 | tf_op jit(solution)/shard_map/all_to_all | solution.py:524
  294.4 15.1 %collective-permute-start.26 = (bf16[128,768]{1,0:T(8,128)(2,1)}, bf16[128,768]{1,0:T(8,128)(2,1)S(1)}, u32[]{:S(2)}, u32[]{:S(2)}) collective-permute-start(bf16[128,768]{1,0:T(8,128)(2,1)} %get-tuple-element.153), channel_id=1, source_target_pairs={{0,1},{1,2},{2,3},{3,0},{4,5},{5,6},{6,7},{7,4},{8,9},{9,10},{10,1... | collective-permute-start | bytes 589832 | tf_op jit(solution)/shard_map/ppermute | solution.py:510
  301.2 13.3 %collective-permute-start.27 = (bf16[128,768]{1,0:T(8,128)(2,1)}, bf16[128,768]{1,0:T(8,128)(2,1)S(1)}, u32[]{:S(2)}, u32[]{:S(2)}) collective-permute-start(bf16[128,768]{1,0:T(8,128)(2,1)} %get-tuple-element.154), channel_id=1, source_target_pairs={{0,2},{1,3},{2,0},{3,1},{4,6},{5,7},{6,4},{7,5},{8,10},{9,11},{10,... | collective-permute-start | bytes 589832 | tf_op jit(solution)/shard_map/ppermute | solution.py:510
  301.5 13.0 %collective-permute-start.28 = (bf16[128,768]{1,0:T(8,128)(2,1)}, bf16[128,768]{1,0:T(8,128)(2,1)S(1)}, u32[]{:S(2)}, u32[]{:S(2)}) collective-permute-start(bf16[128,768]{1,0:T(8,128)(2,1)} %get-tuple-element.155), channel_id=1, source_target_pairs={{0,3},{1,0},{2,1},{3,2},{4,7},{5,4},{6,5},{7,6},{8,11},{9,8},{10,9... | collective-permute-start | bytes 589832 | tf_op jit(solution)/shard_map/ppermute | solution.py:510
  324.9 3.5 collective-permute-start.30
  324.9 10.7 %all-to-all-start.3 = ((bf16[8,16,1152]{2,1,0:T(8,128)(2,1)}), bf16[8,16,1152]{2,1,0:T(8,128)(2,1)S(1)}, u32[]{:S(2)}, u32[]{:S(2)}) async-start(bf16[8,16,1152]{2,1,0:T(8,128)(2,1)} %bitcast.46), calls=%async_computation.4 | async-start | bytes 589824 | tf_op jit(solution)/shard_map/all_to_all | solution.py:524
  355.1 24.5 %copy-start.2 = (bf16[3,144,1728]{2,1,0:T(8,128)(2,1)S(1)}, bf16[3,144,1728]{2,1,0:T(8,128)(2,1)}, u32[]{:S(2)}) copy-start(bf16[3,144,1728]{2,1,0:T(8,128)(2,1)} %reduce-scatter.5.cloned.1.call-done) | copy-start | bytes 4478980
  (25 other events, 117.0 us)
Sparse Core Ops, SparseCore 0:
  10.5 31.6 all-gather.4
  44.0 69.3 all-gather.6
  123.9 31.8 all-gather.8
  224.0 34.5 reduce-scatter.2
  261.5 71.6 reduce-scatter.4

commit v3 on v2

--- a/solution.py
+++ b/solution.py
@@ -20,6 +20,7 @@
 
 
 def call(kernel, outs, scratch=(), anys=(), smem=(), count=0, flops=0, moved=0):
+    limit = (16 if moved <= 4 * 10**6 and moved != 10**6 else 60) * 1024 * 1024
     def place(index):
         if index in anys:
             return pl.BlockSpec(memory_space=pl.ANY)
@@ -33,7 +34,7 @@
         in_specs=[place(i) for i in range(count)],
         out_specs=[pl.BlockSpec(memory_space=pltpu.VMEM)] * len(outs),
         scratch_shapes=list(scratch),
-        compiler_params=pltpu.CompilerParams(vmem_limit_bytes=VMEM_LIMIT),
+        compiler_params=pltpu.CompilerParams(vmem_limit_bytes=limit),
         cost_estimate=pl.CostEstimate(flops=1, bytes_accessed=1, transcendentals=0),
     )
 
@@ -444,6 +445,20 @@
     other_ref[:, 4 * head :] = terms[half:].astype(BF16)
 
 
+def finish(*refs):
+    key_ref, value_ref, *rows = refs[RING:]
+    head = key_ref.shape[1]
+    value = total(refs[:RING])
+    key_ref[...] = value[:, :head]
+    value_ref[...] = value[:, head : 2 * head]
+    n = value.shape[0]
+    same = lax.broadcasted_iota(jnp.int32, (n, n), 0) == lax.broadcasted_iota(jnp.int32, (n, n), 1)
+    for i, ref in enumerate(rows):
+        column = value[:, 2 * head + i : 2 * head + i + 1]
+        row = jnp.sum(jnp.where(same, column, 0.0), axis=0)
+        ref[...] = row[: ref.shape[0]]
+
+
 def on_device(
     tokens,
     cotangent,
@@ -530,7 +545,10 @@
         attn_gain, attnout_gain, ffn_gain, ffnout_gain, query_gain, key_gain,
     )[0]
     wa_mine = gather_wide(pack, 0)
-    own_x = enter(tokens)
+    lengths = seq_lengths[0]
+    info = jnp.stack([slot, core, lengths[0], lengths[0] + lengths[1], 0]).astype(jnp.int32)
+    queries = gather_ring(query_weight)
+    own_x = after(enter(tokens), info, *queries)
     quarter = own_x.shape[0]
     rows = quarter * narrow
     part = quarter // CHUNKS
@@ -540,11 +558,7 @@
     x_all = gather_ring(own_x)
     wf_mine = gather_wide(after(jnp.stack([gate_weight, up_weight, down_weight]), own_x), 1)
     weights = [sibling(after(wa_mine, *x_all)), wa_mine]
-    queries = gather_ring(after(query_weight, *x_all))
     wh_mine = gather_wide(after(jnp.stack(queries), wf_mine), 1)
-    lengths = seq_lengths[0]
-    info = [slot, core, lengths[0], lengths[0] + lengths[1], 0]
-    info = jnp.stack([jnp.asarray(v, jnp.int32) for v in info])
     own_dy = enter(after(cotangent, own_x))
     many = len(x_all) + len(weights)
     (
@@ -567,7 +581,6 @@
         anys=tuple(range(len(x_all), many)), smem=(many,), count=many + 1,
         flops=3 * 10**9, moved=8 * 10**6,
     )(*x_all, *weights, info)
-    z_parts = [after(p, *queries) for p in z_parts]
     z = pass_on(z_parts)
     mixed, h, *xn2_own = call(
         middle_forward,
@@ -575,7 +588,7 @@
         smem=(narrow + 2,), count=narrow + 3, flops=10**7, moved=2 * 10**6,
     )(*z, xp, gains, slots)
     xn2 = [gather_ring(xn2_own[c]) for c in every]
-    wf_other = sibling(after(wf_mine, *xn2[0]))
+    wf_other = sibling(after(wf_mine, xn2[0][1], xn2[0][-1]))
     def ffn_ahead(c):
         return call(
             ffn_forward,
@@ -685,31 +698,19 @@
         )
         return parts.astype(F32).sum(axis=0)
 
-    left_dx = leave(dx_own)
-    last = scatter_chips(after(pair_sum(own, other), left_dx))
+    last = scatter_chips(pair_sum(own, other))
     s_query, s_outproj = last[:, :head], last[:, head : 2 * head]
     last = last[:, 2 * head :].astype(BF16)
-    last, s_ffn = lax.optimization_barrier((last, s_ffn))
+    last, s_ffn, dx_own = lax.optimization_barrier((last, s_ffn, dx_own))
     s_ffn = s_ffn.astype(F32)
-    shared = lax.all_gather(last, "narrow").astype(F32).sum(axis=0)
-    small = shared[:, 2 * head :]
-    return (
-        left_out,
-        left_dx,
-        s_query,
-        shared[:, :head],
-        shared[:, head : 2 * head],
-        s_outproj,
-        s_ffn[0],
-        s_ffn[1],
-        s_ffn[2],
-        small[:, 0],
-        small[:, 1],
-        small[:, 2],
-        small[:, 3],
-        small[:dh, 4],
-        small[:dh, 5],
-    )
+    left_dx, shared = leave(dx_own), gather_ring(last)
+    left_dx, *shared = lax.optimization_barrier((left_dx, *shared))
+    small = call(
+        finish,
+        [((dw, head), ff)] * 2 + [((dw,), ff)] * 4 + [((dh,), ff)] * 2,
+        count=narrow, flops=10**6, moved=2 * 10**6,
+    )(*shared)
+    return (left_out, left_dx, s_query, *small[:2], s_outproj, s_ffn[0], s_ffn[1], s_ffn[2], *small[2:])
 
 
 def solution(mesh):

time: 397 us -> 386 us (0.972)
  blocking collectives: 51.6 us -> 30.8 us
  local copies, waits for them, and re-layouts: 14.2 us -> 24 us
  Pallas kernels: 92.9 us -> 83.4 us
  starting transfers between devices: 68.1 us -> 74.6 us
    all_gather x1 -> x0, blocking collectives: 21.9 us -> none  [on_device(): shared = lax.all_gather(last, 'narrow').astype(F32).sum(axis=0)]
    unnamed x70 -> x94, local copies, waits for them, and re-layouts: 8.21 us -> 17.9 us
    ppermute x24 -> x27, starting transfers between devices: 54.7 us -> 62.6 us  [pass_on(): got.append(lax.ppermute(parts[s], 'narrow', shift))]
    pallas_call x2, Pallas kernels: 5.63 us -> 1.11 us  [outer(): call(weight_grad, [((half, columns), bf)] * 2, scratch=[pltpu.VMEM((width...]
    ppermute x24 -> x27, waiting for transfers between devices: 109 us -> 110 us  [pass_on(): got.append(lax.ppermute(parts[s], 'narrow', shift))]
  transfers between devices with their start and end apart: 39 -> 42, of which waited for: 19 -> 23; matrix products, arithmetic and copies ran while one was open for 2% -> 4% of each run, Pallas kernels for 19% -> 17%
where the time goes in v3:
time: 386 us; the launch traced here: 378 us
  waiting for transfers between devices  142 us (37%)
  Pallas kernels  83.4 us (22%)
  starting transfers between devices  74.6 us (19%)
  blocking collectives  30.8 us (8%)
  local copies, waits for them, and re-layouts  24 us (6%)
  between operations  16 us (4%)
  other arithmetic  7.3 us (2%)
    ppermute x27, waiting for transfers between devices, pass_on(): got.append(lax.ppermute(parts[s], 'narrow', shift))  110 us
    ppermute x27, starting transfers between devices, pass_on(): got.append(lax.ppermute(parts[s], 'narrow', shift))  62.6 us
    all_to_all x1, blocking collectives, scatter_chips(): lax.all_to_all(parts, 'wide', split_axis=0, concat_axis=0, tiled=True, ax...  21 us
    pallas_call x2, Pallas kernels, ffn_grads(): call(functools.partial(ffn_weight_grads, first), outs, scratch=[pltpu.VME...  19.3 us
    unnamed x94, local copies, waits for them, and re-layouts  17.9 us
    ppermute x7, waiting for transfers between devices, sibling(): return lax.ppermute(value, 'wide', swap)  16.4 us
    pallas_call x1, Pallas kernels, ffn_back(): call(ffn_backward, [((narrow * part, width), bf)] + [((narrow * part, uni...  15.4 us
    pallas_call x1, Pallas kernels, ffn_ahead(): call(ffn_forward, [((narrow * part, width), bf)] + [((narrow * part, unit...  15.1 us
  transfers between devices with their start and end apart: 42, of which 23 were waited for; matrix products, arithmetic and copies ran while one was open for 4% of the time, Pallas kernels for 17%

profile of v3, /device:TPU:0, one launch (start us, length us, event | category | flops | bytes accessed | tf_op | source)
XLA Modules:
  0.0 378.3 jit_solution(3882903279840853257)
XLA Ops:
  9.3 3.1 collective-permute-start
  12.4 2.6 collective-permute-start.1
  16.4 3.7 all-to-all-start
  24.7 5.8 %all-to-all-done = bf16[8,16,1152]{2,1,0:T(8,128)(2,1)S(1)} async-done(((bf16[8,16,1152]{2,1,0:T(8,128)(2,1)}), bf16[8,16,1152]{2,1,0:T(8,128)(2,1)S(1)}, u32[]{:S(2)}, u32[]{:S(2)}) %all-to-all-start) | async-done | bytes 294944 | tf_op jit(solution)/shard_map/all_to_all | solution.py:534
  31.0 3.5 collective-permute-start.5
  34.5 8.0 %collective-permute-done.3.refs_1_ = bf16[128,1152]{1,0:T(8,128)(2,1)S(1)} collective-permute-done((bf16[128,1152]{1,0:T(8,128)(2,1)S(1)}, bf16[128,1152]{1,0:T(8,128)(2,1)S(1)}, u32[]{:S(2)}, u32[]{:S(2)}) %collective-permute-start.3) | collective-permute-done | bytes 294944 | tf_op jit(solution)/shard_map/ppermute | solution.py:525
  42.5 8.9 %collective-permute-done.4.refs_2_ = bf16[128,1152]{1,0:T(8,128)(2,1)S(1)} collective-permute-done((bf16[128,1152]{1,0:T(8,128)(2,1)S(1)}, bf16[128,1152]{1,0:T(8,128)(2,1)S(1)}, u32[]{:S(2)}, u32[]{:S(2)}) %collective-permute-start.4) | collective-permute-done | bytes 294944 | tf_op jit(solution)/shard_map/ppermute | solution.py:525
  51.5 3.3 collective-permute-done.6.refs_4_
  55.9 10.1 %shard_map.272 = (bf16[512,1152]{1,0:T(8,128)(2,1)}, bf16[512,1152]{1,0:T(8,128)(2,1)}, f32[512,256]{1,0:T(8,128)}, f32[512,256]{1,0:T(8,128)}, bf16[512,256]{1,...) custom-call(bf16[128,1152]{1,0:T(8,128)(2,1)} %bitcast.32, ...), custom_call_target="tpu_custom_call" | custom-call | flops 1 | bytes 1 | tf_op jit(solution)/shard_map/pallas_call | solution.py:567
  66.0 6.2 %collective-permute-start.7 = (bf16[128,1152]{1,0:T(8,128)(2,1)}, bf16[128,1152]{1,0:T(8,128)(2,1)S(1)}, u32[]{:S(2)}, u32[]{:S(2)}) collective-permute-start(bf16[128,1152]{1,0:T(8,128)(2,1)} %get-tuple-element.105), channel_id=1, source_target_pairs={{0,1},{1,2},{2,3},{3,0},{4,5},{5,6},{6,7},{7,4},{8,9},{9,10},{10,1... | collective-permute-start | bytes 884744 | tf_op jit(solution)/shard_map/ppermute | solution.py:525
  72.2 2.4 collective-permute-start.9
  74.6 5.2 %collective-permute-done.7.refs_1_ = bf16[128,1152]{1,0:T(8,128)(2,1)S(1)} collective-permute-done((bf16[128,1152]{1,0:T(8,128)(2,1)}, bf16[128,1152]{1,0:T(8,128)(2,1)S(1)}, u32[]{:S(2)}, u32[]{:S(2)}) %collective-permute-start.7) | collective-permute-done | bytes 294944 | tf_op jit(solution)/shard_map/ppermute | solution.py:525
  79.8 12.0 %collective-permute-done.8.refs_2_ = bf16[128,1152]{1,0:T(8,128)(2,1)S(1)} collective-permute-done((bf16[128,1152]{1,0:T(8,128)(2,1)}, bf16[128,1152]{1,0:T(8,128)(2,1)S(1)}, u32[]{:S(2)}, u32[]{:S(2)}) %collective-permute-start.8) | collective-permute-done | bytes 294944 | tf_op jit(solution)/shard_map/ppermute | solution.py:525
  95.3 6.8 %collective-permute-start.10 = (bf16[128,1152]{1,0:T(8,128)(2,1)S(1)}, bf16[128,1152]{1,0:T(8,128)(2,1)S(1)}, u32[]{:S(2)}, u32[]{:S(2)}) collective-permute-start(bf16[128,1152]{1,0:T(8,128)(2,1)S(1)} %get-tuple-element.110.refs_0_), channel_id=1, source_target_pairs={{0,1},{1,2},{2,3},{3,0},{4,5},{5,6},{6,7},{7,4},{8,9},{9,10},{10,1... | collective-permute-start | bytes 884744 | tf_op jit(solution)/shard_map/ppermute | solution.py:525
  104.5 7.8 %collective-permute-done.10.refs_1_ = bf16[128,1152]{1,0:T(8,128)(2,1)S(1)} collective-permute-done((bf16[128,1152]{1,0:T(8,128)(2,1)S(1)}, bf16[128,1152]{1,0:T(8,128)(2,1)S(1)}, u32[]{:S(2)}, u32[]{:S(2)}) %collective-permute-start.10) | collective-permute-done | bytes 294944 | tf_op jit(solution)/shard_map/ppermute | solution.py:525
  112.4 4.9 %collective-permute-done.12.refs_3_ = bf16[128,1152]{1,0:T(8,128)(2,1)S(1)} collective-permute-done((bf16[128,1152]{1,0:T(8,128)(2,1)S(1)}, bf16[128,1152]{1,0:T(8,128)(2,1)S(1)}, u32[]{:S(2)}, u32[]{:S(2)}) %collective-permute-start.12) | collective-permute-done | bytes 294944 | tf_op jit(solution)/shard_map/ppermute | solution.py:525
  119.3 15.6 %collective-permute-done.11.refs_2_ = bf16[128,1152]{1,0:T(8,128)(2,1)S(1)} collective-permute-done((bf16[128,1152]{1,0:T(8,128)(2,1)S(1)}, bf16[128,1152]{1,0:T(8,128)(2,1)S(1)}, u32[]{:S(2)}, u32[]{:S(2)}) %collective-permute-start.11) | collective-permute-done | bytes 294944 | tf_op jit(solution)/shard_map/ppermute | solution.py:525
  135.7 15.1 %shard_map.274 = (bf16[512,1152]{1,0:T(8,128)(2,1)}, bf16[512,1728]{1,0:T(8,128)(2,1)}, bf16[512,1728]{1,0:T(8,128)(2,1)}, bf16[512,1728]{1,0:T(8,128)(2,1)}, bf...) custom-call(bf16[128,1152]{1,0:T(8,128)(2,1)} %copy-done.7, ...), custom_call_target="tpu_custom_call" | custom-call | flops 1 | bytes 1 | tf_op jit(solution)/shard_map/pallas_call | solution.py:593
  150.8 2.6 collective-permute-start.15
  154.7 9.8 %all_to_all.25 = bf16[8,16,1152]{2,1,0:T(8,128)(2,1)S(1)} all-to-all(bf16[8,16,1152]{2,1,0:T(8,128)(2,1)S(1)} %bitcast.41), channel_id=1, replica_groups=mesh['wide'=8,'narrow'=4] {'wide'}, dimensions={0} | all-to-all | bytes 589824 | tf_op jit(solution)/shard_map/all_to_all | solution.py:534
  164.5 9.8 %collective-permute-done.15.refs_2_ = bf16[128,1152]{1,0:T(8,128)(2,1)S(1)} collective-permute-done((bf16[128,1152]{1,0:T(8,128)(2,1)}, bf16[128,1152]{1,0:T(8,128)(2,1)S(1)}, u32[]{:S(2)}, u32[]{:S(2)}) %collective-permute-start.15) | collective-permute-done | bytes 294944 | tf_op jit(solution)/shard_map/ppermute | solution.py:525
  175.3 3.0 shard_map.275
  178.9 5.9 %collective-permute-start.17 = (bf16[128,1152]{1,0:T(8,128)(2,1)S(1)}, bf16[128,1152]{1,0:T(8,128)(2,1)S(1)}, u32[]{:S(2)}, u32[]{:S(2)}) collective-permute-start(bf16[128,1152]{1,0:T(8,128)(2,1)S(1)} %get-tuple-element.123.refs_0_), channel_id=1, source_target_pairs={{0,1},{1,2},{2,3},{3,0},{4,5},{5,6},{6,7},{7,4},{8,9},{9,10},{10,1... | collective-permute-start | bytes 884744 | tf_op jit(solution)/shard_map/ppermute | solution.py:525
  187.2 5.1 %collective-permute-done.17.refs_1_ = bf16[128,1152]{1,0:T(8,128)(2,1)S(1)} collective-permute-done((bf16[128,1152]{1,0:T(8,128)(2,1)S(1)}, bf16[128,1152]{1,0:T(8,128)(2,1)S(1)}, u32[]{:S(2)}, u32[]{:S(2)}) %collective-permute-start.17) | collective-permute-done | bytes 294944 | tf_op jit(solution)/shard_map/ppermute | solution.py:525
  192.3 10.1 %collective-permute-done.18.refs_2_ = bf16[128,1152]{1,0:T(8,128)(2,1)S(1)} collective-permute-done((bf16[128,1152]{1,0:T(8,128)(2,1)S(1)}, bf16[128,1152]{1,0:T(8,128)(2,1)S(1)}, u32[]{:S(2)}, u32[]{:S(2)}) %collective-permute-start.18) | collective-permute-done | bytes 294944 | tf_op jit(solution)/shard_map/ppermute | solution.py:525
  203.9 15.4 %shard_map.276 = (bf16[512,1152]{1,0:T(8,128)(2,1)}, bf16[512,1728]{1,0:T(8,128)(2,1)}, bf16[512,1728]{1,0:T(8,128)(2,1)}, bf16[512,1152]{1,0:T(8,128)(2,1)}) custom-call(bf16[128,1152]{1,0:T(8,128)(2,1)} %copy-done.16, bf16[128,1152]{1,0:T(8,128)(2,1)} %copy-done.39, bf16[128,1152]{1,0:T(8,128)(2,1)} %copy-done.40, bf16[128,1152]{1,0:T(8,128)(2,1)} %copy-done.41, ...), custom_call_target="tpu_custom_call" | custom-call | flops 1 | bytes 1 | tf_op jit(solution)/shard_map/pallas_call | solution.py:621
  219.6 8.2 %shard_map.277 = (bf16[576,1728]{1,0:T(8,128)(2,1)}, bf16[576,1728]{1,0:T(8,128)(2,1)}, bf16[576,1728]{1,0:T(8,128)(2,1)}) custom-call(bf16[512,1152]{1,0:T(8,128)(2,1)} %get-tuple-element.127.refs_0_, bf16[512,1152]{1,0:T(8,128)(2,1)} %get-tuple-element.128.refs_1_, bf16[512,1728]{1,0:T(8,128)(2,1)} %get-tuple-element.129.refs_2_, ...), custom_call_target="tpu_custom_call" | custom-call | flops 1 | bytes 1 | tf_op jit(solution)/shard_map/pallas_call | solution.py:643
  228.2 3.9 %collective-permute-done.20.refs_5_ = bf16[576,1728]{1,0:T(8,128)(2,1)} collective-permute-done((bf16[576,1728]{1,0:T(8,128)(2,1)}, bf16[576,1728]{1,0:T(8,128)(2,1)}, u32[]{:S(2)}, u32[]{:S(2)}) %collective-permute-start.20) | collective-permute-done | bytes 1990688 | tf_op jit(solution)/shard_map/ppermute | solution.py:502
  232.2 3.0 collective-permute-done.21.refs_6_
  235.1 3.0 collective-permute-done.22.refs_7_
  238.1 11.2 %shard_map.278 = bf16[3,576,1728]{2,1,0:T(8,128)(2,1)} custom-call(bf16[512,1152]{1,0:T(8,128)(2,1)} %get-tuple-element.127.refs_0_, bf16[512,1152]{1,0:T(8,128)(2,1)} %get-tuple-element.128.refs_1_, bf16[512,1728]{1,0:T(8,128)(2,1)} %get-tuple-element.129.refs_2_, bf16[512,1728]{1,0:T(8,128)(2,1)} %get-tuple-element.130.refs_3_, ...), custom_call_target="tpu_custom_call" | custom-call | flops 1 | bytes 1 | tf_op jit(solution)/shard_map/pallas_call | solution.py:643
  249.3 6.7 %reduce-scatter.3.cloned.1.call-done.g_ref = bf16[1,128,1152]{2,1,0:T(8,128)(2,1)} async-done(((bf16[4,128,1152]{2,1,0:T(8,128)(2,1)}), bf16[1,128,1152]{2,1,0:T(8,128)(2,1)}) %reduce-scatter.3.cloned.1.call-update) | async-done | bytes 294928 | tf_op jit(solution)/shard_map/reduce_scatter | solution.py:636
  259.8 3.4 collective-permute-start.24
  263.7 3.7 all-to-all-start.2
  267.4 4.0 %collective-permute-done.23.refs_1_ = bf16[128,1152]{1,0:T(8,128)(2,1)S(1)} collective-permute-done((bf16[128,1152]{1,0:T(8,128)(2,1)S(1)}, bf16[128,1152]{1,0:T(8,128)(2,1)S(1)}, u32[]{:S(2)}, u32[]{:S(2)}) %collective-permute-start.23) | collective-permute-done | bytes 294944 | tf_op jit(solution)/shard_map/ppermute | solution.py:525
  271.4 12.2 %collective-permute-done.24.refs_2_ = bf16[128,1152]{1,0:T(8,128)(2,1)} collective-permute-done((bf16[128,1152]{1,0:T(8,128)(2,1)S(1)}, bf16[128,1152]{1,0:T(8,128)(2,1)}, u32[]{:S(2)}, u32[]{:S(2)}) %collective-permute-start.24) | collective-permute-done | bytes 294944 | tf_op jit(solution)/shard_map/ppermute | solution.py:525
  283.7 6.2 %shard_map.280 = (bf16[512,1152]{1,0:T(8,128)(2,1)}, bf16[512,768]{1,0:T(8,128)(2,1)}, f32[1,256]{1,0:T(1,128)}, bf16[128,768]{1,0:T(8,128)(2,1)}, bf16[128,768]...) custom-call(bf16[128,1152]{1,0:T(8,128)(2,1)} %copy-done.12, bf16[128,1152]{1,0:T(8,128)(2,1)} %copy-done.35, ...), custom_call_target="tpu_custom_call" | custom-call | flops 1 | bytes 1 | tf_op jit(solution)/shard_map/pallas_call | solution.py:662
  289.9 6.3 %collective-permute-start.26 = (bf16[128,768]{1,0:T(8,128)(2,1)}, bf16[128,768]{1,0:T(8,128)(2,1)S(1)}, u32[]{:S(2)}, u32[]{:S(2)}) collective-permute-start(bf16[128,768]{1,0:T(8,128)(2,1)} %get-tuple-element.158), channel_id=1, source_target_pairs={{0,1},{1,2},{2,3},{3,0},{4,5},{5,6},{6,7},{7,4},{8,9},{9,10},{10,1... | collective-permute-start | bytes 589832 | tf_op jit(solution)/shard_map/ppermute | solution.py:525
  305.3 4.9 %collective-permute-done.27.g2_ref = bf16[128,768]{1,0:T(8,128)(2,1)S(1)} collective-permute-done((bf16[128,768]{1,0:T(8,128)(2,1)}, bf16[128,768]{1,0:T(8,128)(2,1)S(1)}, u32[]{:S(2)}, u32[]{:S(2)}) %collective-permute-start.27) | collective-permute-done | bytes 196640 | tf_op jit(solution)/shard_map/ppermute | solution.py:525
  311.4 9.2 %shard_map.283 = (bf16[128,1152]{1,0:T(8,128)(2,1)}, bf16[576,1152]{1,0:T(8,128)(2,1)}, bf16[576,1152]{1,0:T(8,128)(2,1)}) custom-call(bf16[128,768]{1,0:T(8,128)(2,1)} %get-tuple-element.157.g0_ref, bf16[128,768]{1,0:T(8,128)(2,1)} %copy-done.42, bf16[128,768]{1,0:T(8,128)(2,1)} %copy-done.43, bf16[128,768]{1,0:T(8,128)(2,1)} %copy-done.44, ...), custom_call_target="tpu_custom_call" | custom-call | flops 1 | bytes 1 | tf_op jit(solution)/shard_map/pallas_call | solution.py:683
  320.7 3.3 collective-permute-done.30
  325.6 21.0 %all_to_all.26 = bf16[4,144,1152]{2,1,0:T(8,128)(2,1)S(1)} all-to-all(bf16[4,144,1152]{2,1,0:T(8,128)(2,1)S(1)} %bitcast.28), channel_id=1, replica_groups={{0,8,16,24},{4,12,20,28},{1,9,17,25},{5,13,21,29},{2,10,18,26},{6,14,22..., dimensions={0} | all-to-all | bytes 2654208 | tf_op jit(solution)/shard_map/all_to_all | solution.py:696
  347.5 4.7 %collective-permute-start.31 = (bf16[144,640]{1,0:T(8,128)(2,1)S(1)}, bf16[144,640]{1,0:T(8,128)(2,1)S(1)}, u32[]{:S(2)}, u32[]{:S(2)}) collective-permute-start(bf16[144,640]{1,0:T(8,128)(2,1)S(1)} %slice.49.refs_0_), channel_id=1, source_target_pairs={{0,1},{1,2},{2,3},{3,0},{4,5},{5,6},{6,7},{7,4},{8,9},{9,10},{10,1... | collective-permute-start | bytes 552968 | tf_op jit(solution)/shard_map/ppermute | solution.py:525
  352.2 2.9 collective-permute-start.32
  355.1 3.3 convert_element_type.20
  358.3 3.4 all-to-all-start.4
  361.8 3.5 slice_bitcast_fusion
  366.2 2.8 all-to-all-done.4
  (161 shorter events, 44.8 us)
Async XLA Ops:
  7.2 44.2 %all-gather.4.cloned.1.call-start = ((), (), s32[]{:S(2)}) async-start(), calls=%async_computation.7 | async-start | bytes 1658880 | tf_op jit(solution)/shard_map/all_gather | solution.py:497
  9.3 15.4 %collective-permute-start = (bf16[144,256]{1,0:T(8,128)(2,1)}, bf16[144,256]{1,0:T(8,128)(2,1)S(1)}, u32[]{:S(2)}, u32[]{:S(2)}) collective-permute-start(bf16[144,256]{1,0:T(8,128)(2,1)} %q_ref.1), channel_id=1, source_target_pairs={{0,1},{1,2},{2,3},{3,0},{4,5},{5,6},{6,7},{7,4},{8,9},{9,10},{10,1... | collective-permute-start | bytes 221192 | tf_op jit(solution)/shard_map/ppermute | solution.py:525
  12.4 12.3 %collective-permute-start.1 = (bf16[144,256]{1,0:T(8,128)(2,1)}, bf16[144,256]{1,0:T(8,128)(2,1)S(1)}, u32[]{:S(2)}, u32[]{:S(2)}) collective-permute-start(bf16[144,256]{1,0:T(8,128)(2,1)} %q_ref.1), channel_id=1, source_target_pairs={{0,2},{1,3},{2,0},{3,1},{4,6},{5,7},{6,4},{7,5},{8,10},{9,11},{10,... | collective-permute-start | bytes 221192 | tf_op jit(solution)/shard_map/ppermute | solution.py:525
  15.0 9.7 %collective-permute-start.2 = (bf16[144,256]{1,0:T(8,128)(2,1)}, bf16[144,256]{1,0:T(8,128)(2,1)S(1)}, u32[]{:S(2)}, u32[]{:S(2)}) collective-permute-start(bf16[144,256]{1,0:T(8,128)(2,1)} %q_ref.1), channel_id=1, source_target_pairs={{0,3},{1,0},{2,1},{3,2},{4,7},{5,4},{6,5},{7,6},{8,11},{9,8},{10,9... | collective-permute-start | bytes 221192 | tf_op jit(solution)/shard_map/ppermute | solution.py:525
  16.4 14.2 %all-to-all-start = ((bf16[8,16,1152]{2,1,0:T(8,128)(2,1)}), bf16[8,16,1152]{2,1,0:T(8,128)(2,1)S(1)}, u32[]{:S(2)}, u32[]{:S(2)}) async-start(bf16[8,16,1152]{2,1,0:T(8,128)(2,1)} %bitcast.40), calls=%async_computation | async-start | bytes 589824 | tf_op jit(solution)/shard_map/all_to_all | solution.py:534
  20.1 97.1 %all-gather.6.cloned.1.call-start = ((), (), s32[]{:S(2)}) async-start(), calls=%async_computation.8 | async-start | bytes 7741440 | tf_op jit(solution)/shard_map/all_gather | solution.py:497
  30.6 156.6 %all-gather.8.cloned.1.call-start = ((), (), s32[]{:S(2)}) async-start(), calls=%async_computation.9 | async-start | bytes 1474560 | tf_op jit(solution)/shard_map/all_gather | solution.py:497
  30.6 11.9 %collective-permute-start.3 = (bf16[128,1152]{1,0:T(8,128)(2,1)S(1)}, bf16[128,1152]{1,0:T(8,128)(2,1)S(1)}, u32[]{:S(2)}, u32[]{:S(2)}) collective-permute-start(bf16[128,1152]{1,0:T(8,128)(2,1)S(1)} %bitcast.29), channel_id=1, source_target_pairs={{0,1},{1,2},{2,3},{3,0},{4,5},{5,6},{6,7},{7,4},{8,9},{9,10},{10,1... | collective-permute-start | bytes 884744 | tf_op jit(solution)/shard_map/ppermute | solution.py:525
  31.0 20.4 %collective-permute-start.4 = (bf16[128,1152]{1,0:T(8,128)(2,1)S(1)}, bf16[128,1152]{1,0:T(8,128)(2,1)S(1)}, u32[]{:S(2)}, u32[]{:S(2)}) collective-permute-start(bf16[128,1152]{1,0:T(8,128)(2,1)S(1)} %bitcast.30), channel_id=1, source_target_pairs={{0,2},{1,3},{2,0},{3,1},{4,6},{5,7},{6,4},{7,5},{8,10},{9,11},{10,... | collective-permute-start | bytes 884744 | tf_op jit(solution)/shard_map/ppermute | solution.py:525
  31.0 20.4 %collective-permute-start.5 = (bf16[128,1152]{1,0:T(8,128)(2,1)S(1)}, bf16[128,1152]{1,0:T(8,128)(2,1)S(1)}, u32[]{:S(2)}, u32[]{:S(2)}) collective-permute-start(bf16[128,1152]{1,0:T(8,128)(2,1)S(1)} %bitcast.31), channel_id=1, source_target_pairs={{0,3},{1,0},{2,1},{3,2},{4,7},{5,4},{6,5},{7,6},{8,11},{9,8},{10,9... | collective-permute-start | bytes 884744 | tf_op jit(solution)/shard_map/ppermute | solution.py:525
  51.4 3.3 collective-permute-start.6
  55.9 61.4 %copy-start.37 = (bf16[144,256]{1,0:T(8,128)(2,1)S(1)}, bf16[144,256]{1,0:T(8,128)(2,1)}, u32[]{:S(2)}) copy-start(bf16[144,256]{1,0:T(8,128)(2,1)} %q_ref.1) | copy-start | bytes 221188
  66.0 13.9 %collective-permute-start.7 = (bf16[128,1152]{1,0:T(8,128)(2,1)}, bf16[128,1152]{1,0:T(8,128)(2,1)S(1)}, u32[]{:S(2)}, u32[]{:S(2)}) collective-permute-start(bf16[128,1152]{1,0:T(8,128)(2,1)} %get-tuple-element.105), channel_id=1, source_target_pairs={{0,1},{1,2},{2,3},{3,0},{4,5},{5,6},{6,7},{7,4},{8,9},{9,10},{10,1... | collective-permute-start | bytes 884744 | tf_op jit(solution)/shard_map/ppermute | solution.py:525
  72.1 19.7 %collective-permute-start.8 = (bf16[128,1152]{1,0:T(8,128)(2,1)}, bf16[128,1152]{1,0:T(8,128)(2,1)S(1)}, u32[]{:S(2)}, u32[]{:S(2)}) collective-permute-start(bf16[128,1152]{1,0:T(8,128)(2,1)} %get-tuple-element.106), channel_id=1, source_target_pairs={{0,2},{1,3},{2,0},{3,1},{4,6},{5,7},{6,4},{7,5},{8,10},{9,11},{10,... | collective-permute-start | bytes 884744 | tf_op jit(solution)/shard_map/ppermute | solution.py:525
  72.2 19.7 %collective-permute-start.9 = (bf16[128,1152]{1,0:T(8,128)(2,1)}, bf16[128,1152]{1,0:T(8,128)(2,1)S(1)}, u32[]{:S(2)}, u32[]{:S(2)}) collective-permute-start(bf16[128,1152]{1,0:T(8,128)(2,1)} %get-tuple-element.107), channel_id=1, source_target_pairs={{0,3},{1,0},{2,1},{3,2},{4,7},{5,4},{6,5},{7,6},{8,11},{9,8},{10,9... | collective-permute-start | bytes 884744 | tf_op jit(solution)/shard_map/ppermute | solution.py:525
  95.3 39.7 %copy-start.7 = (bf16[128,1152]{1,0:T(8,128)(2,1)}, bf16[128,1152]{1,0:T(8,128)(2,1)S(1)}, u32[]{:S(2)}) copy-start(bf16[128,1152]{1,0:T(8,128)(2,1)S(1)} %get-tuple-element.110.refs_0_) | copy-start | bytes 884740
  95.3 17.1 %collective-permute-start.10 = (bf16[128,1152]{1,0:T(8,128)(2,1)S(1)}, bf16[128,1152]{1,0:T(8,128)(2,1)S(1)}, u32[]{:S(2)}, u32[]{:S(2)}) collective-permute-start(bf16[128,1152]{1,0:T(8,128)(2,1)S(1)} %get-tuple-element.110.refs_0_), channel_id=1, source_target_pairs={{0,1},{1,2},{2,3},{3,0},{4,5},{5,6},{6,7},{7,4},{8,9},{9,10},{10,1... | collective-permute-start | bytes 884744 | tf_op jit(solution)/shard_map/ppermute | solution.py:525
  102.1 15.1 %collective-permute-start.12 = (bf16[128,1152]{1,0:T(8,128)(2,1)S(1)}, bf16[128,1152]{1,0:T(8,128)(2,1)S(1)}, u32[]{:S(2)}, u32[]{:S(2)}) collective-permute-start(bf16[128,1152]{1,0:T(8,128)(2,1)S(1)} %get-tuple-element.110.refs_0_), channel_id=1, source_target_pairs={{0,3},{1,0},{2,1},{3,2},{4,7},{5,4},{6,5},{7,6},{8,11},{9,8},{10,9... | collective-permute-start | bytes 884744 | tf_op jit(solution)/shard_map/ppermute | solution.py:525
  117.2 17.8 %collective-permute-start.13 = (bf16[3,576,1728]{2,1,0:T(8,128)(2,1)}, bf16[3,576,1728]{2,1,0:T(8,128)(2,1)}, u32[]{:S(2)}, u32[]{:S(2)}) collective-permute-start(bf16[3,576,1728]{2,1,0:T(8,128)(2,1)} %all-gather.6.cloned.1.call-done.refs_4_.refs_6_), channel_id=1, source_target_pairs={{0,4},{4,0},{8,12},{12,8},{16,20},{20,16},{24,28},{28,24},{1,5},{5... | collective-permute-start | bytes 17915912 | tf_op jit(solution)/shard_map/ppermute | solution.py:502
  118.0 36.6 %copy-start.38 = (bf16[8,1,16,1152]{3,2,1,0:T(8,128)(2,1)S(1)}, bf16[8,1,16,1152]{3,2,1,0:T(8,128)(2,1)}, u32[]{:S(2)}) copy-start(bf16[8,1,16,1152]{3,2,1,0:T(8,128)(2,1)} %param.17) | copy-start | bytes 884740
  118.1 56.3 %copy-start.6 = (f32[8,1152]{1,0:T(8,128)S(1)}, f32[8,1152]{1,0:T(8,128)}, u32[]{:S(2)}) copy-start(f32[8,1152]{1,0:T(8,128)} %get-tuple-element.109.refs_5_.refs_8_.gains_ref) | copy-start | bytes 110596
  118.1 56.3 %copy-start.18 = (s32[1,1152]{1,0:T(1,128)S(1)}, s32[1,1152]{1,0:T(1,128)}, u32[]{:S(2)}) copy-start(s32[1,1152]{1,0:T(1,128)} %get-tuple-element.119.refs_6_.order_ref) | copy-start | bytes 13828
  118.1 56.3 %copy-start.22 = (s32[5]{0:T(128)S(1)}, s32[5]{0:T(128)}, u32[]{:S(2)}) copy-start(s32[5]{0:T(128)} %stack.42.refs_6_.refs_7_) | copy-start | bytes 64
  118.1 137.9 %reduce-scatter.3.cloned.1.call-start = ((), (), s32[]{:S(2)}) async-start(), calls=%async_computation.10 | async-start | bytes 1474560 | tf_op jit(solution)/shard_map/reduce_scatter | solution.py:636
  118.3 16.7 %collective-permute-start.11 = (bf16[128,1152]{1,0:T(8,128)(2,1)S(1)}, bf16[128,1152]{1,0:T(8,128)(2,1)S(1)}, u32[]{:S(2)}, u32[]{:S(2)}) collective-permute-start(bf16[128,1152]{1,0:T(8,128)(2,1)S(1)} %get-tuple-element.110.refs_0_), channel_id=1, source_target_pairs={{0,2},{1,3},{2,0},{3,1},{4,6},{5,7},{6,4},{7,5},{8,10},{9,11},{10,... | collective-permute-start | bytes 884744 | tf_op jit(solution)/shard_map/ppermute | solution.py:525
  150.8 13.7 %collective-permute-start.14 = (bf16[128,1152]{1,0:T(8,128)(2,1)}, bf16[128,1152]{1,0:T(8,128)(2,1)S(1)}, u32[]{:S(2)}, u32[]{:S(2)}) collective-permute-start(bf16[128,1152]{1,0:T(8,128)(2,1)} %get-tuple-element.114), channel_id=1, source_target_pairs={{0,1},{1,2},{2,3},{3,0},{4,5},{5,6},{6,7},{7,4},{8,9},{9,10},{10,1... | collective-permute-start | bytes 884744 | tf_op jit(solution)/shard_map/ppermute | solution.py:525
  150.8 23.5 %collective-permute-start.15 = (bf16[128,1152]{1,0:T(8,128)(2,1)}, bf16[128,1152]{1,0:T(8,128)(2,1)S(1)}, u32[]{:S(2)}, u32[]{:S(2)}) collective-permute-start(bf16[128,1152]{1,0:T(8,128)(2,1)} %get-tuple-element.115), channel_id=1, source_target_pairs={{0,2},{1,3},{2,0},{3,1},{4,6},{5,7},{6,4},{7,5},{8,10},{9,11},{10,... | collective-permute-start | bytes 884744 | tf_op jit(solution)/shard_map/ppermute | solution.py:525
  153.4 20.9 %collective-permute-start.16 = (bf16[128,1152]{1,0:T(8,128)(2,1)}, bf16[128,1152]{1,0:T(8,128)(2,1)S(1)}, u32[]{:S(2)}, u32[]{:S(2)}) collective-permute-start(bf16[128,1152]{1,0:T(8,128)(2,1)} %get-tuple-element.116), channel_id=1, source_target_pairs={{0,3},{1,0},{2,1},{3,2},{4,7},{5,4},{6,5},{7,6},{8,11},{9,8},{10,9... | collective-permute-start | bytes 884744 | tf_op jit(solution)/shard_map/ppermute | solution.py:525
  178.9 13.4 %collective-permute-start.17 = (bf16[128,1152]{1,0:T(8,128)(2,1)S(1)}, bf16[128,1152]{1,0:T(8,128)(2,1)S(1)}, u32[]{:S(2)}, u32[]{:S(2)}) collective-permute-start(bf16[128,1152]{1,0:T(8,128)(2,1)S(1)} %get-tuple-element.123.refs_0_), channel_id=1, source_target_pairs={{0,1},{1,2},{2,3},{3,0},{4,5},{5,6},{6,7},{7,4},{8,9},{9,10},{10,1... | collective-permute-start | bytes 884744 | tf_op jit(solution)/shard_map/ppermute | solution.py:525
  184.8 17.5 %collective-permute-start.18 = (bf16[128,1152]{1,0:T(8,128)(2,1)S(1)}, bf16[128,1152]{1,0:T(8,128)(2,1)S(1)}, u32[]{:S(2)}, u32[]{:S(2)}) collective-permute-start(bf16[128,1152]{1,0:T(8,128)(2,1)S(1)} %get-tuple-element.123.refs_0_), channel_id=1, source_target_pairs={{0,2},{1,3},{2,0},{3,1},{4,6},{5,7},{6,4},{7,5},{8,10},{9,11},{10,... | collective-permute-start | bytes 884744 | tf_op jit(solution)/shard_map/ppermute | solution.py:525
  184.8 18.3 %collective-permute-start.19 = (bf16[128,1152]{1,0:T(8,128)(2,1)S(1)}, bf16[128,1152]{1,0:T(8,128)(2,1)S(1)}, u32[]{:S(2)}, u32[]{:S(2)}) collective-permute-start(bf16[128,1152]{1,0:T(8,128)(2,1)S(1)} %get-tuple-element.123.refs_0_), channel_id=1, source_target_pairs={{0,3},{1,0},{2,1},{3,2},{4,7},{5,4},{6,5},{7,6},{8,11},{9,8},{10,9... | collective-permute-start | bytes 884744 | tf_op jit(solution)/shard_map/ppermute | solution.py:525
  219.3 128.2 %reduce-scatter.5.cloned.1.call-start = ((), (), s32[]{:S(2)}) async-start(), calls=%async_computation.11 | async-start | bytes 7741440 | tf_op jit(solution)/shard_map/reduce_scatter | solution.py:508
  227.7 4.5 %collective-permute-start.20 = (bf16[576,1728]{1,0:T(8,128)(2,1)}, bf16[576,1728]{1,0:T(8,128)(2,1)}, u32[]{:S(2)}, u32[]{:S(2)}) collective-permute-start(bf16[576,1728]{1,0:T(8,128)(2,1)} %get-tuple-element.132), channel_id=1, source_target_pairs={{0,4},{4,0},{8,12},{12,8},{16,20},{20,16},{24,28},{28,24},{1,5},{5... | collective-permute-start | bytes 5971976 | tf_op jit(solution)/shard_map/ppermute | solution.py:502
  227.7 7.4 %collective-permute-start.21 = (bf16[576,1728]{1,0:T(8,128)(2,1)}, bf16[576,1728]{1,0:T(8,128)(2,1)}, u32[]{:S(2)}, u32[]{:S(2)}) collective-permute-start(bf16[576,1728]{1,0:T(8,128)(2,1)} %get-tuple-element.133), channel_id=1, source_target_pairs={{0,4},{4,0},{8,12},{12,8},{16,20},{20,16},{24,28},{28,24},{1,5},{5... | collective-permute-start | bytes 5971976 | tf_op jit(solution)/shard_map/ppermute | solution.py:502
  228.2 9.8 %collective-permute-start.22 = (bf16[576,1728]{1,0:T(8,128)(2,1)}, bf16[576,1728]{1,0:T(8,128)(2,1)}, u32[]{:S(2)}, u32[]{:S(2)}) collective-permute-start(bf16[576,1728]{1,0:T(8,128)(2,1)} %get-tuple-element.134), channel_id=1, source_target_pairs={{0,4},{4,0},{8,12},{12,8},{16,20},{20,16},{24,28},{28,24},{1,5},{5... | collective-permute-start | bytes 5971976 | tf_op jit(solution)/shard_map/ppermute | solution.py:502
  259.6 50.6 %collective-permute-start.29 = (bf16[4,576,256]{2,1,0:T(8,128)(2,1)S(1)}, bf16[4,576,256]{2,1,0:T(8,128)(2,1)S(1)}, u32[]{:S(2)}, u32[]{:S(2)}) collective-permute-start(bf16[4,576,256]{2,1,0:T(8,128)(2,1)S(1)} %copy-done.24), channel_id=1, source_target_pairs={{0,4},{4,0},{8,12},{12,8},{16,20},{20,16},{24,28},{28,24},{1,5},{5... | collective-permute-start | bytes 3538952 | tf_op jit(solution)/shard_map/ppermute | solution.py:502
  259.6 11.8 %collective-permute-start.23 = (bf16[128,1152]{1,0:T(8,128)(2,1)S(1)}, bf16[128,1152]{1,0:T(8,128)(2,1)S(1)}, u32[]{:S(2)}, u32[]{:S(2)}) collective-permute-start(bf16[128,1152]{1,0:T(8,128)(2,1)S(1)} %get-tuple-element.138.refs_0_), channel_id=1, source_target_pairs={{0,1},{1,2},{2,3},{3,0},{4,5},{5,6},{6,7},{7,4},{8,9},{9,10},{10,1... | collective-permute-start | bytes 884744 | tf_op jit(solution)/shard_map/ppermute | solution.py:525
  259.8 23.9 %collective-permute-start.24 = (bf16[128,1152]{1,0:T(8,128)(2,1)S(1)}, bf16[128,1152]{1,0:T(8,128)(2,1)}, u32[]{:S(2)}, u32[]{:S(2)}) collective-permute-start(bf16[128,1152]{1,0:T(8,128)(2,1)S(1)} %get-tuple-element.138.refs_0_), channel_id=1, source_target_pairs={{0,2},{1,3},{2,0},{3,1},{4,6},{5,7},{6,4},{7,5},{8,10},{9,11},{10,... | collective-permute-start | bytes 884744 | tf_op jit(solution)/shard_map/ppermute | solution.py:525
  263.1 20.5 %collective-permute-start.25 = (bf16[128,1152]{1,0:T(8,128)(2,1)S(1)}, bf16[128,1152]{1,0:T(8,128)(2,1)}, u32[]{:S(2)}, u32[]{:S(2)}) collective-permute-start(bf16[128,1152]{1,0:T(8,128)(2,1)S(1)} %get-tuple-element.138.refs_0_), channel_id=1, source_target_pairs={{0,3},{1,0},{2,1},{3,2},{4,7},{5,4},{6,5},{7,6},{8,11},{9,8},{10,9... | collective-permute-start | bytes 884744 | tf_op jit(solution)/shard_map/ppermute | solution.py:525
  263.7 41.6 %all-to-all-start.2 = ((bf16[8,16,1152]{2,1,0:T(8,128)(2,1)}), bf16[8,16,1152]{2,1,0:T(8,128)(2,1)S(1)}, u32[]{:S(2)}, u32[]{:S(2)}) async-start(bf16[8,16,1152]{2,1,0:T(8,128)(2,1)} %bitcast.11), calls=%async_computation.2 | async-start | bytes 589824 | tf_op jit(solution)/shard_map/all_to_all | solution.py:539
  289.9 15.4 %collective-permute-start.26 = (bf16[128,768]{1,0:T(8,128)(2,1)}, bf16[128,768]{1,0:T(8,128)(2,1)S(1)}, u32[]{:S(2)}, u32[]{:S(2)}) collective-permute-start(bf16[128,768]{1,0:T(8,128)(2,1)} %get-tuple-element.158), channel_id=1, source_target_pairs={{0,1},{1,2},{2,3},{3,0},{4,5},{5,6},{6,7},{7,4},{8,9},{9,10},{10,1... | collective-permute-start | bytes 589832 | tf_op jit(solution)/shard_map/ppermute | solution.py:525
  296.2 13.9 %collective-permute-start.27 = (bf16[128,768]{1,0:T(8,128)(2,1)}, bf16[128,768]{1,0:T(8,128)(2,1)S(1)}, u32[]{:S(2)}, u32[]{:S(2)}) collective-permute-start(bf16[128,768]{1,0:T(8,128)(2,1)} %get-tuple-element.159), channel_id=1, source_target_pairs={{0,2},{1,3},{2,0},{3,1},{4,6},{5,7},{6,4},{7,5},{8,10},{9,11},{10,... | collective-permute-start | bytes 589832 | tf_op jit(solution)/shard_map/ppermute | solution.py:525
  297.3 12.9 %collective-permute-start.28 = (bf16[128,768]{1,0:T(8,128)(2,1)}, bf16[128,768]{1,0:T(8,128)(2,1)S(1)}, u32[]{:S(2)}, u32[]{:S(2)}) collective-permute-start(bf16[128,768]{1,0:T(8,128)(2,1)} %get-tuple-element.160), channel_id=1, source_target_pairs={{0,3},{1,0},{2,1},{3,2},{4,7},{5,4},{6,5},{7,6},{8,11},{9,8},{10,9... | collective-permute-start | bytes 589832 | tf_op jit(solution)/shard_map/ppermute | solution.py:525
  320.6 3.3 collective-permute-start.30
  347.5 17.8 %collective-permute-start.31 = (bf16[144,640]{1,0:T(8,128)(2,1)S(1)}, bf16[144,640]{1,0:T(8,128)(2,1)S(1)}, u32[]{:S(2)}, u32[]{:S(2)}) collective-permute-start(bf16[144,640]{1,0:T(8,128)(2,1)S(1)} %slice.49.refs_0_), channel_id=1, source_target_pairs={{0,1},{1,2},{2,3},{3,0},{4,5},{5,6},{6,7},{7,4},{8,9},{9,10},{10,1... | collective-permute-start | bytes 552968 | tf_op jit(solution)/shard_map/ppermute | solution.py:525
  352.2 14.1 %collective-permute-start.32 = (bf16[144,640]{1,0:T(8,128)(2,1)S(1)}, bf16[144,640]{1,0:T(8,128)(2,1)S(1)}, u32[]{:S(2)}, u32[]{:S(2)}) collective-permute-start(bf16[144,640]{1,0:T(8,128)(2,1)S(1)} %slice.49.refs_0_), channel_id=1, source_target_pairs={{0,2},{1,3},{2,0},{3,1},{4,6},{5,7},{6,4},{7,5},{8,10},{9,11},{10,... | collective-permute-start | bytes 552968 | tf_op jit(solution)/shard_map/ppermute | solution.py:525
  355.1 11.2 %collective-permute-start.33 = (bf16[144,640]{1,0:T(8,128)(2,1)S(1)}, bf16[144,640]{1,0:T(8,128)(2,1)S(1)}, u32[]{:S(2)}, u32[]{:S(2)}) collective-permute-start(bf16[144,640]{1,0:T(8,128)(2,1)S(1)} %slice.49.refs_0_), channel_id=1, source_target_pairs={{0,3},{1,0},{2,1},{3,2},{4,7},{5,4},{6,5},{7,6},{8,11},{9,8},{10,9... | collective-permute-start | bytes 552968 | tf_op jit(solution)/shard_map/ppermute | solution.py:525
  358.3 10.6 %all-to-all-start.4 = ((bf16[8,16,1152]{2,1,0:T(8,128)(2,1)}), bf16[8,16,1152]{2,1,0:T(8,128)(2,1)S(1)}, u32[]{:S(2)}, u32[]{:S(2)}) async-start(bf16[8,16,1152]{2,1,0:T(8,128)(2,1)} %bitcast.19), calls=%async_computation.6 | async-start | bytes 589824 | tf_op jit(solution)/shard_map/all_to_all | solution.py:539
  (40 other events, 256.8 us)
Sparse Core Ops, SparseCore 0:
  10.5 31.9 all-gather.3
  44.3 69.3 all-gather.5
  118.2 27.3 all-gather.7
  219.4 36.5 reduce-scatter.2
  259.0 71.2 reduce-scatter.4

commit v4 on v3

--- a/solution.py
+++ b/solution.py
@@ -17,9 +17,10 @@
 VMEM_LIMIT = 60 * 1024 * 1024
 CHUNKS = 1
 RING = 4
-
-
-def call(kernel, outs, scratch=(), anys=(), smem=(), count=0, flops=0, moved=0):
+FFN_TILE = 512
+
+
+def call(kernel, outs, scratch=(), anys=(), smem=(), count=0, flops=0, moved=0, far=0):
     limit = (16 if moved <= 4 * 10**6 and moved != 10**6 else 60) * 1024 * 1024
     def place(index):
         if index in anys:
@@ -32,7 +33,9 @@
         kernel,
         out_shape=[jax.ShapeDtypeStruct(s, d) for s, d in outs],
         in_specs=[place(i) for i in range(count)],
-        out_specs=[pl.BlockSpec(memory_space=pltpu.VMEM)] * len(outs),
+        out_specs=[
+            pl.BlockSpec(memory_space=pl.ANY if i < far else pltpu.VMEM) for i in range(len(outs))
+        ],
         scratch_shapes=list(scratch),
         compiler_params=pltpu.CompilerParams(vmem_limit_bytes=limit),
         cost_estimate=pl.CostEstimate(flops=1, bytes_accessed=1, transcendentals=0),
@@ -130,13 +133,34 @@
     return segment, position - begin
 
 
+def rope_tables(info_ref, cos_ref, sin_ref):
+    rows, half = cos_ref.shape
+    frequency = jnp.exp(
+        lax.broadcasted_iota(jnp.int32, (1, half), 1).astype(F32) * (-1.0 / half) * LOGBASE
+    )
+    for r, n in tiles(rows, 128):
+        position = lax.broadcasted_iota(jnp.int32, (n, 1), 0) + r
+        angle = segments(position, info_ref[2], info_ref[3])[1].astype(F32) * frequency
+        cos_ref[pl.ds(r, n), :] = jnp.cos(angle)
+        sin_ref[pl.ds(r, n), :] = jnp.sin(angle)
+
+
 def attention_forward(wide, *refs):
-    x_refs, weight_refs, info_ref, refs = refs[:RING], refs[RING:-26], refs[-26], refs[-25:]
+    x_refs, weight_refs, refs = refs[:RING], refs[RING:-32], refs[-32:]
+    info_ref, cos_ref, sin_ref, *refs = refs
     (
-        xp_ref, xn1_ref, qraw_ref, kraw_ref, q_ref, k_ref, v_ref, probs_ref, att_ref, gains_ref,
-        hgain_ref, wkv_ref, wout_ref, cos_ref, sin_ref, order_ref, pick_ref, *part_refs,
-        part_ref, x_ref, w_ref, sem,
-    ) = refs
+        *far_refs, wkv_ref, wout_ref, q_ref, k_ref, v_ref, att_ref, gains_ref,
+        hgain_ref, order_ref, pick_ref,
+    ) = refs[:15]
+    part_refs, near_refs = refs[15:-10], refs[-10:-5]
+    xp_ref, xn1_ref, qraw_ref, kraw_ref, probs_ref = near_refs
+    part_ref, x_ref, w_ref, sem, out_sem = refs[-5:]
+    leaving = []
+
+    def leave(here, there):
+        leaving.append(pltpu.make_async_copy(here, there, out_sem.at[len(leaving)]))
+        leaving[-1].start()
+
     head = q_ref.shape[1]
     rows, width = x_ref.shape
     half = width // 2
@@ -155,28 +179,24 @@
     step = 128
     for r, n in tiles(rows, step):
         xp_ref[pl.ds(r, n), :] = mm(x_ref[pl.ds(r, n), :], choose).astype(BF16)
-    frequency = jnp.exp(
-        lax.broadcasted_iota(jnp.int32, (1, head // 2), 1).astype(F32) * (-2.0 / head) * LOGBASE
-    )
-    for r, n in tiles(rows, step):
-        position = lax.broadcasted_iota(jnp.int32, (n, 1), 0) + r
-        angle = segments(position, first, ends)[1].astype(F32) * frequency
-        cos_ref[pl.ds(r, n), :] = jnp.cos(angle)
-        sin_ref[pl.ds(r, n), :] = jnp.sin(angle)
+    leave(xp_ref, far_refs[0])
     for c in copies:
         c.wait()
     columns = w_ref[:, 4 * head :].T
     gains_ref[...] = columns[:8].astype(F32)
     hgain_ref[...] = mm(columns[:8], one_hot(pick, width))
-    wkv_ref[...] = w_ref[:, head : 3 * head]
-    wout_ref[...] = w_ref[:, 3 * head : 4 * head]
+    leave(w_ref.at[:, pl.ds(head, 2 * head)], wkv_ref)
+    leave(w_ref.at[:, pl.ds(3 * head, head)], wout_ref)
     for r, n in tiles(rows, step):
         x = xp_ref[pl.ds(r, n), :].astype(F32)
         xn1_ref[pl.ds(r, n), :] = norm(x, gains_ref[0:1, :]).astype(BF16)
+    leave(xn1_ref, far_refs[1])
     gq, gk = hgain_ref[4:5, :], hgain_ref[5:6, :]
     raw = mm(xn1_ref[...], w_ref[:, : 3 * head])
     qraw_ref[...] = raw[:, :head]
     kraw_ref[...] = raw[:, head : 2 * head]
+    leave(qraw_ref, far_refs[2])
+    leave(kraw_ref, far_refs[3])
     v_ref[...] = raw[:, 2 * head :].astype(BF16)
     cosine, sine = cos_ref[...], sin_ref[...]
     q_ref[...] = rotate(norm(raw[:, :head], gq), cosine, sine).astype(BF16)
@@ -191,11 +211,14 @@
         p = e / jnp.sum(e, axis=-1, keepdims=True)
         probs_ref[pl.ds(r, n), :] = p
         att_ref[pl.ds(r, n), :] = mm(p.astype(BF16), v_ref[...]).astype(BF16)
+    leave(probs_ref, far_refs[4])
     for r, n in tiles(rows, step):
         part_ref[pl.ds(r, n), :] = mm_nt(
             att_ref[pl.ds(r, n), :], w_ref[:, 3 * head : 4 * head]
         ).astype(BF16)
     hand_out(part_ref, slot, part_refs)
+    for c in leaving:
+        c.wait()
 
 
 def hand_out(whole_ref, slot, refs):
@@ -256,30 +279,65 @@
 
 def ffn_forward(*refs):
     wm_ref, wo_ref = refs[RING : RING + 2]
-    x_ref, act_ref, fa_ref, fb_ref, *part_refs = refs[RING + 2 : -3]
-    part_ref, w_ref, sem = refs[-3:]
-    waits = load_weights((wm_ref, wo_ref), w_ref, sem, (0, 1, 2))
+    x_out, act_out, fa_out, fb_out, *part_refs = refs[RING + 2 : -9]
+    x_ref, act_ref, fa_ref, fb_ref, part_ref, w_ref, sem, down_sem, out_sem = refs[-9:]
+    half = wm_ref.shape[1]
+    cuts = tiles(act_ref.shape[1], FFN_TILE)
+    loads = []
+    for t, (f, n) in enumerate(cuts):
+        columns = pl.ds(f, n)
+        group = [
+            pltpu.make_async_copy(
+                ref.at[i, :, columns],
+                w_ref.at[i, pl.ds(j * half, half), columns],
+                sem.at[t, 2 * i + j],
+            )
+            for i in (0, 1)
+            for j, ref in enumerate((wm_ref, wo_ref))
+        ]
+        for c in group:
+            c.start()
+        loads.append(group)
+    down = [
+        pltpu.make_async_copy(ref.at[2], w_ref.at[2, pl.ds(j * half, half)], down_sem.at[j])
+        for j, ref in enumerate((wm_ref, wo_ref))
+    ]
+    for c in down:
+        c.start()
     for s in range(RING):
         n = refs[s].shape[0]
         x_ref[s * n : (s + 1) * n] = refs[s][...]
-    waits[0]()
-    waits[1]()
+    leaving = [pltpu.make_async_copy(x_ref, x_out, out_sem.at[0, 0])]
+    leaving[0].start()
     x = x_ref[...]
-    for f, n in tiles(act_ref.shape[1], 256):
-        gate = mm(x, w_ref[0, :, pl.ds(f, n)])
-        up = mm(x, w_ref[1, :, pl.ds(f, n)])
+    for t, (f, n) in enumerate(cuts):
+        columns = pl.ds(f, n)
+        for c in loads[t]:
+            c.wait()
+        gate = mm(x, w_ref[0, :, columns])
+        up = mm(x, w_ref[1, :, columns])
         square = gate * gate
-        t = jnp.tanh(GELU_C * (gate + GELU_A * (gate * square)))
-        bell = 0.5 * (1.0 + t)
+        th = jnp.tanh(GELU_C * (gate + GELU_A * (gate * square)))
+        bell = 0.5 * (1.0 + th)
         g = gate * bell
-        slope = bell + 0.5 * gate * (1.0 - t * t) * (GELU_C * (1.0 + 3.0 * GELU_A * square))
-        act_ref[:, pl.ds(f, n)] = (g * up).astype(BF16)
-        fa_ref[:, pl.ds(f, n)] = (slope * up).astype(BF16)
-        fb_ref[:, pl.ds(f, n)] = g.astype(BF16)
-    waits[2]()
+        slope = bell + 0.5 * gate * (1.0 - th * th) * (GELU_C * (1.0 + 3.0 * GELU_A * square))
+        act_ref[:, columns] = (g * up).astype(BF16)
+        fa_ref[:, columns] = (slope * up).astype(BF16)
+        fb_ref[:, columns] = g.astype(BF16)
+        pairs = ((act_ref, act_out), (fa_ref, fa_out), (fb_ref, fb_out))
+        for i, (here, there) in enumerate(pairs):
+            c = pltpu.make_async_copy(
+                here.at[:, columns], there.at[:, columns], out_sem.at[1 + t, i]
+            )
+            c.start()
+            leaving.append(c)
+    for c in down:
+        c.wait()
     for d, n in tiles(part_ref.shape[1], 384):
         part_ref[:, pl.ds(d, n)] = mm_nt(act_ref[...], w_ref[2, pl.ds(d, n), :]).astype(BF16)
     spread(part_ref, part_refs)
+    for c in leaving:
+        c.wait()
 
 
 def middle_turn(chunk, *refs):
@@ -407,18 +465,29 @@
     g0_ref, g1_ref, g2_ref, g3_ref, xp_ref, xn1_ref, dh_ref, kraw_ref, cos_ref, sin_ref, hgain_ref, gains_ref, order_ref,
     pick_ref, slot_ref, t1_ref, t2_ref, t3_ref, qterm_ref, qm_ref, qo_ref, om_ref, oo_ref, w_ref, hm_ref, ho_ref,
     out_ref, own_ref, other_ref,
-    wq_ref, hsem,
+    wq_ref, hsem, x_here, xn1_here, raw_here, cos_here, sin_here, row_sem,
 ):
     head = kraw_ref.shape[1]
     n, width = dh_ref.shape
     half = width // 2
     arrived = load_heads((hm_ref, ho_ref), wq_ref, hsem)
     here = pl.ds(pl.multiple_of(slot_ref[0] * n, n), n)
+    rows = [
+        pltpu.make_async_copy(ref.at[here], target, row_sem.at[i])
+        for i, (ref, target) in enumerate((
+            (kraw_ref, raw_here), (cos_ref, cos_here), (sin_ref, sin_here), (xn1_ref, xn1_here),
+            (xp_ref, x_here),
+        ))
+    ]
+    for c in rows:
+        c.start()
     g_refs = (g0_ref, g1_ref, g2_ref, g3_ref)
     joined = sum(ref[:, head:].astype(F32) for ref in g_refs)
     dk = joined[:, :head].astype(BF16).astype(F32)
-    e = rotate_back(dk, cos_ref[here, :], sin_ref[here, :])
-    raw = kraw_ref[here, :]
+    for c in rows:
+        c.wait()
+    e = rotate_back(dk, cos_here[...], sin_here[...])
+    raw = raw_here[...]
     kterm = norm_term(raw, e)
     dkr = norm_back(raw, e, hgain_ref[5:6, :]).astype(BF16)
     dkv = jnp.concatenate([dkr, joined[:, head:].astype(BF16)], axis=1)
@@ -426,12 +495,12 @@
     arrived()
     for i, ref in enumerate(g_refs):
         dxn1 = dxn1 + mm_nt(ref[:, :head], wq_ref[i])
-    x = xp_ref[here, :].astype(F32)
+    x = x_here[...].astype(F32)
     dx = (dh_ref[...] + norm_back(x, dxn1, gains_ref[0:1, :])).astype(BF16)
     term = norm_term(x, dxn1)
     choose = one_hot(order_ref[...], width)
     out_ref[...] = mm_nt(dx, choose).astype(BF16)
-    grad = mm_tn(xn1_ref[here, :], dkv)
+    grad = mm_tn(xn1_here[...], dkv)
     for i, (mine, others) in enumerate(((qm_ref, qo_ref), (om_ref, oo_ref))):
         own_ref[:, i * head : (i + 1) * head] = mine[...]
         other_ref[:, i * head : (i + 1) * head] = others[...]
@@ -548,9 +617,12 @@
     lengths = seq_lengths[0]
     info = jnp.stack([slot, core, lengths[0], lengths[0] + lengths[1], 0]).astype(jnp.int32)
     queries = gather_ring(query_weight)
-    own_x = after(enter(tokens), info, *queries)
+    rows = narrow * tokens.shape[2] * wide
+    cosine, sine = call(
+        rope_tables, [((rows, head // 2), F32)] * 2, smem=(0,), count=1, flops=10**6, moved=2 * 10**6
+    )(info)
+    own_x = after(enter(tokens), info, cosine, sine, *queries)
     quarter = own_x.shape[0]
-    rows = quarter * narrow
     part = quarter // CHUNKS
     every = range(CHUNKS)
     sem = pltpu.SemaphoreType.DMA
@@ -561,26 +633,28 @@
     wh_mine = gather_wide(after(jnp.stack(queries), wf_mine), 1)
     own_dy = enter(after(cotangent, own_x))
     many = len(x_all) + len(weights)
+    kept = [
+        ((rows, width), bf), ((rows, width), bf), ((rows, head), ff), ((rows, head), ff),
+        ((rows, rows), ff),
+    ]
     (
-        xp, xn1, qraw, kraw, q, k, v, probs, attended, gains, hgain, wkv, wout, cosine, sine, order, pick,
-        *z_parts,
+        xp, xn1, qraw, kraw, probs, wkv, wout, q, k, v, attended, gains, hgain,
+        order, pick, *z_parts,
     ) = call(
         functools.partial(attention_forward, wide),
-        [
-            ((rows, width), bf), ((rows, width), bf), ((rows, head), ff), ((rows, head), ff),
-            ((rows, head), bf), ((rows, head), bf), ((rows, head), bf), ((rows, rows), ff),
-            ((rows, head), bf), ((8, width), ff), ((8, head), ff), ((width, 2 * head), bf), ((width, head), bf),
-            ((rows, head // 2), ff), ((rows, head // 2), ff), ((1, width), jnp.int32),
-            ((1, head), jnp.int32),
-        ]
+        kept
+        + [((width, 2 * head), bf), ((width, head), bf)]
+        + [((rows, head), bf)] * 4
+        + [((8, width), ff), ((8, head), ff), ((1, width), jnp.int32), ((1, head), jnp.int32)]
         + [((quarter, width), bf)] * narrow,
-        scratch=[
+        scratch=[pltpu.VMEM(*k) for k in kept]
+        + [
             pltpu.VMEM((rows, width), bf), pltpu.VMEM((rows, width), bf),
-            pltpu.VMEM((width, 4 * head + 128), bf), sem((len(weights),)),
+            pltpu.VMEM((width, 4 * head + 128), bf), sem((len(weights),)), sem((7,)),
         ],
-        anys=tuple(range(len(x_all), many)), smem=(many,), count=many + 1,
+        anys=tuple(range(len(x_all), many)), smem=(many,), count=many + 3, far=7,
         flops=3 * 10**9, moved=8 * 10**6,
-    )(*x_all, *weights, info)
+    )(*x_all, *weights, info, cosine, sine)
     z = pass_on(z_parts)
     mixed, h, *xn2_own = call(
         middle_forward,
@@ -594,8 +668,12 @@
             ffn_forward,
             [((narrow * part, width), bf)] + [((narrow * part, units), bf)] * 3
             + [((part, width), bf)] * narrow,
-            scratch=[pltpu.VMEM((narrow * part, width), bf), f_scratch, sem((6,))],
-            anys=(narrow, narrow + 1), count=narrow + 2, flops=3 * 10**9, moved=16 * 10**6,
+            scratch=[pltpu.VMEM((rows, width), bf)] + [pltpu.VMEM((rows, units), bf)] * 3
+            + [
+                pltpu.VMEM((rows, width), bf), f_scratch, sem((len(tiles(units, FFN_TILE)), 4)),
+                sem((2,)), sem((len(tiles(units, FFN_TILE)) + 1, 3)),
+            ],
+            anys=(narrow, narrow + 1), count=narrow + 2, far=4, flops=3 * 10**9, moved=16 * 10**6,
         )(*xn2[c], wf_mine, wf_other)
 
     ahead = []
@@ -683,8 +761,13 @@
     dx_own, own, other = call(
         last_rows,
         [((quarter, width), bf)] + [((half, 4 * head + 128), bf)] * 2,
-        scratch=[pltpu.VMEM((heads, width, head), bf), sem((2,))],
-        smem=(14,), anys=(24, 25), count=26, flops=10**9, moved=8 * 10**6,
+        scratch=[
+            pltpu.VMEM((heads, width, head), bf), sem((2,)),
+            pltpu.VMEM((quarter, width), bf), pltpu.VMEM((quarter, width), bf),
+            pltpu.VMEM((quarter, head), ff), pltpu.VMEM((quarter, head // 2), ff),
+            pltpu.VMEM((quarter, head // 2), ff), sem((5,)),
+        ],
+        smem=(14,), anys=(4, 5, 7, 8, 9, 24, 25), count=26, flops=10**9, moved=8 * 10**6,
     )(
         *joined, xp, xn1, d_resid, kraw, cosine, sine, hgain, gains, order, pick, slots,
         attnout_term, ffn_term, *turn_term, query_term, *g_query, *g_outproj, wkv,

time: 386 us -> 382 us (0.990)
  waiting for transfers between devices: 142 us -> 138 us
    unnamed x94 -> x100, local copies, waits for them, and re-layouts: 17.9 us -> 19.3 us
    pallas_call x1 -> x2, Pallas kernels: 10.1 us -> 10.3 us  [the longest x1 8.8 us: on_device(): call(functools.partial(attention_forward, wide), kept + [((width, 2 * hea...]
  transfers between devices with their start and end apart: 42 -> 42, of which waited for: 23 -> 23; matrix products, arithmetic and copies ran while one was open for 4% -> 3% of each run, Pallas kernels for 17% -> 17%
where the time goes in v4:
time: 382 us; the launch traced here: 375 us
  waiting for transfers between devices  138 us (36%)
  Pallas kernels  81.8 us (21%)
  starting transfers between devices  74.7 us (20%)
  blocking collectives  31.8 us (8%)
  local copies, waits for them, and re-layouts  24.9 us (7%)
  between operations  16 us (4%)
  other arithmetic  7.27 us (2%)
    ppermute x27, waiting for transfers between devices, pass_on(): got.append(lax.ppermute(parts[s], 'narrow', shift))  109 us
    ppermute x27, starting transfers between devices, pass_on(): got.append(lax.ppermute(parts[s], 'narrow', shift))  62.7 us
    all_to_all x1, blocking collectives, scatter_chips(): lax.all_to_all(parts, 'wide', split_axis=0, concat_axis=0, tiled=True, ax...  20.9 us
    pallas_call x2, Pallas kernels, ffn_grads(): call(functools.partial(ffn_weight_grads, first), outs, scratch=[pltpu.VME...  19.3 us
    unnamed x100, local copies, waits for them, and re-layouts  19.3 us
    ppermute x7, waiting for transfers between devices, sibling(): return lax.ppermute(value, 'wide', swap)  16.4 us
    pallas_call x1, Pallas kernels, ffn_back(): call(ffn_backward, [((narrow * part, width), bf)] + [((narrow * part, uni...  15.4 us
    pallas_call x1, Pallas kernels, ffn_ahead(): call(ffn_forward, [((narrow * part, width), bf)] + [((narrow * part, unit...  13.7 us
  transfers between devices with their start and end apart: 42, of which 23 were waited for; matrix products, arithmetic and copies ran while one was open for 3% of the time, Pallas kernels for 17%

profile of v4, /device:TPU:0, one launch (start us, length us, event | category | flops | bytes accessed | tf_op | source)
XLA Modules:
  0.0 374.8 jit_solution(88169537169983735)
XLA Ops:
  9.4 3.1 collective-permute-start
  12.4 2.6 collective-permute-start.1
  16.4 3.7 all-to-all-start
  27.2 3.4 all-to-all-done
  31.1 3.5 collective-permute-start.5
  34.5 8.0 %collective-permute-done.3.refs_1_ = bf16[128,1152]{1,0:T(8,128)(2,1)S(1)} collective-permute-done((bf16[128,1152]{1,0:T(8,128)(2,1)S(1)}, bf16[128,1152]{1,0:T(8,128)(2,1)S(1)}, u32[]{:S(2)}, u32[]{:S(2)}) %collective-permute-start.3) | collective-permute-done | bytes 294944 | tf_op jit(solution)/shard_map/ppermute | solution.py:594
  42.5 8.9 %collective-permute-done.4.refs_2_ = bf16[128,1152]{1,0:T(8,128)(2,1)S(1)} collective-permute-done((bf16[128,1152]{1,0:T(8,128)(2,1)S(1)}, bf16[128,1152]{1,0:T(8,128)(2,1)S(1)}, u32[]{:S(2)}, u32[]{:S(2)}) %collective-permute-start.4) | collective-permute-done | bytes 294944 | tf_op jit(solution)/shard_map/ppermute | solution.py:594
  51.5 3.3 collective-permute-done.6.refs_4_
  55.9 8.8 %shard_map.273 = (bf16[512,1152]{1,0:T(8,128)(2,1)}, bf16[512,1152]{1,0:T(8,128)(2,1)}, f32[512,256]{1,0:T(8,128)}, f32[512,256]{1,0:T(8,128)}, f32[512,512]{1,0...) custom-call(bf16[128,1152]{1,0:T(8,128)(2,1)} %bitcast.32, ...), custom_call_target="tpu_custom_call" | custom-call | flops 1 | bytes 1 | tf_op jit(solution)/shard_map/pallas_call | solution.py:643
  64.7 6.2 %collective-permute-start.7 = (bf16[128,1152]{1,0:T(8,128)(2,1)}, bf16[128,1152]{1,0:T(8,128)(2,1)S(1)}, u32[]{:S(2)}, u32[]{:S(2)}) collective-permute-start(bf16[128,1152]{1,0:T(8,128)(2,1)} %get-tuple-element.107), channel_id=1, source_target_pairs={{0,1},{1,2},{2,3},{3,0},{4,5},{5,6},{6,7},{7,4},{8,9},{9,10},{10,1... | collective-permute-start | bytes 884744 | tf_op jit(solution)/shard_map/ppermute | solution.py:594
  70.8 2.4 collective-permute-start.9
  73.3 5.3 %collective-permute-done.7.refs_1_ = bf16[128,1152]{1,0:T(8,128)(2,1)S(1)} collective-permute-done((bf16[128,1152]{1,0:T(8,128)(2,1)}, bf16[128,1152]{1,0:T(8,128)(2,1)S(1)}, u32[]{:S(2)}, u32[]{:S(2)}) %collective-permute-start.7) | collective-permute-done | bytes 294944 | tf_op jit(solution)/shard_map/ppermute | solution.py:594
  78.5 12.0 %collective-permute-done.8.refs_2_ = bf16[128,1152]{1,0:T(8,128)(2,1)S(1)} collective-permute-done((bf16[128,1152]{1,0:T(8,128)(2,1)}, bf16[128,1152]{1,0:T(8,128)(2,1)S(1)}, u32[]{:S(2)}, u32[]{:S(2)}) %collective-permute-start.8) | collective-permute-done | bytes 294944 | tf_op jit(solution)/shard_map/ppermute | solution.py:594
  94.0 6.8 %collective-permute-start.10 = (bf16[128,1152]{1,0:T(8,128)(2,1)S(1)}, bf16[128,1152]{1,0:T(8,128)(2,1)S(1)}, u32[]{:S(2)}, u32[]{:S(2)}) collective-permute-start(bf16[128,1152]{1,0:T(8,128)(2,1)S(1)} %get-tuple-element.112.refs_0_), channel_id=1, source_target_pairs={{0,1},{1,2},{2,3},{3,0},{4,5},{5,6},{6,7},{7,4},{8,9},{9,10},{10,1... | collective-permute-start | bytes 884744 | tf_op jit(solution)/shard_map/ppermute | solution.py:594
  103.2 7.8 %collective-permute-done.10.refs_1_ = bf16[128,1152]{1,0:T(8,128)(2,1)S(1)} collective-permute-done((bf16[128,1152]{1,0:T(8,128)(2,1)S(1)}, bf16[128,1152]{1,0:T(8,128)(2,1)S(1)}, u32[]{:S(2)}, u32[]{:S(2)}) %collective-permute-start.10) | collective-permute-done | bytes 294944 | tf_op jit(solution)/shard_map/ppermute | solution.py:594
  111.0 4.8 %collective-permute-done.12.refs_3_ = bf16[128,1152]{1,0:T(8,128)(2,1)S(1)} collective-permute-done((bf16[128,1152]{1,0:T(8,128)(2,1)S(1)}, bf16[128,1152]{1,0:T(8,128)(2,1)S(1)}, u32[]{:S(2)}, u32[]{:S(2)}) %collective-permute-start.12) | collective-permute-done | bytes 294944 | tf_op jit(solution)/shard_map/ppermute | solution.py:594
  118.0 15.6 %collective-permute-done.11.refs_2_ = bf16[128,1152]{1,0:T(8,128)(2,1)S(1)} collective-permute-done((bf16[128,1152]{1,0:T(8,128)(2,1)S(1)}, bf16[128,1152]{1,0:T(8,128)(2,1)S(1)}, u32[]{:S(2)}, u32[]{:S(2)}) %collective-permute-start.11) | collective-permute-done | bytes 294944 | tf_op jit(solution)/shard_map/ppermute | solution.py:594
  134.4 13.7 %shard_map.275 = (bf16[512,1152]{1,0:T(8,128)(2,1)}, bf16[512,1728]{1,0:T(8,128)(2,1)}, bf16[512,1728]{1,0:T(8,128)(2,1)}, bf16[512,1728]{1,0:T(8,128)(2,1)}, bf...) custom-call(bf16[128,1152]{1,0:T(8,128)(2,1)} %copy-done.9, ...), custom_call_target="tpu_custom_call" | custom-call | flops 1 | bytes 1 | tf_op jit(solution)/shard_map/pallas_call | solution.py:667
  148.2 2.4 collective-permute-start.15
  152.0 10.9 %all_to_all.25 = bf16[8,16,1152]{2,1,0:T(8,128)(2,1)S(1)} all-to-all(bf16[8,16,1152]{2,1,0:T(8,128)(2,1)S(1)} %bitcast.41), channel_id=1, replica_groups=mesh['wide'=8,'narrow'=4] {'wide'}, dimensions={0} | all-to-all | bytes 589824 | tf_op jit(solution)/shard_map/all_to_all | solution.py:603
  162.9 8.8 %collective-permute-done.15.refs_2_ = bf16[128,1152]{1,0:T(8,128)(2,1)S(1)} collective-permute-done((bf16[128,1152]{1,0:T(8,128)(2,1)}, bf16[128,1152]{1,0:T(8,128)(2,1)S(1)}, u32[]{:S(2)}, u32[]{:S(2)}) %collective-permute-start.15) | collective-permute-done | bytes 294944 | tf_op jit(solution)/shard_map/ppermute | solution.py:594
  172.7 3.0 shard_map.276
  176.3 5.9 %collective-permute-start.17 = (bf16[128,1152]{1,0:T(8,128)(2,1)S(1)}, bf16[128,1152]{1,0:T(8,128)(2,1)S(1)}, u32[]{:S(2)}, u32[]{:S(2)}) collective-permute-start(bf16[128,1152]{1,0:T(8,128)(2,1)S(1)} %get-tuple-element.125.refs_0_), channel_id=1, source_target_pairs={{0,1},{1,2},{2,3},{3,0},{4,5},{5,6},{6,7},{7,4},{8,9},{9,10},{10,1... | collective-permute-start | bytes 884744 | tf_op jit(solution)/shard_map/ppermute | solution.py:594
  184.6 5.1 %collective-permute-done.17.refs_1_ = bf16[128,1152]{1,0:T(8,128)(2,1)S(1)} collective-permute-done((bf16[128,1152]{1,0:T(8,128)(2,1)S(1)}, bf16[128,1152]{1,0:T(8,128)(2,1)S(1)}, u32[]{:S(2)}, u32[]{:S(2)}) %collective-permute-start.17) | collective-permute-done | bytes 294944 | tf_op jit(solution)/shard_map/ppermute | solution.py:594
  189.7 10.1 %collective-permute-done.18.refs_2_ = bf16[128,1152]{1,0:T(8,128)(2,1)S(1)} collective-permute-done((bf16[128,1152]{1,0:T(8,128)(2,1)S(1)}, bf16[128,1152]{1,0:T(8,128)(2,1)S(1)}, u32[]{:S(2)}, u32[]{:S(2)}) %collective-permute-start.18) | collective-permute-done | bytes 294944 | tf_op jit(solution)/shard_map/ppermute | solution.py:594
  201.2 15.4 %shard_map.277 = (bf16[512,1152]{1,0:T(8,128)(2,1)}, bf16[512,1728]{1,0:T(8,128)(2,1)}, bf16[512,1728]{1,0:T(8,128)(2,1)}, bf16[512,1152]{1,0:T(8,128)(2,1)}) custom-call(bf16[128,1152]{1,0:T(8,128)(2,1)} %copy-done.18, bf16[128,1152]{1,0:T(8,128)(2,1)} %copy-done.42, bf16[128,1152]{1,0:T(8,128)(2,1)} %copy-done.43, bf16[128,1152]{1,0:T(8,128)(2,1)} %copy-done.44, ...), custom_call_target="tpu_custom_call" | custom-call | flops 1 | bytes 1 | tf_op jit(solution)/shard_map/pallas_call | solution.py:699
  216.9 8.2 %shard_map.278 = (bf16[576,1728]{1,0:T(8,128)(2,1)}, bf16[576,1728]{1,0:T(8,128)(2,1)}, bf16[576,1728]{1,0:T(8,128)(2,1)}) custom-call(bf16[512,1152]{1,0:T(8,128)(2,1)} %get-tuple-element.129.refs_0_, bf16[512,1152]{1,0:T(8,128)(2,1)} %get-tuple-element.130.refs_1_, bf16[512,1728]{1,0:T(8,128)(2,1)} %get-tuple-element.131.refs_2_, ...), custom_call_target="tpu_custom_call" | custom-call | flops 1 | bytes 1 | tf_op jit(solution)/shard_map/pallas_call | solution.py:721
  225.6 3.9 %collective-permute-done.20.refs_5_ = bf16[576,1728]{1,0:T(8,128)(2,1)} collective-permute-done((bf16[576,1728]{1,0:T(8,128)(2,1)}, bf16[576,1728]{1,0:T(8,128)(2,1)}, u32[]{:S(2)}, u32[]{:S(2)}) %collective-permute-start.20) | collective-permute-done | bytes 1990688 | tf_op jit(solution)/shard_map/ppermute | solution.py:571
  229.5 3.0 collective-permute-done.21.refs_6_
  232.5 3.0 collective-permute-done.22.refs_7_
  235.4 11.2 %shard_map.279 = bf16[3,576,1728]{2,1,0:T(8,128)(2,1)} custom-call(bf16[512,1152]{1,0:T(8,128)(2,1)} %get-tuple-element.129.refs_0_, bf16[512,1152]{1,0:T(8,128)(2,1)} %get-tuple-element.130.refs_1_, bf16[512,1728]{1,0:T(8,128)(2,1)} %get-tuple-element.131.refs_2_, bf16[512,1728]{1,0:T(8,128)(2,1)} %get-tuple-element.132.refs_3_, ...), custom_call_target="tpu_custom_call" | custom-call | flops 1 | bytes 1 | tf_op jit(solution)/shard_map/pallas_call | solution.py:721
  246.6 6.6 %reduce-scatter.3.cloned.1.call-done.g_ref = bf16[1,128,1152]{2,1,0:T(8,128)(2,1)} async-done(((bf16[4,128,1152]{2,1,0:T(8,128)(2,1)}), bf16[1,128,1152]{2,1,0:T(8,128)(2,1)}) %reduce-scatter.3.cloned.1.call-update) | async-done | bytes 294928 | tf_op jit(solution)/shard_map/reduce_scatter | solution.py:714
  257.1 3.4 collective-permute-start.24
  260.8 3.7 all-to-all-start.2
  264.5 4.0 %collective-permute-done.23.refs_1_ = bf16[128,1152]{1,0:T(8,128)(2,1)S(1)} collective-permute-done((bf16[128,1152]{1,0:T(8,128)(2,1)S(1)}, bf16[128,1152]{1,0:T(8,128)(2,1)S(1)}, u32[]{:S(2)}, u32[]{:S(2)}) %collective-permute-start.23) | collective-permute-done | bytes 294944 | tf_op jit(solution)/shard_map/ppermute | solution.py:594
  268.5 12.2 %collective-permute-done.24.refs_2_ = bf16[128,1152]{1,0:T(8,128)(2,1)} collective-permute-done((bf16[128,1152]{1,0:T(8,128)(2,1)S(1)}, bf16[128,1152]{1,0:T(8,128)(2,1)}, u32[]{:S(2)}, u32[]{:S(2)}) %collective-permute-start.24) | collective-permute-done | bytes 294944 | tf_op jit(solution)/shard_map/ppermute | solution.py:594
  280.8 6.2 %shard_map.281 = (bf16[512,1152]{1,0:T(8,128)(2,1)}, bf16[512,768]{1,0:T(8,128)(2,1)}, f32[1,256]{1,0:T(1,128)}, bf16[128,768]{1,0:T(8,128)(2,1)}, bf16[128,768]...) custom-call(bf16[128,1152]{1,0:T(8,128)(2,1)} %copy-done.14, bf16[128,1152]{1,0:T(8,128)(2,1)} %copy-done.38, ...), custom_call_target="tpu_custom_call" | custom-call | flops 1 | bytes 1 | tf_op jit(solution)/shard_map/pallas_call | solution.py:740
  287.0 6.5 %collective-permute-start.26 = (bf16[128,768]{1,0:T(8,128)(2,1)}, bf16[128,768]{1,0:T(8,128)(2,1)S(1)}, u32[]{:S(2)}, u32[]{:S(2)}) collective-permute-start(bf16[128,768]{1,0:T(8,128)(2,1)} %get-tuple-element.158), channel_id=1, source_target_pairs={{0,1},{1,2},{2,3},{3,0},{4,5},{5,6},{6,7},{7,4},{8,9},{9,10},{10,1... | collective-permute-start | bytes 589832 | tf_op jit(solution)/shard_map/ppermute | solution.py:594
  302.6 4.7 %collective-permute-done.27.g2_ref = bf16[128,768]{1,0:T(8,128)(2,1)S(1)} collective-permute-done((bf16[128,768]{1,0:T(8,128)(2,1)}, bf16[128,768]{1,0:T(8,128)(2,1)S(1)}, u32[]{:S(2)}, u32[]{:S(2)}) %collective-permute-start.27) | collective-permute-done | bytes 196640 | tf_op jit(solution)/shard_map/ppermute | solution.py:594
  308.5 8.7 %shard_map.284 = (bf16[128,1152]{1,0:T(8,128)(2,1)}, bf16[576,1152]{1,0:T(8,128)(2,1)}, bf16[576,1152]{1,0:T(8,128)(2,1)}) custom-call(bf16[128,768]{1,0:T(8,128)(2,1)} %get-tuple-element.157.g0_ref, bf16[128,768]{1,0:T(8,128)(2,1)} %copy-done.45, bf16[128,768]{1,0:T(8,128)(2,1)} %copy-done.46, bf16[128,768]{1,0:T(8,128)(2,1)} %copy-done.47, ...), custom_call_target="tpu_custom_call" | custom-call | flops 1 | bytes 1 | tf_op jit(solution)/shard_map/pallas_call | solution.py:761
  317.3 3.3 collective-permute-done.30
  322.2 20.9 %all_to_all.26 = bf16[4,144,1152]{2,1,0:T(8,128)(2,1)S(1)} all-to-all(bf16[4,144,1152]{2,1,0:T(8,128)(2,1)S(1)} %bitcast.28), channel_id=1, replica_groups={{0,8,16,24},{4,12,20,28},{1,9,17,25},{5,13,21,29},{2,10,18,26},{6,14,22..., dimensions={0} | all-to-all | bytes 2654208 | tf_op jit(solution)/shard_map/all_to_all | solution.py:779
  344.1 4.7 %collective-permute-start.31 = (bf16[144,640]{1,0:T(8,128)(2,1)S(1)}, bf16[144,640]{1,0:T(8,128)(2,1)S(1)}, u32[]{:S(2)}, u32[]{:S(2)}) collective-permute-start(bf16[144,640]{1,0:T(8,128)(2,1)S(1)} %slice.49.refs_0_), channel_id=1, source_target_pairs={{0,1},{1,2},{2,3},{3,0},{4,5},{5,6},{6,7},{7,4},{8,9},{9,10},{10,1... | collective-permute-start | bytes 552968 | tf_op jit(solution)/shard_map/ppermute | solution.py:594
  348.7 2.8 collective-permute-start.32
  351.6 3.3 convert_element_type.20
  354.8 3.4 all-to-all-start.4
  358.3 3.5 slice_bitcast_fusion
  362.7 2.7 all-to-all-done.4
  (168 shorter events, 47.4 us)
Async XLA Ops:
  7.2 44.2 %all-gather.4.cloned.1.call-start = ((), (), s32[]{:S(2)}) async-start(), calls=%async_computation.7 | async-start | bytes 1658880 | tf_op jit(solution)/shard_map/all_gather | solution.py:566
  9.4 17.8 %collective-permute-start = (bf16[144,256]{1,0:T(8,128)(2,1)}, bf16[144,256]{1,0:T(8,128)(2,1)S(1)}, u32[]{:S(2)}, u32[]{:S(2)}) collective-permute-start(bf16[144,256]{1,0:T(8,128)(2,1)} %q_ref.1), channel_id=1, source_target_pairs={{0,1},{1,2},{2,3},{3,0},{4,5},{5,6},{6,7},{7,4},{8,9},{9,10},{10,1... | collective-permute-start | bytes 221192 | tf_op jit(solution)/shard_map/ppermute | solution.py:594
  12.4 14.7 %collective-permute-start.1 = (bf16[144,256]{1,0:T(8,128)(2,1)}, bf16[144,256]{1,0:T(8,128)(2,1)S(1)}, u32[]{:S(2)}, u32[]{:S(2)}) collective-permute-start(bf16[144,256]{1,0:T(8,128)(2,1)} %q_ref.1), channel_id=1, source_target_pairs={{0,2},{1,3},{2,0},{3,1},{4,6},{5,7},{6,4},{7,5},{8,10},{9,11},{10,... | collective-permute-start | bytes 221192 | tf_op jit(solution)/shard_map/ppermute | solution.py:594
  15.0 12.1 %collective-permute-start.2 = (bf16[144,256]{1,0:T(8,128)(2,1)}, bf16[144,256]{1,0:T(8,128)(2,1)S(1)}, u32[]{:S(2)}, u32[]{:S(2)}) collective-permute-start(bf16[144,256]{1,0:T(8,128)(2,1)} %q_ref.1), channel_id=1, source_target_pairs={{0,3},{1,0},{2,1},{3,2},{4,7},{5,4},{6,5},{7,6},{8,11},{9,8},{10,9... | collective-permute-start | bytes 221192 | tf_op jit(solution)/shard_map/ppermute | solution.py:594
  16.4 14.2 %all-to-all-start = ((bf16[8,16,1152]{2,1,0:T(8,128)(2,1)}), bf16[8,16,1152]{2,1,0:T(8,128)(2,1)S(1)}, u32[]{:S(2)}, u32[]{:S(2)}) async-start(bf16[8,16,1152]{2,1,0:T(8,128)(2,1)} %bitcast.40), calls=%async_computation | async-start | bytes 589824 | tf_op jit(solution)/shard_map/all_to_all | solution.py:603
  20.1 95.8 %all-gather.6.cloned.1.call-start = ((), (), s32[]{:S(2)}) async-start(), calls=%async_computation.8 | async-start | bytes 7741440 | tf_op jit(solution)/shard_map/all_gather | solution.py:566
  30.6 154.0 %all-gather.8.cloned.1.call-start = ((), (), s32[]{:S(2)}) async-start(), calls=%async_computation.9 | async-start | bytes 1474560 | tf_op jit(solution)/shard_map/all_gather | solution.py:566
  30.6 11.9 %collective-permute-start.3 = (bf16[128,1152]{1,0:T(8,128)(2,1)S(1)}, bf16[128,1152]{1,0:T(8,128)(2,1)S(1)}, u32[]{:S(2)}, u32[]{:S(2)}) collective-permute-start(bf16[128,1152]{1,0:T(8,128)(2,1)S(1)} %bitcast.29), channel_id=1, source_target_pairs={{0,1},{1,2},{2,3},{3,0},{4,5},{5,6},{6,7},{7,4},{8,9},{9,10},{10,1... | collective-permute-start | bytes 884744 | tf_op jit(solution)/shard_map/ppermute | solution.py:594
  31.1 20.4 %collective-permute-start.4 = (bf16[128,1152]{1,0:T(8,128)(2,1)S(1)}, bf16[128,1152]{1,0:T(8,128)(2,1)S(1)}, u32[]{:S(2)}, u32[]{:S(2)}) collective-permute-start(bf16[128,1152]{1,0:T(8,128)(2,1)S(1)} %bitcast.30), channel_id=1, source_target_pairs={{0,2},{1,3},{2,0},{3,1},{4,6},{5,7},{6,4},{7,5},{8,10},{9,11},{10,... | collective-permute-start | bytes 884744 | tf_op jit(solution)/shard_map/ppermute | solution.py:594
  31.1 20.4 %collective-permute-start.5 = (bf16[128,1152]{1,0:T(8,128)(2,1)S(1)}, bf16[128,1152]{1,0:T(8,128)(2,1)S(1)}, u32[]{:S(2)}, u32[]{:S(2)}) collective-permute-start(bf16[128,1152]{1,0:T(8,128)(2,1)S(1)} %bitcast.31), channel_id=1, source_target_pairs={{0,3},{1,0},{2,1},{3,2},{4,7},{5,4},{6,5},{7,6},{8,11},{9,8},{10,9... | collective-permute-start | bytes 884744 | tf_op jit(solution)/shard_map/ppermute | solution.py:594
  51.4 3.3 collective-permute-start.6
  55.9 60.0 %copy-start.40 = (bf16[144,256]{1,0:T(8,128)(2,1)S(1)}, bf16[144,256]{1,0:T(8,128)(2,1)}, u32[]{:S(2)}) copy-start(bf16[144,256]{1,0:T(8,128)(2,1)} %q_ref.1) | copy-start | bytes 221188
  64.7 13.9 %collective-permute-start.7 = (bf16[128,1152]{1,0:T(8,128)(2,1)}, bf16[128,1152]{1,0:T(8,128)(2,1)S(1)}, u32[]{:S(2)}, u32[]{:S(2)}) collective-permute-start(bf16[128,1152]{1,0:T(8,128)(2,1)} %get-tuple-element.107), channel_id=1, source_target_pairs={{0,1},{1,2},{2,3},{3,0},{4,5},{5,6},{6,7},{7,4},{8,9},{9,10},{10,1... | collective-permute-start | bytes 884744 | tf_op jit(solution)/shard_map/ppermute | solution.py:594
  70.8 19.7 %collective-permute-start.8 = (bf16[128,1152]{1,0:T(8,128)(2,1)}, bf16[128,1152]{1,0:T(8,128)(2,1)S(1)}, u32[]{:S(2)}, u32[]{:S(2)}) collective-permute-start(bf16[128,1152]{1,0:T(8,128)(2,1)} %get-tuple-element.108), channel_id=1, source_target_pairs={{0,2},{1,3},{2,0},{3,1},{4,6},{5,7},{6,4},{7,5},{8,10},{9,11},{10,... | collective-permute-start | bytes 884744 | tf_op jit(solution)/shard_map/ppermute | solution.py:594
  70.8 19.7 %collective-permute-start.9 = (bf16[128,1152]{1,0:T(8,128)(2,1)}, bf16[128,1152]{1,0:T(8,128)(2,1)S(1)}, u32[]{:S(2)}, u32[]{:S(2)}) collective-permute-start(bf16[128,1152]{1,0:T(8,128)(2,1)} %get-tuple-element.109), channel_id=1, source_target_pairs={{0,3},{1,0},{2,1},{3,2},{4,7},{5,4},{6,5},{7,6},{8,11},{9,8},{10,9... | collective-permute-start | bytes 884744 | tf_op jit(solution)/shard_map/ppermute | solution.py:594
  94.0 39.7 %copy-start.9 = (bf16[128,1152]{1,0:T(8,128)(2,1)}, bf16[128,1152]{1,0:T(8,128)(2,1)S(1)}, u32[]{:S(2)}) copy-start(bf16[128,1152]{1,0:T(8,128)(2,1)S(1)} %get-tuple-element.112.refs_0_) | copy-start | bytes 884740
  94.0 17.1 %collective-permute-start.10 = (bf16[128,1152]{1,0:T(8,128)(2,1)S(1)}, bf16[128,1152]{1,0:T(8,128)(2,1)S(1)}, u32[]{:S(2)}, u32[]{:S(2)}) collective-permute-start(bf16[128,1152]{1,0:T(8,128)(2,1)S(1)} %get-tuple-element.112.refs_0_), channel_id=1, source_target_pairs={{0,1},{1,2},{2,3},{3,0},{4,5},{5,6},{6,7},{7,4},{8,9},{9,10},{10,1... | collective-permute-start | bytes 884744 | tf_op jit(solution)/shard_map/ppermute | solution.py:594
  100.8 15.1 %collective-permute-start.12 = (bf16[128,1152]{1,0:T(8,128)(2,1)S(1)}, bf16[128,1152]{1,0:T(8,128)(2,1)S(1)}, u32[]{:S(2)}, u32[]{:S(2)}) collective-permute-start(bf16[128,1152]{1,0:T(8,128)(2,1)S(1)} %get-tuple-element.112.refs_0_), channel_id=1, source_target_pairs={{0,3},{1,0},{2,1},{3,2},{4,7},{5,4},{6,5},{7,6},{8,11},{9,8},{10,9... | collective-permute-start | bytes 884744 | tf_op jit(solution)/shard_map/ppermute | solution.py:594
  115.9 17.8 %collective-permute-start.13 = (bf16[3,576,1728]{2,1,0:T(8,128)(2,1)}, bf16[3,576,1728]{2,1,0:T(8,128)(2,1)}, u32[]{:S(2)}, u32[]{:S(2)}) collective-permute-start(bf16[3,576,1728]{2,1,0:T(8,128)(2,1)} %all-gather.6.cloned.1.call-done.refs_4_.refs_6_), channel_id=1, source_target_pairs={{0,4},{4,0},{8,12},{12,8},{16,20},{20,16},{24,28},{28,24},{1,5},{5... | collective-permute-start | bytes 17915912 | tf_op jit(solution)/shard_map/ppermute | solution.py:571
  116.7 35.3 %copy-start.41 = (bf16[8,1,16,1152]{3,2,1,0:T(8,128)(2,1)S(1)}, bf16[8,1,16,1152]{3,2,1,0:T(8,128)(2,1)}, u32[]{:S(2)}) copy-start(bf16[8,1,16,1152]{3,2,1,0:T(8,128)(2,1)} %param.17) | copy-start | bytes 884740
  116.7 55.0 %copy-start.8 = (f32[8,1152]{1,0:T(8,128)S(1)}, f32[8,1152]{1,0:T(8,128)}, u32[]{:S(2)}) copy-start(f32[8,1152]{1,0:T(8,128)} %get-tuple-element.111.refs_5_.refs_8_.gains_ref) | copy-start | bytes 110596
  116.8 55.0 %copy-start.20 = (s32[1,1152]{1,0:T(1,128)S(1)}, s32[1,1152]{1,0:T(1,128)}, u32[]{:S(2)}) copy-start(s32[1,1152]{1,0:T(1,128)} %get-tuple-element.121.refs_6_.order_ref) | copy-start | bytes 13828
  116.8 54.9 %copy-start.25 = (s32[5]{0:T(128)S(1)}, s32[5]{0:T(128)}, u32[]{:S(2)}) copy-start(s32[5]{0:T(128)} %copy-done.24) | copy-start | bytes 64
  116.8 136.4 %reduce-scatter.3.cloned.1.call-start = ((), (), s32[]{:S(2)}) async-start(), calls=%async_computation.10 | async-start | bytes 1474560 | tf_op jit(solution)/shard_map/reduce_scatter | solution.py:714
  117.0 16.7 %collective-permute-start.11 = (bf16[128,1152]{1,0:T(8,128)(2,1)S(1)}, bf16[128,1152]{1,0:T(8,128)(2,1)S(1)}, u32[]{:S(2)}, u32[]{:S(2)}) collective-permute-start(bf16[128,1152]{1,0:T(8,128)(2,1)S(1)} %get-tuple-element.112.refs_0_), channel_id=1, source_target_pairs={{0,2},{1,3},{2,0},{3,1},{4,6},{5,7},{6,4},{7,5},{8,10},{9,11},{10,... | collective-permute-start | bytes 884744 | tf_op jit(solution)/shard_map/ppermute | solution.py:594
  148.1 14.8 %collective-permute-start.14 = (bf16[128,1152]{1,0:T(8,128)(2,1)}, bf16[128,1152]{1,0:T(8,128)(2,1)S(1)}, u32[]{:S(2)}, u32[]{:S(2)}) collective-permute-start(bf16[128,1152]{1,0:T(8,128)(2,1)} %get-tuple-element.116), channel_id=1, source_target_pairs={{0,1},{1,2},{2,3},{3,0},{4,5},{5,6},{6,7},{7,4},{8,9},{9,10},{10,1... | collective-permute-start | bytes 884744 | tf_op jit(solution)/shard_map/ppermute | solution.py:594
  148.2 23.5 %collective-permute-start.15 = (bf16[128,1152]{1,0:T(8,128)(2,1)}, bf16[128,1152]{1,0:T(8,128)(2,1)S(1)}, u32[]{:S(2)}, u32[]{:S(2)}) collective-permute-start(bf16[128,1152]{1,0:T(8,128)(2,1)} %get-tuple-element.117), channel_id=1, source_target_pairs={{0,2},{1,3},{2,0},{3,1},{4,6},{5,7},{6,4},{7,5},{8,10},{9,11},{10,... | collective-permute-start | bytes 884744 | tf_op jit(solution)/shard_map/ppermute | solution.py:594
  150.6 21.1 %collective-permute-start.16 = (bf16[128,1152]{1,0:T(8,128)(2,1)}, bf16[128,1152]{1,0:T(8,128)(2,1)S(1)}, u32[]{:S(2)}, u32[]{:S(2)}) collective-permute-start(bf16[128,1152]{1,0:T(8,128)(2,1)} %get-tuple-element.118), channel_id=1, source_target_pairs={{0,3},{1,0},{2,1},{3,2},{4,7},{5,4},{6,5},{7,6},{8,11},{9,8},{10,9... | collective-permute-start | bytes 884744 | tf_op jit(solution)/shard_map/ppermute | solution.py:594
  176.3 13.4 %collective-permute-start.17 = (bf16[128,1152]{1,0:T(8,128)(2,1)S(1)}, bf16[128,1152]{1,0:T(8,128)(2,1)S(1)}, u32[]{:S(2)}, u32[]{:S(2)}) collective-permute-start(bf16[128,1152]{1,0:T(8,128)(2,1)S(1)} %get-tuple-element.125.refs_0_), channel_id=1, source_target_pairs={{0,1},{1,2},{2,3},{3,0},{4,5},{5,6},{6,7},{7,4},{8,9},{9,10},{10,1... | collective-permute-start | bytes 884744 | tf_op jit(solution)/shard_map/ppermute | solution.py:594
  182.2 17.6 %collective-permute-start.18 = (bf16[128,1152]{1,0:T(8,128)(2,1)S(1)}, bf16[128,1152]{1,0:T(8,128)(2,1)S(1)}, u32[]{:S(2)}, u32[]{:S(2)}) collective-permute-start(bf16[128,1152]{1,0:T(8,128)(2,1)S(1)} %get-tuple-element.125.refs_0_), channel_id=1, source_target_pairs={{0,2},{1,3},{2,0},{3,1},{4,6},{5,7},{6,4},{7,5},{8,10},{9,11},{10,... | collective-permute-start | bytes 884744 | tf_op jit(solution)/shard_map/ppermute | solution.py:594
  182.2 18.3 %collective-permute-start.19 = (bf16[128,1152]{1,0:T(8,128)(2,1)S(1)}, bf16[128,1152]{1,0:T(8,128)(2,1)S(1)}, u32[]{:S(2)}, u32[]{:S(2)}) collective-permute-start(bf16[128,1152]{1,0:T(8,128)(2,1)S(1)} %get-tuple-element.125.refs_0_), channel_id=1, source_target_pairs={{0,3},{1,0},{2,1},{3,2},{4,7},{5,4},{6,5},{7,6},{8,11},{9,8},{10,9... | collective-permute-start | bytes 884744 | tf_op jit(solution)/shard_map/ppermute | solution.py:594
  216.6 127.5 %reduce-scatter.5.cloned.1.call-start = ((), (), s32[]{:S(2)}) async-start(), calls=%async_computation.11 | async-start | bytes 7741440 | tf_op jit(solution)/shard_map/reduce_scatter | solution.py:577
  225.1 4.5 %collective-permute-start.20 = (bf16[576,1728]{1,0:T(8,128)(2,1)}, bf16[576,1728]{1,0:T(8,128)(2,1)}, u32[]{:S(2)}, u32[]{:S(2)}) collective-permute-start(bf16[576,1728]{1,0:T(8,128)(2,1)} %get-tuple-element.134), channel_id=1, source_target_pairs={{0,4},{4,0},{8,12},{12,8},{16,20},{20,16},{24,28},{28,24},{1,5},{5... | collective-permute-start | bytes 5971976 | tf_op jit(solution)/shard_map/ppermute | solution.py:571
  225.1 7.4 %collective-permute-start.21 = (bf16[576,1728]{1,0:T(8,128)(2,1)}, bf16[576,1728]{1,0:T(8,128)(2,1)}, u32[]{:S(2)}, u32[]{:S(2)}) collective-permute-start(bf16[576,1728]{1,0:T(8,128)(2,1)} %get-tuple-element.135), channel_id=1, source_target_pairs={{0,4},{4,0},{8,12},{12,8},{16,20},{20,16},{24,28},{28,24},{1,5},{5... | collective-permute-start | bytes 5971976 | tf_op jit(solution)/shard_map/ppermute | solution.py:571
  225.6 9.8 %collective-permute-start.22 = (bf16[576,1728]{1,0:T(8,128)(2,1)}, bf16[576,1728]{1,0:T(8,128)(2,1)}, u32[]{:S(2)}, u32[]{:S(2)}) collective-permute-start(bf16[576,1728]{1,0:T(8,128)(2,1)} %get-tuple-element.136), channel_id=1, source_target_pairs={{0,4},{4,0},{8,12},{12,8},{16,20},{20,16},{24,28},{28,24},{1,5},{5... | collective-permute-start | bytes 5971976 | tf_op jit(solution)/shard_map/ppermute | solution.py:571
  256.7 50.6 %collective-permute-start.29 = (bf16[4,576,256]{2,1,0:T(8,128)(2,1)S(1)}, bf16[4,576,256]{2,1,0:T(8,128)(2,1)S(1)}, u32[]{:S(2)}, u32[]{:S(2)}) collective-permute-start(bf16[4,576,256]{2,1,0:T(8,128)(2,1)S(1)} %copy-done.27), channel_id=1, source_target_pairs={{0,4},{4,0},{8,12},{12,8},{16,20},{20,16},{24,28},{28,24},{1,5},{5... | collective-permute-start | bytes 3538952 | tf_op jit(solution)/shard_map/ppermute | solution.py:571
  256.7 11.8 %collective-permute-start.23 = (bf16[128,1152]{1,0:T(8,128)(2,1)S(1)}, bf16[128,1152]{1,0:T(8,128)(2,1)S(1)}, u32[]{:S(2)}, u32[]{:S(2)}) collective-permute-start(bf16[128,1152]{1,0:T(8,128)(2,1)S(1)} %get-tuple-element.140.refs_0_), channel_id=1, source_target_pairs={{0,1},{1,2},{2,3},{3,0},{4,5},{5,6},{6,7},{7,4},{8,9},{9,10},{10,1... | collective-permute-start | bytes 884744 | tf_op jit(solution)/shard_map/ppermute | solution.py:594
  257.1 23.7 %collective-permute-start.24 = (bf16[128,1152]{1,0:T(8,128)(2,1)S(1)}, bf16[128,1152]{1,0:T(8,128)(2,1)}, u32[]{:S(2)}, u32[]{:S(2)}) collective-permute-start(bf16[128,1152]{1,0:T(8,128)(2,1)S(1)} %get-tuple-element.140.refs_0_), channel_id=1, source_target_pairs={{0,2},{1,3},{2,0},{3,1},{4,6},{5,7},{6,4},{7,5},{8,10},{9,11},{10,... | collective-permute-start | bytes 884744 | tf_op jit(solution)/shard_map/ppermute | solution.py:594
  260.5 20.3 %collective-permute-start.25 = (bf16[128,1152]{1,0:T(8,128)(2,1)S(1)}, bf16[128,1152]{1,0:T(8,128)(2,1)}, u32[]{:S(2)}, u32[]{:S(2)}) collective-permute-start(bf16[128,1152]{1,0:T(8,128)(2,1)S(1)} %get-tuple-element.140.refs_0_), channel_id=1, source_target_pairs={{0,3},{1,0},{2,1},{3,2},{4,7},{5,4},{6,5},{7,6},{8,11},{9,8},{10,9... | collective-permute-start | bytes 884744 | tf_op jit(solution)/shard_map/ppermute | solution.py:594
  260.8 41.8 %all-to-all-start.2 = ((bf16[8,16,1152]{2,1,0:T(8,128)(2,1)}), bf16[8,16,1152]{2,1,0:T(8,128)(2,1)S(1)}, u32[]{:S(2)}, u32[]{:S(2)}) async-start(bf16[8,16,1152]{2,1,0:T(8,128)(2,1)} %bitcast.11), calls=%async_computation.2 | async-start | bytes 589824 | tf_op jit(solution)/shard_map/all_to_all | solution.py:608
  287.0 15.6 %collective-permute-start.26 = (bf16[128,768]{1,0:T(8,128)(2,1)}, bf16[128,768]{1,0:T(8,128)(2,1)S(1)}, u32[]{:S(2)}, u32[]{:S(2)}) collective-permute-start(bf16[128,768]{1,0:T(8,128)(2,1)} %get-tuple-element.158), channel_id=1, source_target_pairs={{0,1},{1,2},{2,3},{3,0},{4,5},{5,6},{6,7},{7,4},{8,9},{9,10},{10,1... | collective-permute-start | bytes 589832 | tf_op jit(solution)/shard_map/ppermute | solution.py:594
  293.5 13.8 %collective-permute-start.27 = (bf16[128,768]{1,0:T(8,128)(2,1)}, bf16[128,768]{1,0:T(8,128)(2,1)S(1)}, u32[]{:S(2)}, u32[]{:S(2)}) collective-permute-start(bf16[128,768]{1,0:T(8,128)(2,1)} %get-tuple-element.159), channel_id=1, source_target_pairs={{0,2},{1,3},{2,0},{3,1},{4,6},{5,7},{6,4},{7,5},{8,10},{9,11},{10,... | collective-permute-start | bytes 589832 | tf_op jit(solution)/shard_map/ppermute | solution.py:594
  294.4 12.9 %collective-permute-start.28 = (bf16[128,768]{1,0:T(8,128)(2,1)}, bf16[128,768]{1,0:T(8,128)(2,1)S(1)}, u32[]{:S(2)}, u32[]{:S(2)}) collective-permute-start(bf16[128,768]{1,0:T(8,128)(2,1)} %get-tuple-element.160), channel_id=1, source_target_pairs={{0,3},{1,0},{2,1},{3,2},{4,7},{5,4},{6,5},{7,6},{8,11},{9,8},{10,9... | collective-permute-start | bytes 589832 | tf_op jit(solution)/shard_map/ppermute | solution.py:594
  317.2 3.3 collective-permute-start.30
  344.1 17.7 %collective-permute-start.31 = (bf16[144,640]{1,0:T(8,128)(2,1)S(1)}, bf16[144,640]{1,0:T(8,128)(2,1)S(1)}, u32[]{:S(2)}, u32[]{:S(2)}) collective-permute-start(bf16[144,640]{1,0:T(8,128)(2,1)S(1)} %slice.49.refs_0_), channel_id=1, source_target_pairs={{0,1},{1,2},{2,3},{3,0},{4,5},{5,6},{6,7},{7,4},{8,9},{9,10},{10,1... | collective-permute-start | bytes 552968 | tf_op jit(solution)/shard_map/ppermute | solution.py:594
  348.7 14.0 %collective-permute-start.32 = (bf16[144,640]{1,0:T(8,128)(2,1)S(1)}, bf16[144,640]{1,0:T(8,128)(2,1)S(1)}, u32[]{:S(2)}, u32[]{:S(2)}) collective-permute-start(bf16[144,640]{1,0:T(8,128)(2,1)S(1)} %slice.49.refs_0_), channel_id=1, source_target_pairs={{0,2},{1,3},{2,0},{3,1},{4,6},{5,7},{6,4},{7,5},{8,10},{9,11},{10,... | collective-permute-start | bytes 552968 | tf_op jit(solution)/shard_map/ppermute | solution.py:594
  351.6 11.2 %collective-permute-start.33 = (bf16[144,640]{1,0:T(8,128)(2,1)S(1)}, bf16[144,640]{1,0:T(8,128)(2,1)S(1)}, u32[]{:S(2)}, u32[]{:S(2)}) collective-permute-start(bf16[144,640]{1,0:T(8,128)(2,1)S(1)} %slice.49.refs_0_), channel_id=1, source_target_pairs={{0,3},{1,0},{2,1},{3,2},{4,7},{5,4},{6,5},{7,6},{8,11},{9,8},{10,9... | collective-permute-start | bytes 552968 | tf_op jit(solution)/shard_map/ppermute | solution.py:594
  354.8 10.6 %all-to-all-start.4 = ((bf16[8,16,1152]{2,1,0:T(8,128)(2,1)}), bf16[8,16,1152]{2,1,0:T(8,128)(2,1)S(1)}, u32[]{:S(2)}, u32[]{:S(2)}) async-start(bf16[8,16,1152]{2,1,0:T(8,128)(2,1)} %bitcast.19), calls=%async_computation.6 | async-start | bytes 589824 | tf_op jit(solution)/shard_map/all_to_all | solution.py:608
  (43 other events, 278.9 us)
Sparse Core Ops, SparseCore 0:
  10.5 31.9 all-gather.3
  44.4 69.3 all-gather.5
  116.9 27.6 all-gather.7
  216.8 36.3 reduce-scatter.2
  256.1 71.2 reduce-scatter.4

commit v5 on v4

--- a/solution.py
+++ b/solution.py
@@ -359,7 +359,7 @@
 
 def ffn_backward(*refs):
     fa_ref, fb_ref, wm_ref, wo_ref = refs[RING : RING + 4]
-    slot_ref, dm_ref, dg_ref, du_ref, part_ref, w_ref, sem = refs[RING + 4 :]
+    slot_ref, dm_ref, dg_ref, du_ref, out_ref, part_ref, w_ref, sem = refs[RING + 4 :]
     waits = load_weights((wm_ref, wo_ref), w_ref, sem, (2, 0, 1))
     for s in range(RING):
         n = refs[s].shape[0]
@@ -374,11 +374,9 @@
     waits[2]()
     for d, n in tiles(part_ref.shape[1], 384):
         part = mm_nt(dg_ref[...], w_ref[0, pl.ds(d, n), :])
-        part = (part + mm_nt(du_ref[...], w_ref[1, pl.ds(d, n), :])).astype(BF16)
-        for s in range(RING):
-            m = refs[s].shape[0]
-            at = pl.multiple_of(lax.rem(slot_ref[0] + RING - s, RING) * m, m)
-            part_ref[pl.ds(at, m), pl.ds(d, n)] = part[s * m : (s + 1) * m]
+        part_ref[:, pl.ds(d, n)] = (part + mm_nt(du_ref[...], w_ref[1, pl.ds(d, n), :])).astype(BF16)
+    n = refs[0].shape[0]
+    collect([part_ref.at[pl.ds(s * n, n)] for s in range(RING)], slot_ref[0], out_ref)
 
 
 def weight_grad(left_ref, right_ref, own_ref, other_ref, turned_ref):
@@ -438,10 +436,12 @@
 def attention_backward(*refs):
     (
         slot_ref, wout_ref, qraw_ref, q_ref, k_ref, v_ref, probs_ref, hgain_ref, cos_ref, sin_ref,
-        dz_ref, part_ref, term_ref, *out_refs, datt_ref, ds_ref,
+        dz_out, dq_ref, term_ref, *out_refs, part_ref, dz_ref, datt_ref, ds_ref, sem,
     ) = refs[RING:]
     rows, head = q_ref.shape
     collect(refs[:RING], slot_ref[0], dz_ref)
+    leaving = pltpu.make_async_copy(dz_ref, dz_out, sem.at[0])
+    leaving.start()
     datt_ref[...] = mm(dz_ref[...], wout_ref[...]).astype(BF16)
     term = jnp.zeros((1, head), F32)
     for r, n in tiles(rows, 128):
@@ -459,6 +459,8 @@
     part_ref[:, head : 2 * head] = (mm_tn(ds_ref[...], q_ref[...]) * SCALE).astype(BF16)
     part_ref[:, 2 * head :] = mm_tn(probs_ref[...].astype(BF16), datt_ref[...]).astype(BF16)
     hand_out(part_ref, slot_ref[0], out_refs)
+    dq_ref[...] = part_ref[:, :head]
+    leaving.wait()
 
 
 def last_rows(
@@ -700,7 +702,7 @@
             ffn_backward,
             [((narrow * part, width), bf)] + [((narrow * part, units), bf)] * 2
             + [((narrow * part, width), bf)],
-            scratch=[f_scratch, sem((6,))],
+            scratch=[pltpu.VMEM((rows, width), bf), f_scratch, sem((6,))],
             anys=(narrow + 2, narrow + 3), smem=(narrow + 4,), count=narrow + 5,
             flops=3 * 10**9, moved=16 * 10**6,
         )(*dm[c], fa[c], fb[c], wf_mine, wf_other, slots)
@@ -737,12 +739,15 @@
     )(dxn2, d_out[0], h, mixed, gains)
     dz = gather_ring(dz_own)
     wh_other = sibling(after(wh_mine, dz_own))
-    dz_all, joined_part, query_term, *joined = call(
+    dz_all, dq_raw, query_term, *joined = call(
         attention_backward,
-        [((rows, width), bf), ((rows, 3 * head), bf), ((1, head), ff)]
+        [((rows, width), bf), ((rows, head), bf), ((1, head), ff)]
         + [((quarter, 3 * head), bf)] * narrow,
-        scratch=[pltpu.VMEM((rows, head), bf), pltpu.VMEM((rows, rows), bf)],
-        smem=(narrow,), count=narrow + 10, flops=2 * 10**9, moved=6 * 10**6,
+        scratch=[
+            pltpu.VMEM((rows, 3 * head), bf), pltpu.VMEM((rows, width), bf),
+            pltpu.VMEM((rows, head), bf), pltpu.VMEM((rows, rows), bf), sem((1,)),
+        ],
+        smem=(narrow,), count=narrow + 10, far=1, flops=2 * 10**9, moved=6 * 10**6,
     )(*dz, slots, wout, qraw, q, k, v, probs, hgain, cosine, sine)
     joined = pass_on(joined)
 
@@ -754,7 +759,7 @@
             count=2, flops=2 * width * left.shape[0] * columns, moved=3 * 10**6,
         )(left, right)
 
-    g_query = outer(xn1, joined_part, head)
+    g_query = outer(xn1, dq_raw, head)
     g_outproj = outer(dz_all, attended, head)
     joined[0] = after(joined[0], left_out, *g_query, *g_outproj)
     heads = wh_mine.shape[0]

time: 382 us -> 382 us (level)
  no operation moved by 1% of the time
where the time goes in v5:
time: 382 us; the launch traced here: 375 us
  waiting for transfers between devices  140 us (37%)
  Pallas kernels  81.7 us (21%)
  starting transfers between devices  74.7 us (20%)
  blocking collectives  31.8 us (8%)
  local copies, waits for them, and re-layouts  23.8 us (6%)
  between operations  16 us (4%)
  other arithmetic  7.29 us (2%)
    ppermute x27, waiting for transfers between devices, pass_on(): got.append(lax.ppermute(parts[s], 'narrow', shift))  110 us
    ppermute x27, starting transfers between devices, pass_on(): got.append(lax.ppermute(parts[s], 'narrow', shift))  62.7 us
    all_to_all x1, blocking collectives, scatter_chips(): lax.all_to_all(parts, 'wide', split_axis=0, concat_axis=0, tiled=True, ax...  20.9 us
    pallas_call x2, Pallas kernels, ffn_grads(): call(functools.partial(ffn_weight_grads, first), outs, scratch=[pltpu.VME...  19.3 us
    unnamed x100, local copies, waits for them, and re-layouts  18.2 us
    ppermute x7, waiting for transfers between devices, sibling(): return lax.ppermute(value, 'wide', swap)  16.4 us
    pallas_call x1, Pallas kernels, ffn_back(): call(ffn_backward, [((narrow * part, width), bf)] + [((narrow * part, uni...  15.5 us
    pallas_call x1, Pallas kernels, ffn_ahead(): call(ffn_forward, [((narrow * part, width), bf)] + [((narrow * part, unit...  13.7 us
  transfers between devices with their start and end apart: 42, of which 23 were waited for; matrix products, arithmetic and copies ran while one was open for 3% of the time, Pallas kernels for 17%

profile of v5, /device:TPU:0, one launch (start us, length us, event | category | flops | bytes accessed | tf_op | source)
XLA Modules:
  0.0 374.8 jit_solution(7012535626269718007)
XLA Ops:
  9.4 3.1 collective-permute-start
  12.4 2.6 collective-permute-start.1
  16.4 3.7 all-to-all-start
  27.1 3.4 all-to-all-done
  31.1 3.5 collective-permute-start.5
  34.5 8.0 %collective-permute-done.3.refs_1_ = bf16[128,1152]{1,0:T(8,128)(2,1)S(1)} collective-permute-done((bf16[128,1152]{1,0:T(8,128)(2,1)S(1)}, bf16[128,1152]{1,0:T(8,128)(2,1)S(1)}, u32[]{:S(2)}, u32[]{:S(2)}) %collective-permute-start.3) | collective-permute-done | bytes 294944 | tf_op jit(solution)/shard_map/ppermute | solution.py:596
  42.5 8.9 %collective-permute-done.4.refs_2_ = bf16[128,1152]{1,0:T(8,128)(2,1)S(1)} collective-permute-done((bf16[128,1152]{1,0:T(8,128)(2,1)S(1)}, bf16[128,1152]{1,0:T(8,128)(2,1)S(1)}, u32[]{:S(2)}, u32[]{:S(2)}) %collective-permute-start.4) | collective-permute-done | bytes 294944 | tf_op jit(solution)/shard_map/ppermute | solution.py:596
  51.5 3.3 collective-permute-done.6.refs_4_
  55.9 8.8 %shard_map.273 = (bf16[512,1152]{1,0:T(8,128)(2,1)}, bf16[512,1152]{1,0:T(8,128)(2,1)}, f32[512,256]{1,0:T(8,128)}, f32[512,256]{1,0:T(8,128)}, f32[512,512]{1,0...) custom-call(bf16[128,1152]{1,0:T(8,128)(2,1)} %bitcast.32, ...), custom_call_target="tpu_custom_call" | custom-call | flops 1 | bytes 1 | tf_op jit(solution)/shard_map/pallas_call | solution.py:645
  64.7 6.2 %collective-permute-start.7 = (bf16[128,1152]{1,0:T(8,128)(2,1)}, bf16[128,1152]{1,0:T(8,128)(2,1)S(1)}, u32[]{:S(2)}, u32[]{:S(2)}) collective-permute-start(bf16[128,1152]{1,0:T(8,128)(2,1)} %get-tuple-element.107), channel_id=1, source_target_pairs={{0,1},{1,2},{2,3},{3,0},{4,5},{5,6},{6,7},{7,4},{8,9},{9,10},{10,1... | collective-permute-start | bytes 884744 | tf_op jit(solution)/shard_map/ppermute | solution.py:596
  70.9 2.4 collective-permute-start.9
  73.3 5.2 %collective-permute-done.7.refs_1_ = bf16[128,1152]{1,0:T(8,128)(2,1)S(1)} collective-permute-done((bf16[128,1152]{1,0:T(8,128)(2,1)}, bf16[128,1152]{1,0:T(8,128)(2,1)S(1)}, u32[]{:S(2)}, u32[]{:S(2)}) %collective-permute-start.7) | collective-permute-done | bytes 294944 | tf_op jit(solution)/shard_map/ppermute | solution.py:596
  78.6 12.1 %collective-permute-done.8.refs_2_ = bf16[128,1152]{1,0:T(8,128)(2,1)S(1)} collective-permute-done((bf16[128,1152]{1,0:T(8,128)(2,1)}, bf16[128,1152]{1,0:T(8,128)(2,1)S(1)}, u32[]{:S(2)}, u32[]{:S(2)}) %collective-permute-start.8) | collective-permute-done | bytes 294944 | tf_op jit(solution)/shard_map/ppermute | solution.py:596
  94.0 6.8 %collective-permute-start.10 = (bf16[128,1152]{1,0:T(8,128)(2,1)S(1)}, bf16[128,1152]{1,0:T(8,128)(2,1)S(1)}, u32[]{:S(2)}, u32[]{:S(2)}) collective-permute-start(bf16[128,1152]{1,0:T(8,128)(2,1)S(1)} %get-tuple-element.112.refs_0_), channel_id=1, source_target_pairs={{0,1},{1,2},{2,3},{3,0},{4,5},{5,6},{6,7},{7,4},{8,9},{9,10},{10,1... | collective-permute-start | bytes 884744 | tf_op jit(solution)/shard_map/ppermute | solution.py:596
  103.2 7.8 %collective-permute-done.10.refs_1_ = bf16[128,1152]{1,0:T(8,128)(2,1)S(1)} collective-permute-done((bf16[128,1152]{1,0:T(8,128)(2,1)S(1)}, bf16[128,1152]{1,0:T(8,128)(2,1)S(1)}, u32[]{:S(2)}, u32[]{:S(2)}) %collective-permute-start.10) | collective-permute-done | bytes 294944 | tf_op jit(solution)/shard_map/ppermute | solution.py:596
  111.1 4.8 %collective-permute-done.12.refs_3_ = bf16[128,1152]{1,0:T(8,128)(2,1)S(1)} collective-permute-done((bf16[128,1152]{1,0:T(8,128)(2,1)S(1)}, bf16[128,1152]{1,0:T(8,128)(2,1)S(1)}, u32[]{:S(2)}, u32[]{:S(2)}) %collective-permute-start.12) | collective-permute-done | bytes 294944 | tf_op jit(solution)/shard_map/ppermute | solution.py:596
  118.1 15.6 %collective-permute-done.11.refs_2_ = bf16[128,1152]{1,0:T(8,128)(2,1)S(1)} collective-permute-done((bf16[128,1152]{1,0:T(8,128)(2,1)S(1)}, bf16[128,1152]{1,0:T(8,128)(2,1)S(1)}, u32[]{:S(2)}, u32[]{:S(2)}) %collective-permute-start.11) | collective-permute-done | bytes 294944 | tf_op jit(solution)/shard_map/ppermute | solution.py:596
  134.4 13.7 %shard_map.275 = (bf16[512,1152]{1,0:T(8,128)(2,1)}, bf16[512,1728]{1,0:T(8,128)(2,1)}, bf16[512,1728]{1,0:T(8,128)(2,1)}, bf16[512,1728]{1,0:T(8,128)(2,1)}, bf...) custom-call(bf16[128,1152]{1,0:T(8,128)(2,1)} %copy-done.8, ...), custom_call_target="tpu_custom_call" | custom-call | flops 1 | bytes 1 | tf_op jit(solution)/shard_map/pallas_call | solution.py:669
  148.2 2.4 collective-permute-start.15
  152.0 10.9 %all_to_all.25 = bf16[8,16,1152]{2,1,0:T(8,128)(2,1)S(1)} all-to-all(bf16[8,16,1152]{2,1,0:T(8,128)(2,1)S(1)} %bitcast.41), channel_id=1, replica_groups=mesh['wide'=8,'narrow'=4] {'wide'}, dimensions={0} | all-to-all | bytes 589824 | tf_op jit(solution)/shard_map/all_to_all | solution.py:605
  162.9 8.8 %collective-permute-done.15.refs_2_ = bf16[128,1152]{1,0:T(8,128)(2,1)S(1)} collective-permute-done((bf16[128,1152]{1,0:T(8,128)(2,1)}, bf16[128,1152]{1,0:T(8,128)(2,1)S(1)}, u32[]{:S(2)}, u32[]{:S(2)}) %collective-permute-start.15) | collective-permute-done | bytes 294944 | tf_op jit(solution)/shard_map/ppermute | solution.py:596
  172.7 3.0 shard_map.276
  176.2 5.9 %collective-permute-start.17 = (bf16[128,1152]{1,0:T(8,128)(2,1)S(1)}, bf16[128,1152]{1,0:T(8,128)(2,1)S(1)}, u32[]{:S(2)}, u32[]{:S(2)}) collective-permute-start(bf16[128,1152]{1,0:T(8,128)(2,1)S(1)} %get-tuple-element.125.refs_0_), channel_id=1, source_target_pairs={{0,1},{1,2},{2,3},{3,0},{4,5},{5,6},{6,7},{7,4},{8,9},{9,10},{10,1... | collective-permute-start | bytes 884744 | tf_op jit(solution)/shard_map/ppermute | solution.py:596
  184.5 5.1 %collective-permute-done.17.refs_1_ = bf16[128,1152]{1,0:T(8,128)(2,1)S(1)} collective-permute-done((bf16[128,1152]{1,0:T(8,128)(2,1)S(1)}, bf16[128,1152]{1,0:T(8,128)(2,1)S(1)}, u32[]{:S(2)}, u32[]{:S(2)}) %collective-permute-start.17) | collective-permute-done | bytes 294944 | tf_op jit(solution)/shard_map/ppermute | solution.py:596
  189.6 10.1 %collective-permute-done.18.refs_2_ = bf16[128,1152]{1,0:T(8,128)(2,1)S(1)} collective-permute-done((bf16[128,1152]{1,0:T(8,128)(2,1)S(1)}, bf16[128,1152]{1,0:T(8,128)(2,1)S(1)}, u32[]{:S(2)}, u32[]{:S(2)}) %collective-permute-start.18) | collective-permute-done | bytes 294944 | tf_op jit(solution)/shard_map/ppermute | solution.py:596
  201.2 15.5 %shard_map.277 = (bf16[512,1152]{1,0:T(8,128)(2,1)}, bf16[512,1728]{1,0:T(8,128)(2,1)}, bf16[512,1728]{1,0:T(8,128)(2,1)}, bf16[512,1152]{1,0:T(8,128)(2,1)}) custom-call(bf16[128,1152]{1,0:T(8,128)(2,1)} %copy-done.17, bf16[128,1152]{1,0:T(8,128)(2,1)} %copy-done.42, bf16[128,1152]{1,0:T(8,128)(2,1)} %copy-done.43, bf16[128,1152]{1,0:T(8,128)(2,1)} %copy-done.44, ...), custom_call_target="tpu_custom_call" | custom-call | flops 1 | bytes 1 | tf_op jit(solution)/shard_map/pallas_call | solution.py:701
  216.9 8.2 %shard_map.278 = (bf16[576,1728]{1,0:T(8,128)(2,1)}, bf16[576,1728]{1,0:T(8,128)(2,1)}, bf16[576,1728]{1,0:T(8,128)(2,1)}) custom-call(bf16[512,1152]{1,0:T(8,128)(2,1)} %get-tuple-element.129.refs_0_, bf16[512,1152]{1,0:T(8,128)(2,1)} %get-tuple-element.130.refs_1_, bf16[512,1728]{1,0:T(8,128)(2,1)} %get-tuple-element.131.refs_2_, ...), custom_call_target="tpu_custom_call" | custom-call | flops 1 | bytes 1 | tf_op jit(solution)/shard_map/pallas_call | solution.py:723
  225.6 3.9 %collective-permute-done.20.refs_5_ = bf16[576,1728]{1,0:T(8,128)(2,1)} collective-permute-done((bf16[576,1728]{1,0:T(8,128)(2,1)}, bf16[576,1728]{1,0:T(8,128)(2,1)}, u32[]{:S(2)}, u32[]{:S(2)}) %collective-permute-start.20) | collective-permute-done | bytes 1990688 | tf_op jit(solution)/shard_map/ppermute | solution.py:573
  229.6 3.0 collective-permute-done.21.refs_6_
  232.5 3.0 collective-permute-done.22.refs_7_
  235.5 11.2 %shard_map.279 = bf16[3,576,1728]{2,1,0:T(8,128)(2,1)} custom-call(bf16[512,1152]{1,0:T(8,128)(2,1)} %get-tuple-element.129.refs_0_, bf16[512,1152]{1,0:T(8,128)(2,1)} %get-tuple-element.130.refs_1_, bf16[512,1728]{1,0:T(8,128)(2,1)} %get-tuple-element.131.refs_2_, bf16[512,1728]{1,0:T(8,128)(2,1)} %get-tuple-element.132.refs_3_, ...), custom_call_target="tpu_custom_call" | custom-call | flops 1 | bytes 1 | tf_op jit(solution)/shard_map/pallas_call | solution.py:723
  246.7 6.6 %reduce-scatter.3.cloned.1.call-done.g_ref = bf16[1,128,1152]{2,1,0:T(8,128)(2,1)} async-done(((bf16[4,128,1152]{2,1,0:T(8,128)(2,1)}), bf16[1,128,1152]{2,1,0:T(8,128)(2,1)}) %reduce-scatter.3.cloned.1.call-update) | async-done | bytes 294928 | tf_op jit(solution)/shard_map/reduce_scatter | solution.py:716
  257.2 3.4 collective-permute-start.24
  260.9 3.7 all-to-all-start.2
  264.6 4.0 %collective-permute-done.23.refs_1_ = bf16[128,1152]{1,0:T(8,128)(2,1)S(1)} collective-permute-done((bf16[128,1152]{1,0:T(8,128)(2,1)S(1)}, bf16[128,1152]{1,0:T(8,128)(2,1)S(1)}, u32[]{:S(2)}, u32[]{:S(2)}) %collective-permute-start.23) | collective-permute-done | bytes 294944 | tf_op jit(solution)/shard_map/ppermute | solution.py:596
  268.6 12.3 %collective-permute-done.24.refs_2_ = bf16[128,1152]{1,0:T(8,128)(2,1)} collective-permute-done((bf16[128,1152]{1,0:T(8,128)(2,1)S(1)}, bf16[128,1152]{1,0:T(8,128)(2,1)}, u32[]{:S(2)}, u32[]{:S(2)}) %collective-permute-start.24) | collective-permute-done | bytes 294944 | tf_op jit(solution)/shard_map/ppermute | solution.py:596
  280.9 6.1 %shard_map.281 = (bf16[512,1152]{1,0:T(8,128)(2,1)}, bf16[512,256]{1,0:T(8,128)(2,1)}, f32[1,256]{1,0:T(1,128)}, bf16[128,768]{1,0:T(8,128)(2,1)}, bf16[128,768]...) custom-call(bf16[128,1152]{1,0:T(8,128)(2,1)} %copy-done.13, bf16[128,1152]{1,0:T(8,128)(2,1)} %copy-done.38, ...), custom_call_target="tpu_custom_call" | custom-call | flops 1 | bytes 1 | tf_op jit(solution)/shard_map/pallas_call | solution.py:742
  287.0 6.5 %collective-permute-start.26 = (bf16[128,768]{1,0:T(8,128)(2,1)}, bf16[128,768]{1,0:T(8,128)(2,1)S(1)}, u32[]{:S(2)}, u32[]{:S(2)}) collective-permute-start(bf16[128,768]{1,0:T(8,128)(2,1)} %get-tuple-element.158), channel_id=1, source_target_pairs={{0,1},{1,2},{2,3},{3,0},{4,5},{5,6},{6,7},{7,4},{8,9},{9,10},{10,1... | collective-permute-start | bytes 589832 | tf_op jit(solution)/shard_map/ppermute | solution.py:596
  301.5 5.8 %collective-permute-done.27.g2_ref = bf16[128,768]{1,0:T(8,128)(2,1)S(1)} collective-permute-done((bf16[128,768]{1,0:T(8,128)(2,1)}, bf16[128,768]{1,0:T(8,128)(2,1)S(1)}, u32[]{:S(2)}, u32[]{:S(2)}) %collective-permute-start.27) | collective-permute-done | bytes 196640 | tf_op jit(solution)/shard_map/ppermute | solution.py:596
  308.5 8.7 %shard_map.284 = (bf16[128,1152]{1,0:T(8,128)(2,1)}, bf16[576,1152]{1,0:T(8,128)(2,1)}, bf16[576,1152]{1,0:T(8,128)(2,1)}) custom-call(bf16[128,768]{1,0:T(8,128)(2,1)} %get-tuple-element.157.g0_ref, bf16[128,768]{1,0:T(8,128)(2,1)} %copy-done.45, bf16[128,768]{1,0:T(8,128)(2,1)} %copy-done.46, bf16[128,768]{1,0:T(8,128)(2,1)} %copy-done.47, ...), custom_call_target="tpu_custom_call" | custom-call | flops 1 | bytes 1 | tf_op jit(solution)/shard_map/pallas_call | solution.py:766
  317.3 3.3 collective-permute-done.30
  322.2 20.9 %all_to_all.26 = bf16[4,144,1152]{2,1,0:T(8,128)(2,1)S(1)} all-to-all(bf16[4,144,1152]{2,1,0:T(8,128)(2,1)S(1)} %bitcast.28), channel_id=1, replica_groups={{0,8,16,24},{4,12,20,28},{1,9,17,25},{5,13,21,29},{2,10,18,26},{6,14,22..., dimensions={0} | all-to-all | bytes 2654208 | tf_op jit(solution)/shard_map/all_to_all | solution.py:784
  344.1 4.7 %collective-permute-start.31 = (bf16[144,640]{1,0:T(8,128)(2,1)S(1)}, bf16[144,640]{1,0:T(8,128)(2,1)S(1)}, u32[]{:S(2)}, u32[]{:S(2)}) collective-permute-start(bf16[144,640]{1,0:T(8,128)(2,1)S(1)} %slice.49.refs_0_), channel_id=1, source_target_pairs={{0,1},{1,2},{2,3},{3,0},{4,5},{5,6},{6,7},{7,4},{8,9},{9,10},{10,1... | collective-permute-start | bytes 552968 | tf_op jit(solution)/shard_map/ppermute | solution.py:596
  348.8 2.8 collective-permute-start.32
  351.6 3.3 convert_element_type.20
  354.8 3.4 all-to-all-start.4
  358.3 3.5 slice_bitcast_fusion
  362.8 2.7 all-to-all-done.4
  (168 shorter events, 46.3 us)
Async XLA Ops:
  7.2 44.2 %all-gather.4.cloned.1.call-start = ((), (), s32[]{:S(2)}) async-start(), calls=%async_computation.7 | async-start | bytes 1658880 | tf_op jit(solution)/shard_map/all_gather | solution.py:568
  9.4 17.8 %collective-permute-start = (bf16[144,256]{1,0:T(8,128)(2,1)}, bf16[144,256]{1,0:T(8,128)(2,1)S(1)}, u32[]{:S(2)}, u32[]{:S(2)}) collective-permute-start(bf16[144,256]{1,0:T(8,128)(2,1)} %q_ref.1), channel_id=1, source_target_pairs={{0,1},{1,2},{2,3},{3,0},{4,5},{5,6},{6,7},{7,4},{8,9},{9,10},{10,1... | collective-permute-start | bytes 221192 | tf_op jit(solution)/shard_map/ppermute | solution.py:596
  12.4 14.7 %collective-permute-start.1 = (bf16[144,256]{1,0:T(8,128)(2,1)}, bf16[144,256]{1,0:T(8,128)(2,1)S(1)}, u32[]{:S(2)}, u32[]{:S(2)}) collective-permute-start(bf16[144,256]{1,0:T(8,128)(2,1)} %q_ref.1), channel_id=1, source_target_pairs={{0,2},{1,3},{2,0},{3,1},{4,6},{5,7},{6,4},{7,5},{8,10},{9,11},{10,... | collective-permute-start | bytes 221192 | tf_op jit(solution)/shard_map/ppermute | solution.py:596
  15.0 12.1 %collective-permute-start.2 = (bf16[144,256]{1,0:T(8,128)(2,1)}, bf16[144,256]{1,0:T(8,128)(2,1)S(1)}, u32[]{:S(2)}, u32[]{:S(2)}) collective-permute-start(bf16[144,256]{1,0:T(8,128)(2,1)} %q_ref.1), channel_id=1, source_target_pairs={{0,3},{1,0},{2,1},{3,2},{4,7},{5,4},{6,5},{7,6},{8,11},{9,8},{10,9... | collective-permute-start | bytes 221192 | tf_op jit(solution)/shard_map/ppermute | solution.py:596
  16.4 14.2 %all-to-all-start = ((bf16[8,16,1152]{2,1,0:T(8,128)(2,1)}), bf16[8,16,1152]{2,1,0:T(8,128)(2,1)S(1)}, u32[]{:S(2)}, u32[]{:S(2)}) async-start(bf16[8,16,1152]{2,1,0:T(8,128)(2,1)} %bitcast.40), calls=%async_computation | async-start | bytes 589824 | tf_op jit(solution)/shard_map/all_to_all | solution.py:605
  20.1 95.8 %all-gather.6.cloned.1.call-start = ((), (), s32[]{:S(2)}) async-start(), calls=%async_computation.8 | async-start | bytes 7741440 | tf_op jit(solution)/shard_map/all_gather | solution.py:568
  30.6 153.9 %all-gather.8.cloned.1.call-start = ((), (), s32[]{:S(2)}) async-start(), calls=%async_computation.9 | async-start | bytes 1474560 | tf_op jit(solution)/shard_map/all_gather | solution.py:568
  30.6 11.9 %collective-permute-start.3 = (bf16[128,1152]{1,0:T(8,128)(2,1)S(1)}, bf16[128,1152]{1,0:T(8,128)(2,1)S(1)}, u32[]{:S(2)}, u32[]{:S(2)}) collective-permute-start(bf16[128,1152]{1,0:T(8,128)(2,1)S(1)} %bitcast.29), channel_id=1, source_target_pairs={{0,1},{1,2},{2,3},{3,0},{4,5},{5,6},{6,7},{7,4},{8,9},{9,10},{10,1... | collective-permute-start | bytes 884744 | tf_op jit(solution)/shard_map/ppermute | solution.py:596
  31.1 20.4 %collective-permute-start.4 = (bf16[128,1152]{1,0:T(8,128)(2,1)S(1)}, bf16[128,1152]{1,0:T(8,128)(2,1)S(1)}, u32[]{:S(2)}, u32[]{:S(2)}) collective-permute-start(bf16[128,1152]{1,0:T(8,128)(2,1)S(1)} %bitcast.30), channel_id=1, source_target_pairs={{0,2},{1,3},{2,0},{3,1},{4,6},{5,7},{6,4},{7,5},{8,10},{9,11},{10,... | collective-permute-start | bytes 884744 | tf_op jit(solution)/shard_map/ppermute | solution.py:596
  31.1 20.4 %collective-permute-start.5 = (bf16[128,1152]{1,0:T(8,128)(2,1)S(1)}, bf16[128,1152]{1,0:T(8,128)(2,1)S(1)}, u32[]{:S(2)}, u32[]{:S(2)}) collective-permute-start(bf16[128,1152]{1,0:T(8,128)(2,1)S(1)} %bitcast.31), channel_id=1, source_target_pairs={{0,3},{1,0},{2,1},{3,2},{4,7},{5,4},{6,5},{7,6},{8,11},{9,8},{10,9... | collective-permute-start | bytes 884744 | tf_op jit(solution)/shard_map/ppermute | solution.py:596
  51.5 3.3 collective-permute-start.6
  55.9 60.1 %copy-start.40 = (bf16[144,256]{1,0:T(8,128)(2,1)S(1)}, bf16[144,256]{1,0:T(8,128)(2,1)}, u32[]{:S(2)}) copy-start(bf16[144,256]{1,0:T(8,128)(2,1)} %q_ref.1) | copy-start | bytes 221188
  64.7 13.9 %collective-permute-start.7 = (bf16[128,1152]{1,0:T(8,128)(2,1)}, bf16[128,1152]{1,0:T(8,128)(2,1)S(1)}, u32[]{:S(2)}, u32[]{:S(2)}) collective-permute-start(bf16[128,1152]{1,0:T(8,128)(2,1)} %get-tuple-element.107), channel_id=1, source_target_pairs={{0,1},{1,2},{2,3},{3,0},{4,5},{5,6},{6,7},{7,4},{8,9},{9,10},{10,1... | collective-permute-start | bytes 884744 | tf_op jit(solution)/shard_map/ppermute | solution.py:596
  70.9 19.7 %collective-permute-start.8 = (bf16[128,1152]{1,0:T(8,128)(2,1)}, bf16[128,1152]{1,0:T(8,128)(2,1)S(1)}, u32[]{:S(2)}, u32[]{:S(2)}) collective-permute-start(bf16[128,1152]{1,0:T(8,128)(2,1)} %get-tuple-element.108), channel_id=1, source_target_pairs={{0,2},{1,3},{2,0},{3,1},{4,6},{5,7},{6,4},{7,5},{8,10},{9,11},{10,... | collective-permute-start | bytes 884744 | tf_op jit(solution)/shard_map/ppermute | solution.py:596
  70.9 19.7 %collective-permute-start.9 = (bf16[128,1152]{1,0:T(8,128)(2,1)}, bf16[128,1152]{1,0:T(8,128)(2,1)S(1)}, u32[]{:S(2)}, u32[]{:S(2)}) collective-permute-start(bf16[128,1152]{1,0:T(8,128)(2,1)} %get-tuple-element.109), channel_id=1, source_target_pairs={{0,3},{1,0},{2,1},{3,2},{4,7},{5,4},{6,5},{7,6},{8,11},{9,8},{10,9... | collective-permute-start | bytes 884744 | tf_op jit(solution)/shard_map/ppermute | solution.py:596
  94.0 39.7 %copy-start.8 = (bf16[128,1152]{1,0:T(8,128)(2,1)}, bf16[128,1152]{1,0:T(8,128)(2,1)S(1)}, u32[]{:S(2)}) copy-start(bf16[128,1152]{1,0:T(8,128)(2,1)S(1)} %get-tuple-element.112.refs_0_) | copy-start | bytes 884740
  94.0 17.1 %collective-permute-start.10 = (bf16[128,1152]{1,0:T(8,128)(2,1)S(1)}, bf16[128,1152]{1,0:T(8,128)(2,1)S(1)}, u32[]{:S(2)}, u32[]{:S(2)}) collective-permute-start(bf16[128,1152]{1,0:T(8,128)(2,1)S(1)} %get-tuple-element.112.refs_0_), channel_id=1, source_target_pairs={{0,1},{1,2},{2,3},{3,0},{4,5},{5,6},{6,7},{7,4},{8,9},{9,10},{10,1... | collective-permute-start | bytes 884744 | tf_op jit(solution)/shard_map/ppermute | solution.py:596
  100.8 15.1 %collective-permute-start.12 = (bf16[128,1152]{1,0:T(8,128)(2,1)S(1)}, bf16[128,1152]{1,0:T(8,128)(2,1)S(1)}, u32[]{:S(2)}, u32[]{:S(2)}) collective-permute-start(bf16[128,1152]{1,0:T(8,128)(2,1)S(1)} %get-tuple-element.112.refs_0_), channel_id=1, source_target_pairs={{0,3},{1,0},{2,1},{3,2},{4,7},{5,4},{6,5},{7,6},{8,11},{9,8},{10,9... | collective-permute-start | bytes 884744 | tf_op jit(solution)/shard_map/ppermute | solution.py:596
  115.9 17.8 %collective-permute-start.13 = (bf16[3,576,1728]{2,1,0:T(8,128)(2,1)}, bf16[3,576,1728]{2,1,0:T(8,128)(2,1)}, u32[]{:S(2)}, u32[]{:S(2)}) collective-permute-start(bf16[3,576,1728]{2,1,0:T(8,128)(2,1)} %all-gather.6.cloned.1.call-done.refs_4_.refs_6_), channel_id=1, source_target_pairs={{0,4},{4,0},{8,12},{12,8},{16,20},{20,16},{24,28},{28,24},{1,5},{5... | collective-permute-start | bytes 17915912 | tf_op jit(solution)/shard_map/ppermute | solution.py:573
  116.8 35.2 %copy-start.41 = (bf16[8,1,16,1152]{3,2,1,0:T(8,128)(2,1)S(1)}, bf16[8,1,16,1152]{3,2,1,0:T(8,128)(2,1)}, u32[]{:S(2)}) copy-start(bf16[8,1,16,1152]{3,2,1,0:T(8,128)(2,1)} %param.17) | copy-start | bytes 884740
  116.8 54.9 %copy-start.7 = (f32[8,1152]{1,0:T(8,128)S(1)}, f32[8,1152]{1,0:T(8,128)}, u32[]{:S(2)}) copy-start(f32[8,1152]{1,0:T(8,128)} %get-tuple-element.111.refs_5_.refs_8_.gains_ref) | copy-start | bytes 110596
  116.8 54.9 %copy-start.20 = (s32[1,1152]{1,0:T(1,128)S(1)}, s32[1,1152]{1,0:T(1,128)}, u32[]{:S(2)}) copy-start(s32[1,1152]{1,0:T(1,128)} %get-tuple-element.121.refs_6_.order_ref) | copy-start | bytes 13828
  116.8 54.9 %copy-start.25 = (s32[5]{0:T(128)S(1)}, s32[5]{0:T(128)}, u32[]{:S(2)}) copy-start(s32[5]{0:T(128)} %copy-done.24) | copy-start | bytes 64
  116.8 136.4 %reduce-scatter.3.cloned.1.call-start = ((), (), s32[]{:S(2)}) async-start(), calls=%async_computation.10 | async-start | bytes 1474560 | tf_op jit(solution)/shard_map/reduce_scatter | solution.py:716
  117.0 16.6 %collective-permute-start.11 = (bf16[128,1152]{1,0:T(8,128)(2,1)S(1)}, bf16[128,1152]{1,0:T(8,128)(2,1)S(1)}, u32[]{:S(2)}, u32[]{:S(2)}) collective-permute-start(bf16[128,1152]{1,0:T(8,128)(2,1)S(1)} %get-tuple-element.112.refs_0_), channel_id=1, source_target_pairs={{0,2},{1,3},{2,0},{3,1},{4,6},{5,7},{6,4},{7,5},{8,10},{9,11},{10,... | collective-permute-start | bytes 884744 | tf_op jit(solution)/shard_map/ppermute | solution.py:596
  148.1 14.8 %collective-permute-start.14 = (bf16[128,1152]{1,0:T(8,128)(2,1)}, bf16[128,1152]{1,0:T(8,128)(2,1)S(1)}, u32[]{:S(2)}, u32[]{:S(2)}) collective-permute-start(bf16[128,1152]{1,0:T(8,128)(2,1)} %get-tuple-element.116), channel_id=1, source_target_pairs={{0,1},{1,2},{2,3},{3,0},{4,5},{5,6},{6,7},{7,4},{8,9},{9,10},{10,1... | collective-permute-start | bytes 884744 | tf_op jit(solution)/shard_map/ppermute | solution.py:596
  148.2 23.5 %collective-permute-start.15 = (bf16[128,1152]{1,0:T(8,128)(2,1)}, bf16[128,1152]{1,0:T(8,128)(2,1)S(1)}, u32[]{:S(2)}, u32[]{:S(2)}) collective-permute-start(bf16[128,1152]{1,0:T(8,128)(2,1)} %get-tuple-element.117), channel_id=1, source_target_pairs={{0,2},{1,3},{2,0},{3,1},{4,6},{5,7},{6,4},{7,5},{8,10},{9,11},{10,... | collective-permute-start | bytes 884744 | tf_op jit(solution)/shard_map/ppermute | solution.py:596
  150.6 21.1 %collective-permute-start.16 = (bf16[128,1152]{1,0:T(8,128)(2,1)}, bf16[128,1152]{1,0:T(8,128)(2,1)S(1)}, u32[]{:S(2)}, u32[]{:S(2)}) collective-permute-start(bf16[128,1152]{1,0:T(8,128)(2,1)} %get-tuple-element.118), channel_id=1, source_target_pairs={{0,3},{1,0},{2,1},{3,2},{4,7},{5,4},{6,5},{7,6},{8,11},{9,8},{10,9... | collective-permute-start | bytes 884744 | tf_op jit(solution)/shard_map/ppermute | solution.py:596
  176.2 13.4 %collective-permute-start.17 = (bf16[128,1152]{1,0:T(8,128)(2,1)S(1)}, bf16[128,1152]{1,0:T(8,128)(2,1)S(1)}, u32[]{:S(2)}, u32[]{:S(2)}) collective-permute-start(bf16[128,1152]{1,0:T(8,128)(2,1)S(1)} %get-tuple-element.125.refs_0_), channel_id=1, source_target_pairs={{0,1},{1,2},{2,3},{3,0},{4,5},{5,6},{6,7},{7,4},{8,9},{9,10},{10,1... | collective-permute-start | bytes 884744 | tf_op jit(solution)/shard_map/ppermute | solution.py:596
  182.2 17.6 %collective-permute-start.18 = (bf16[128,1152]{1,0:T(8,128)(2,1)S(1)}, bf16[128,1152]{1,0:T(8,128)(2,1)S(1)}, u32[]{:S(2)}, u32[]{:S(2)}) collective-permute-start(bf16[128,1152]{1,0:T(8,128)(2,1)S(1)} %get-tuple-element.125.refs_0_), channel_id=1, source_target_pairs={{0,2},{1,3},{2,0},{3,1},{4,6},{5,7},{6,4},{7,5},{8,10},{9,11},{10,... | collective-permute-start | bytes 884744 | tf_op jit(solution)/shard_map/ppermute | solution.py:596
  182.2 18.3 %collective-permute-start.19 = (bf16[128,1152]{1,0:T(8,128)(2,1)S(1)}, bf16[128,1152]{1,0:T(8,128)(2,1)S(1)}, u32[]{:S(2)}, u32[]{:S(2)}) collective-permute-start(bf16[128,1152]{1,0:T(8,128)(2,1)S(1)} %get-tuple-element.125.refs_0_), channel_id=1, source_target_pairs={{0,3},{1,0},{2,1},{3,2},{4,7},{5,4},{6,5},{7,6},{8,11},{9,8},{10,9... | collective-permute-start | bytes 884744 | tf_op jit(solution)/shard_map/ppermute | solution.py:596
  216.7 127.4 %reduce-scatter.5.cloned.1.call-start = ((), (), s32[]{:S(2)}) async-start(), calls=%async_computation.11 | async-start | bytes 7741440 | tf_op jit(solution)/shard_map/reduce_scatter | solution.py:579
  225.1 4.5 %collective-permute-start.20 = (bf16[576,1728]{1,0:T(8,128)(2,1)}, bf16[576,1728]{1,0:T(8,128)(2,1)}, u32[]{:S(2)}, u32[]{:S(2)}) collective-permute-start(bf16[576,1728]{1,0:T(8,128)(2,1)} %get-tuple-element.134), channel_id=1, source_target_pairs={{0,4},{4,0},{8,12},{12,8},{16,20},{20,16},{24,28},{28,24},{1,5},{5... | collective-permute-start | bytes 5971976 | tf_op jit(solution)/shard_map/ppermute | solution.py:573
  225.1 7.4 %collective-permute-start.21 = (bf16[576,1728]{1,0:T(8,128)(2,1)}, bf16[576,1728]{1,0:T(8,128)(2,1)}, u32[]{:S(2)}, u32[]{:S(2)}) collective-permute-start(bf16[576,1728]{1,0:T(8,128)(2,1)} %get-tuple-element.135), channel_id=1, source_target_pairs={{0,4},{4,0},{8,12},{12,8},{16,20},{20,16},{24,28},{28,24},{1,5},{5... | collective-permute-start | bytes 5971976 | tf_op jit(solution)/shard_map/ppermute | solution.py:573
  225.6 9.8 %collective-permute-start.22 = (bf16[576,1728]{1,0:T(8,128)(2,1)}, bf16[576,1728]{1,0:T(8,128)(2,1)}, u32[]{:S(2)}, u32[]{:S(2)}) collective-permute-start(bf16[576,1728]{1,0:T(8,128)(2,1)} %get-tuple-element.136), channel_id=1, source_target_pairs={{0,4},{4,0},{8,12},{12,8},{16,20},{20,16},{24,28},{28,24},{1,5},{5... | collective-permute-start | bytes 5971976 | tf_op jit(solution)/shard_map/ppermute | solution.py:573
  256.8 50.5 %collective-permute-start.29 = (bf16[4,576,256]{2,1,0:T(8,128)(2,1)S(1)}, bf16[4,576,256]{2,1,0:T(8,128)(2,1)S(1)}, u32[]{:S(2)}, u32[]{:S(2)}) collective-permute-start(bf16[4,576,256]{2,1,0:T(8,128)(2,1)S(1)} %copy-done.27), channel_id=1, source_target_pairs={{0,4},{4,0},{8,12},{12,8},{16,20},{20,16},{24,28},{28,24},{1,5},{5... | collective-permute-start | bytes 3538952 | tf_op jit(solution)/shard_map/ppermute | solution.py:573
  256.8 11.8 %collective-permute-start.23 = (bf16[128,1152]{1,0:T(8,128)(2,1)S(1)}, bf16[128,1152]{1,0:T(8,128)(2,1)S(1)}, u32[]{:S(2)}, u32[]{:S(2)}) collective-permute-start(bf16[128,1152]{1,0:T(8,128)(2,1)S(1)} %get-tuple-element.140.refs_0_), channel_id=1, source_target_pairs={{0,1},{1,2},{2,3},{3,0},{4,5},{5,6},{6,7},{7,4},{8,9},{9,10},{10,1... | collective-permute-start | bytes 884744 | tf_op jit(solution)/shard_map/ppermute | solution.py:596
  257.2 23.7 %collective-permute-start.24 = (bf16[128,1152]{1,0:T(8,128)(2,1)S(1)}, bf16[128,1152]{1,0:T(8,128)(2,1)}, u32[]{:S(2)}, u32[]{:S(2)}) collective-permute-start(bf16[128,1152]{1,0:T(8,128)(2,1)S(1)} %get-tuple-element.140.refs_0_), channel_id=1, source_target_pairs={{0,2},{1,3},{2,0},{3,1},{4,6},{5,7},{6,4},{7,5},{8,10},{9,11},{10,... | collective-permute-start | bytes 884744 | tf_op jit(solution)/shard_map/ppermute | solution.py:596
  260.5 20.4 %collective-permute-start.25 = (bf16[128,1152]{1,0:T(8,128)(2,1)S(1)}, bf16[128,1152]{1,0:T(8,128)(2,1)}, u32[]{:S(2)}, u32[]{:S(2)}) collective-permute-start(bf16[128,1152]{1,0:T(8,128)(2,1)S(1)} %get-tuple-element.140.refs_0_), channel_id=1, source_target_pairs={{0,3},{1,0},{2,1},{3,2},{4,7},{5,4},{6,5},{7,6},{8,11},{9,8},{10,9... | collective-permute-start | bytes 884744 | tf_op jit(solution)/shard_map/ppermute | solution.py:596
  260.9 40.6 %all-to-all-start.2 = ((bf16[8,16,1152]{2,1,0:T(8,128)(2,1)}), bf16[8,16,1152]{2,1,0:T(8,128)(2,1)S(1)}, u32[]{:S(2)}, u32[]{:S(2)}) async-start(bf16[8,16,1152]{2,1,0:T(8,128)(2,1)} %bitcast.11), calls=%async_computation.2 | async-start | bytes 589824 | tf_op jit(solution)/shard_map/all_to_all | solution.py:610
  287.0 14.4 %collective-permute-start.26 = (bf16[128,768]{1,0:T(8,128)(2,1)}, bf16[128,768]{1,0:T(8,128)(2,1)S(1)}, u32[]{:S(2)}, u32[]{:S(2)}) collective-permute-start(bf16[128,768]{1,0:T(8,128)(2,1)} %get-tuple-element.158), channel_id=1, source_target_pairs={{0,1},{1,2},{2,3},{3,0},{4,5},{5,6},{6,7},{7,4},{8,9},{9,10},{10,1... | collective-permute-start | bytes 589832 | tf_op jit(solution)/shard_map/ppermute | solution.py:596
  293.5 13.8 %collective-permute-start.27 = (bf16[128,768]{1,0:T(8,128)(2,1)}, bf16[128,768]{1,0:T(8,128)(2,1)S(1)}, u32[]{:S(2)}, u32[]{:S(2)}) collective-permute-start(bf16[128,768]{1,0:T(8,128)(2,1)} %get-tuple-element.159), channel_id=1, source_target_pairs={{0,2},{1,3},{2,0},{3,1},{4,6},{5,7},{6,4},{7,5},{8,10},{9,11},{10,... | collective-permute-start | bytes 589832 | tf_op jit(solution)/shard_map/ppermute | solution.py:596
  294.4 12.9 %collective-permute-start.28 = (bf16[128,768]{1,0:T(8,128)(2,1)}, bf16[128,768]{1,0:T(8,128)(2,1)S(1)}, u32[]{:S(2)}, u32[]{:S(2)}) collective-permute-start(bf16[128,768]{1,0:T(8,128)(2,1)} %get-tuple-element.160), channel_id=1, source_target_pairs={{0,3},{1,0},{2,1},{3,2},{4,7},{5,4},{6,5},{7,6},{8,11},{9,8},{10,9... | collective-permute-start | bytes 589832 | tf_op jit(solution)/shard_map/ppermute | solution.py:596
  317.2 3.3 collective-permute-start.30
  344.1 17.7 %collective-permute-start.31 = (bf16[144,640]{1,0:T(8,128)(2,1)S(1)}, bf16[144,640]{1,0:T(8,128)(2,1)S(1)}, u32[]{:S(2)}, u32[]{:S(2)}) collective-permute-start(bf16[144,640]{1,0:T(8,128)(2,1)S(1)} %slice.49.refs_0_), channel_id=1, source_target_pairs={{0,1},{1,2},{2,3},{3,0},{4,5},{5,6},{6,7},{7,4},{8,9},{9,10},{10,1... | collective-permute-start | bytes 552968 | tf_op jit(solution)/shard_map/ppermute | solution.py:596
  348.8 14.0 %collective-permute-start.32 = (bf16[144,640]{1,0:T(8,128)(2,1)S(1)}, bf16[144,640]{1,0:T(8,128)(2,1)S(1)}, u32[]{:S(2)}, u32[]{:S(2)}) collective-permute-start(bf16[144,640]{1,0:T(8,128)(2,1)S(1)} %slice.49.refs_0_), channel_id=1, source_target_pairs={{0,2},{1,3},{2,0},{3,1},{4,6},{5,7},{6,4},{7,5},{8,10},{9,11},{10,... | collective-permute-start | bytes 552968 | tf_op jit(solution)/shard_map/ppermute | solution.py:596
  351.6 11.2 %collective-permute-start.33 = (bf16[144,640]{1,0:T(8,128)(2,1)S(1)}, bf16[144,640]{1,0:T(8,128)(2,1)S(1)}, u32[]{:S(2)}, u32[]{:S(2)}) collective-permute-start(bf16[144,640]{1,0:T(8,128)(2,1)S(1)} %slice.49.refs_0_), channel_id=1, source_target_pairs={{0,3},{1,0},{2,1},{3,2},{4,7},{5,4},{6,5},{7,6},{8,11},{9,8},{10,9... | collective-permute-start | bytes 552968 | tf_op jit(solution)/shard_map/ppermute | solution.py:596
  354.8 10.6 %all-to-all-start.4 = ((bf16[8,16,1152]{2,1,0:T(8,128)(2,1)}), bf16[8,16,1152]{2,1,0:T(8,128)(2,1)S(1)}, u32[]{:S(2)}, u32[]{:S(2)}) async-start(bf16[8,16,1152]{2,1,0:T(8,128)(2,1)} %bitcast.19), calls=%async_computation.6 | async-start | bytes 589824 | tf_op jit(solution)/shard_map/all_to_all | solution.py:610
  (43 other events, 280.9 us)
Sparse Core Ops, SparseCore 0:
  10.5 31.9 all-gather.3
  44.4 69.3 all-gather.5
  116.9 27.5 all-gather.7
  216.8 36.3 reduce-scatter.2
  256.2 71.2 reduce-scatter.4
